TPU v7x, 32 devices: a whole 2x2x4 slice. The times are simulated.
32 devices in a mesh: sec: 4 (over x, core), dev: 8 (over z, y).
Axes of the slice: x: 2, y: 2, z: 4, core: 2. Of those that a mesh axis runs over, the one named last changes fastest.
Arguments:
- queries: bfloat16 [256, 64, 576], P(('sec', 'dev')), may hold values from -6 to 6
- latent_cache: bfloat16 [256, 1024, 576], P(('sec', 'dev')), may hold values from -9 to 9
- cache_length: int32 [256], P(('sec', 'dev')), may hold values from 2 to 1024, as said below
- residual: bfloat16 [256, 7168], P(('sec', 'dev')), may hold values from -9 to 9
- norm_gain: float32 [7168], replicated, may hold values from 0.1 to 1.9
- value_up: bfloat16 [64, 512, 128], P('dev'), may hold values from -4 to 4
- out_weight: bfloat16 [8192, 7168], P('dev'), may hold values from -0.0625 to 0.0625
- gate_weight: bfloat16 [7168, 8192], P(None, 'dev'), may hold values from -0.0625 to 0.0625
- up_weight: bfloat16 [7168, 8192], P(None, 'dev'), may hold values from -0.0625 to 0.0625
- down_weight: bfloat16 [8192, 7168], P('dev'), may hold values from -0.125 to 0.125
- expert_index: int32 [256, 2], P(('sec', 'dev')), may hold values from 0 to 3, all different within a row; in each aligned block of 4 rows (0 to 3, 4 to 7, ...) at most 3 rows name the same one
- gate_level: int32 [256, 2], P(('sec', 'dev')), may hold values from 1 to 4095
Outputs:
- layer_output: bfloat16 [256, 7168], P(('sec', 'dev'))
Inputs may be any that keep to these rules, and one draw needn't show every extreme that they name: `expert_index`: each token names 2 different experts. The rows of one device form 2 aligned blocks of 4 rows, and within such a block no expert is named more than 3 times. `cache_length`: some request of the first 3 sections holds exactly 1024 live positions.
All inputs are finite; a program needn't handle non-finite values.
Results may differ from a plain program's by a relative error of at most 0.03.
Values may be sent and summed in bfloat16 or wider, within the bound.
No kernel may reach another device: no remote copies, remote signals or barrier semaphores. Data moves between devices by JAX's collectives and lax.ppermute only.
A program may use at most 192 MiB of HBM per device.

v0:
```python
import jax
import jax.numpy as jnp
from jax import lax
from jax.sharding import PartitionSpec as P

EXPERTS = 4
TOPK = 2
MICRO = 2
CAP = 3


def from_behind(x, axis, by):
    length = lax.axis_size(axis)
    pairs = [(i, i + by) for i in range(length) if 0 <= i + by < length]
    return lax.ppermute(x, axis, pairs)


def expert_block(expert_rows, gate_weight, up_weight, down_weight):
    gate_hidden = jnp.dot(expert_rows, gate_weight, preferred_element_type=jnp.float32)
    up_hidden = jnp.dot(expert_rows, up_weight, preferred_element_type=jnp.float32)
    activated = (jax.nn.silu(gate_hidden) * up_hidden).astype(jnp.bfloat16)
    return jnp.dot(activated, down_weight, preferred_element_type=jnp.float32).astype(jnp.bfloat16)


def layer_block(
    queries,
    latent_cache,
    cache_length,
    residual,
    norm_gain,
    value_up,
    out_weight,
    gate_weight,
    up_weight,
    down_weight,
    expert_index,
    gate_level,
    groups,
):
    sections = lax.axis_size("sec")
    group_size = lax.axis_size("dev")
    section_index = lax.axis_index("sec")
    attending = section_index < sections - 1
    token_count = queries.shape[0]
    latent_width = value_up.shape[1]
    score_scale = (value_up.shape[2] + queries.shape[2] - latent_width) ** (-0.5)
    width = residual.shape[1]
    scores = (
        jnp.einsum("thc,tpc->thp", queries, latent_cache, preferred_element_type=jnp.float32)
        * score_scale
    )
    position = lax.broadcasted_iota(jnp.int32, (1, 1, latent_cache.shape[1]), 2)
    usable = position < cache_length[:, None, None]
    masked = jnp.where(usable, scores, -1e30)
    highest = jnp.max(masked, axis=2, keepdims=True)
    expos = jnp.where(usable, jnp.exp(masked - highest), 0.0)
    weights = (expos / jnp.sum(expos, axis=2, keepdims=True)).astype(jnp.bfloat16)
    latent_out = jnp.einsum(
        "thp,tpc->thc", weights, latent_cache, preferred_element_type=jnp.float32
    )[:, :, :latent_width].astype(jnp.bfloat16)
    by_heads = lax.all_to_all(latent_out, "dev", split_axis=1, concat_axis=0, tiled=True)
    head_out = jnp.einsum(
        "thc,hcv->thv", by_heads, value_up, preferred_element_type=jnp.float32
    ).astype(jnp.bfloat16)
    head_flat = head_out.reshape(head_out.shape[0], -1)
    attended = lax.psum_scatter(
        jnp.dot(head_flat, out_weight, preferred_element_type=jnp.float32).astype(jnp.bfloat16),
        "dev",
        scatter_dimension=0,
        tiled=True,
    ).astype(jnp.float32)
    stream = (residual.astype(jnp.float32) + attended).astype(jnp.bfloat16)
    stream_float = stream.astype(jnp.float32)
    mean_square = jnp.mean(stream_float * stream_float, axis=1, keepdims=True)
    normed = (stream_float * lax.rsqrt(mean_square + 1e-06) * norm_gain).astype(jnp.bfloat16)
    route_count = token_count * TOPK
    per_micro = token_count // groups
    slot_width = groups * CAP
    flat_expert = expert_index.reshape(route_count)
    route_order = jnp.arange(route_count, dtype=jnp.int32)
    micro_of = route_order // TOPK // per_micro
    earlier = (
        (route_order[:, None] > route_order[None, :])
        & (flat_expert[:, None] == flat_expert[None, :])
        & (micro_of[:, None] == micro_of[None, :])
    )
    rank_in = jnp.sum(earlier.astype(jnp.int32), axis=1)
    target = (flat_expert * slot_width + micro_of * CAP + rank_in).reshape(token_count, TOPK)
    slot_index = jnp.arange(EXPERTS * slot_width, dtype=jnp.int32)
    placing = jnp.any(slot_index[:, None, None] == target[None, :, :], axis=2).astype(jnp.bfloat16)
    levels = gate_level.astype(jnp.float32)
    mix = levels / jnp.sum(levels, axis=1, keepdims=True)
    gathering = jnp.sum(
        jnp.where(slot_index[None, None, :] == target[:, :, None], mix[:, :, None], 0.0), axis=1
    )
    packed = jnp.dot(placing, normed, preferred_element_type=jnp.float32)
    packed = jnp.where(attending, packed, 0.0).astype(jnp.bfloat16)
    slab_count = group_size // EXPERTS
    last_section = sections - 1
    pieces = []
    for source in range(last_section):
        pieces.append(from_behind(packed, "sec", last_section - source))
    stacked = jnp.stack(pieces, axis=0).reshape(last_section, EXPERTS, 1, slot_width, width)
    spread = jnp.broadcast_to(stacked, (last_section, EXPERTS, slab_count, slot_width, width))
    spread = jnp.transpose(spread, (1, 2, 0, 3, 4)).reshape(
        group_size, last_section, slot_width, width
    )
    arrived = lax.all_to_all(spread, "dev", split_axis=0, concat_axis=0, tiled=True)
    partial_out = expert_block(arrived.reshape(-1, width), gate_weight, up_weight, down_weight)
    back = lax.all_to_all(
        partial_out.reshape(group_size, last_section, slot_width, width),
        "dev",
        split_axis=0,
        concat_axis=0,
        tiled=True,
    )
    from_flat = jnp.zeros((group_size, slot_width, width), jnp.bfloat16)
    for source in range(last_section):
        moved = from_behind(back[:, source], "sec", source - last_section)
        from_flat = jnp.where(section_index == source, moved, from_flat)
    from_experts = from_flat.reshape(EXPERTS, slab_count, slot_width, width)
    slab_total = jnp.sum(from_experts.astype(jnp.float32), axis=1).reshape(
        EXPERTS * slot_width, width
    )
    moe = jnp.dot(gathering, slab_total, precision=lax.Precision.HIGHEST)
    result = (stream_float + moe).astype(jnp.bfloat16)
    return jnp.where(attending, result, jnp.zeros_like(result))


def body(
    queries,
    latent_cache,
    cache_length,
    residual,
    norm_gain,
    value_up,
    out_weight,
    gate_weight,
    up_weight,
    down_weight,
    expert_index,
    gate_level,
):
    return layer_block(
        queries,
        latent_cache,
        cache_length,
        residual,
        norm_gain,
        value_up,
        out_weight,
        gate_weight,
        up_weight,
        down_weight,
        expert_index,
        gate_level,
        MICRO,
    )


def solution(mesh):
    placed = (
        P(("sec", "dev"), None, None),
        P(("sec", "dev"), None, None),
        P(("sec", "dev")),
        P(("sec", "dev"), None),
        P(),
        P("dev", None, None),
        P("dev", None),
        P(None, "dev"),
        P(None, "dev"),
        P("dev", None),
        P(("sec", "dev"), None),
        P(("sec", "dev"), None),
    )
    return jax.shard_map(
        body, mesh=mesh, in_specs=placed, out_specs=P(("sec", "dev"), None), check_vma=False
    )
```

profile of v0, /device:TPU:0, one launch (start us, length us, event | category | flops | bytes accessed | tf_op | source)
XLA Modules:
  0.0 338.8 jit_solution(6789449442383732138)
XLA Ops:
  6.5 0.8 iota_compare_fusion
  7.4 6.2 %fusion.36 = (f32[8,64]{1,0:T(8,128)S(1)}, f32[8,64,1024]{2,1,0:T(8,128)S(1)}) fusion(pred[8,1024]{1,0:T(8,128)(4,1)S(1)} %iota_compare_fusion, bf16[8,64,576]{2,1,0:T(8,128)(2,1)} %param.12, bf16[8,1024,576]{1,2,0:T(8,128)(2,1)} %param.13), kind=kOutput, calls=%fused_computation.81 | convolution fusion | flops 606602240 | bytes 12134400 | tf_op jit(solution)/shard_map/sub | solution.py:56
  13.6 6.7 %fusion.7 = bf16[8,64,576]{2,1,0:T(8,128)(2,1)S(1)} fusion(bf16[8,1024,576]{1,2,0:T(8,128)(2,1)} %param.13, f32[8,64,1024]{2,1,0:T(8,128)S(1)} %get-tuple-element.9, f32[8,64]{1,0:T(8,128)S(1)} %get-tuple-element.8), kind=kOutput, calls=%fused_computation.17 | convolution fusion | flops 605028352 | bytes 12126208 | tf_op jit(solution)/shard_map/thp,tpc->thc/dot_general | solution.py:58
  20.7 21.6 %all_to_all.28 = bf16[8,64,512]{2,0,1:T(8,128)(2,1)S(1)} all-to-all(bf16[8,64,512]{2,0,1:T(8,128)(2,1)S(1)} %copy.48), channel_id=1, replica_groups=mesh['sec'=4,'dev'=8] {'dev'}, dimensions={1} | all-to-all | bytes 1048576 | tf_op jit(solution)/shard_map/all_to_all | solution.py:61
  42.7 3.6 %convolution_convert_fusion.1 = bf16[64,7168]{1,0:T(8,128)(2,1)} fusion(bf16[1024,7168]{1,0:T(8,128)(2,1)S(1)} %copy-done.2, bf16[8,8,8,128]{3,2,1,0:T(8,128)(2,1)S(1)} %fusion.6), kind=kOutput, calls=%fused_computation.2 | convolution fusion | flops 939982848 | bytes 15728640 | tf_op jit(solution)/shard_map/dot_general | solution.py:67
  46.9 61.9 %reduce-scatter.2.cloned.1.call-done = bf16[8,7168]{1,0:T(8,128)(2,1)} async-done(((bf16[64,7168]{1,0:T(8,128)(2,1)}), bf16[8,7168]{1,0:T(8,128)(2,1)}) %reduce-scatter.2.cloned.1.call-update) | async-done | bytes 114704 | tf_op jit(solution)/shard_map/reduce_scatter | solution.py:66
  108.8 1.1 fusion.14
  109.9 1.2 fusion.1
  111.1 1.3 collective-permute-start
  112.4 2.7 collective-permute-start.1
  115.2 1.3 collective-permute-start.2
  116.5 3.9 %collective-permute-done = bf16[24,7168]{1,0:T(8,128)(2,1)S(1)} collective-permute-done((bf16[24,7168]{1,0:T(8,128)(2,1)S(1)}, bf16[24,7168]{1,0:T(8,128)(2,1)S(1)}, u32[]{:S(2)}, u32[]{:S(2)}) %collective-permute-start) | collective-permute-done | bytes 344096 | tf_op jit(solution)/shard_map/ppermute | solution.py:15
  120.5 7.2 %collective-permute-done.1 = bf16[24,7168]{1,0:T(8,128)(2,1)S(1)} collective-permute-done((bf16[24,7168]{1,0:T(8,128)(2,1)S(1)}, bf16[24,7168]{1,0:T(8,128)(2,1)S(1)}, u32[]{:S(2)}, u32[]{:S(2)}) %collective-permute-start.1) | collective-permute-done | bytes 344096 | tf_op jit(solution)/shard_map/ppermute | solution.py:15
  128.7 66.7 %all_to_all.29 = bf16[8,3,6,7168]{3,2,1,0:T(8,128)(2,1)} all-to-all(bf16[8,3,6,7168]{3,2,1,0:T(8,128)(2,1)S(1)} %bitcast.38), channel_id=1, replica_groups=mesh['sec'=4,'dev'=8] {'dev'}, dimensions={0} | all-to-all | bytes 4128768 | tf_op jit(solution)/shard_map/all_to_all | solution.py:108
  195.4 2.9 reshape.218
  198.3 7.5 %fusion.39 = f32[144,1024]{1,0:T(8,128)S(1)} fusion(bf16[144,7168]{1,0:T(8,128)(2,1)S(1)} %reshape.218, bf16[7168,1024]{1,0:T(8,128)(2,1)} %param.19), kind=kOutput, calls=%fused_computation.83 | convolution fusion | flops 2113929216 | bytes 17334272 | tf_op jit(solution)/shard_map/dot_general | solution.py:19
  205.8 15.2 %convolution_convert_fusion = bf16[144,7168]{1,0:T(8,128)(2,1)} fusion(bf16[1024,7168]{1,0:T(8,128)(2,1)} %param.21, bf16[144,7168]{1,0:T(8,128)(2,1)S(1)} %reshape.218, bf16[7168,1024]{1,0:T(8,128)(2,1)} %param.20, f32[144,1024]{1,0:T(8,128)S(1)} %fusion.39), kind=kOutput, calls=%fused_computation.1 | convolution fusion | flops 4229775360 | bytes 34078720 | tf_op jit(solution)/shard_map/dot_general | solution.py:22
  221.0 4.1 %reshape.219 = bf16[8,3,6,7168]{3,2,1,0:T(8,128)(2,1)} reshape(bf16[144,7168]{1,0:T(8,128)(2,1)} %convolution_convert_fusion) | data formatting | bytes 4128768 | tf_op jit(solution)/shard_map/reshape | solution.py:111
  225.2 65.9 %all_to_all.30 = bf16[8,3,6,7168]{3,2,1,0:T(8,128)(2,1)S(1)} all-to-all(bf16[8,3,6,7168]{3,2,1,0:T(8,128)(2,1)} %reshape.219), channel_id=1, replica_groups=mesh['sec'=4,'dev'=8] {'dev'}, dimensions={0} | all-to-all | bytes 4128768 | tf_op jit(solution)/shard_map/all_to_all | solution.py:110
  291.3 0.4 copy.56
  291.7 1.3 collective-permute-start.3
  293.0 1.2 copy.57
  294.2 1.3 collective-permute-start.4
  295.5 1.2 copy.58
  296.7 1.5 collective-permute-start.5
  298.4 21.4 %collective-permute-done.4 = bf16[8,6,7168]{2,0,1:T(8,128)(2,1)S(1)} collective-permute-done((bf16[8,6,7168]{2,0,1:T(8,128)(2,1)}, bf16[8,6,7168]{2,0,1:T(8,128)(2,1)S(1)}, u32[]{:S(2)}, u32[]{:S(2)}) %collective-permute-start.4) | collective-permute-done | bytes 688160 | tf_op jit(solution)/shard_map/ppermute | solution.py:15
  319.8 0.8 copy-done.5
  320.6 4.1 %collective-permute-done.5 = bf16[8,6,7168]{2,0,1:T(8,128)(2,1)S(1)} collective-permute-done((bf16[8,6,7168]{2,0,1:T(8,128)(2,1)}, bf16[8,6,7168]{2,0,1:T(8,128)(2,1)S(1)}, u32[]{:S(2)}, u32[]{:S(2)}) %collective-permute-start.5) | collective-permute-done | bytes 688160 | tf_op jit(solution)/shard_map/ppermute | solution.py:15
  324.8 1.9 reshape.221
  326.7 3.2 reduce_sum.62
  329.9 0.4 copy.59
  330.8 1.1 fusion.3
  (45 shorter events, 3.3 us)
Async XLA Ops:
  6.5 35.8 %copy-start = (bf16[8,512,128]{2,1,0:T(8,128)(2,1)S(1)}, bf16[8,512,128]{2,1,0:T(8,128)(2,1)}, u32[]{:S(2)}) copy-start(bf16[8,512,128]{2,1,0:T(8,128)(2,1)} %param.17) | copy-start | bytes 3145732
  6.5 102.2 %reduce-scatter.2.cloned.1.call-start = ((), (), s32[]{:S(2)}) async-start(), calls=%async_computation.4 | async-start | bytes 1032192 | tf_op jit(solution)/shard_map/reduce_scatter | solution.py:66
  13.6 29.0 %copy-start.2 = (bf16[1024,7168]{1,0:T(8,128)(2,1)S(1)}, bf16[1024,7168]{1,0:T(8,128)(2,1)}, u32[]{:S(2)}) copy-start(bf16[1024,7168]{1,0:T(8,128)(2,1)} %param.18) | copy-start | bytes 44040196
  42.6 3.7 %copy-start.7 = (s32[8,2]{0,1:T(2,128)S(1)}, s32[8,2]{0,1:T(2,128)}, u32[]{:S(2)}) copy-start(s32[8,2]{0,1:T(2,128)} %param.22) | copy-start | bytes 196
  42.6 66.2 %copy-start.3 = (bf16[8,7168]{1,0:T(8,128)(2,1)S(1)}, bf16[8,7168]{1,0:T(8,128)(2,1)}, u32[]{:S(2)}) copy-start(bf16[8,7168]{1,0:T(8,128)(2,1)} %param.15) | copy-start | bytes 344068
  42.6 67.2 %copy-start.6 = (f32[7168]{0:T(1024)S(1)}, f32[7168]{0:T(1024)}, u32[]{:S(2)}) copy-start(f32[7168]{0:T(1024)} %param.16) | copy-start | bytes 86020
  111.1 9.3 %collective-permute-start = (bf16[24,7168]{1,0:T(8,128)(2,1)S(1)}, bf16[24,7168]{1,0:T(8,128)(2,1)S(1)}, u32[]{:S(2)}, u32[]{:S(2)}) collective-permute-start(bf16[24,7168]{1,0:T(8,128)(2,1)S(1)} %fusion.1), channel_id=1, source_target_pairs={{0,24},{1,25},{2,26},{3,27},{4,28},{5,29},{6,30},{7,31}} | collective-permute-start | bytes 1032200 | tf_op jit(solution)/shard_map/ppermute | solution.py:15
  112.4 15.3 %collective-permute-start.1 = (bf16[24,7168]{1,0:T(8,128)(2,1)S(1)}, bf16[24,7168]{1,0:T(8,128)(2,1)S(1)}, u32[]{:S(2)}, u32[]{:S(2)}) collective-permute-start(bf16[24,7168]{1,0:T(8,128)(2,1)S(1)} %fusion.1), channel_id=1, source_target_pairs={{0,16},{8,24},{1,17},{9,25},{2,18},{10,26},{3,19},{11,27},{4,20},{... | collective-permute-start | bytes 1032200 | tf_op jit(solution)/shard_map/ppermute | solution.py:15
  115.2 12.7 %collective-permute-start.2 = (bf16[24,7168]{1,0:T(8,128)(2,1)S(1)}, bf16[24,7168]{1,0:T(8,128)(2,1)S(1)}, u32[]{:S(2)}, u32[]{:S(2)}) collective-permute-start(bf16[24,7168]{1,0:T(8,128)(2,1)S(1)} %fusion.1), channel_id=1, source_target_pairs={{0,8},{8,16},{16,24},{1,9},{9,17},{17,25},{2,10},{10,18},{18,26},{... | collective-permute-start | bytes 1032200 | tf_op jit(solution)/shard_map/ppermute | solution.py:15
  291.3 7.0 %copy-start.8 = (s32[8,2]{0,1:T(2,128)S(1)}, s32[8,2]{0,1:T(2,128)}, u32[]{:S(2)}) copy-start(s32[8,2]{0,1:T(2,128)} %param.23) | copy-start | bytes 196
  291.7 6.7 %collective-permute-start.3 = (bf16[8,6,7168]{2,0,1:T(8,128)(2,1)S(1)}, bf16[8,6,7168]{2,0,1:T(8,128)(2,1)S(1)}, u32[]{:S(2)}, u32[]{:S(2)}) collective-permute-start(bf16[8,6,7168]{2,0,1:T(8,128)(2,1)S(1)} %copy.56), channel_id=1, source_target_pairs={{8,0},{16,8},{24,16},{9,1},{17,9},{25,17},{10,2},{18,10},{26,18},{... | collective-permute-start | bytes 2064392 | tf_op jit(solution)/shard_map/ppermute | solution.py:15
  294.2 25.6 %collective-permute-start.4 = (bf16[8,6,7168]{2,0,1:T(8,128)(2,1)}, bf16[8,6,7168]{2,0,1:T(8,128)(2,1)S(1)}, u32[]{:S(2)}, u32[]{:S(2)}) collective-permute-start(bf16[8,6,7168]{2,0,1:T(8,128)(2,1)} %copy.57), channel_id=1, source_target_pairs={{16,0},{24,8},{17,1},{25,9},{18,2},{26,10},{19,3},{27,11},{20,4},{... | collective-permute-start | bytes 2064392 | tf_op jit(solution)/shard_map/ppermute | solution.py:15
  296.7 27.9 %collective-permute-start.5 = (bf16[8,6,7168]{2,0,1:T(8,128)(2,1)}, bf16[8,6,7168]{2,0,1:T(8,128)(2,1)S(1)}, u32[]{:S(2)}, u32[]{:S(2)}) collective-permute-start(bf16[8,6,7168]{2,0,1:T(8,128)(2,1)} %copy.58), channel_id=1, source_target_pairs={{24,0},{25,1},{26,2},{27,3},{28,4},{29,5},{30,6},{31,7}} | collective-permute-start | bytes 2064392 | tf_op jit(solution)/shard_map/ppermute | solution.py:15
  319.8 0.9 copy-start.5
  326.7 5.2 %copy-start.1 = (bf16[8,512,128]{2,1,0:T(8,128)(2,1)S(1)}, bf16[8,512,128]{2,1,0:T(8,128)(2,1)}, u32[]{:S(2)}) copy-start(bf16[8,512,128]{2,1,0:T(8,128)(2,1)} %param.17) | copy-start | bytes 3145732
  329.9 0.9 copy-start.4
Sparse Core Ops, SparseCore 0:
  46.4 62.3 reduce-scatter.1
where the time goes:
time: 339 us
  blocking collectives  154 us (45%)
  waiting for transfers between devices  98.5 us (29%)
  matrix products  41.9 us (12%)
  local copies, waits for them, and re-layouts  15.2 us (4%)
  between operations  13.7 us (4%)
  starting transfers between devices  9.44 us (3%)
  other arithmetic  5.97 us (2%)
    all_to_all x1, blocking collectives, layer_block(): lax.all_to_all(spread, 'dev', split_axis=0, concat_axis=0, tiled=True)  66.7 us
    all_to_all x1, blocking collectives, layer_block(): lax.all_to_all(partial_out.reshape(group_size, last_section, slot_width,...  65.9 us
    reduce_scatter x1, waiting for transfers between devices, layer_block(): lax.psum_scatter(jnp.dot(head_flat, out_weight, preferred_element_type=jn...  61.9 us
    ppermute x6, waiting for transfers between devices, from_behind(): return lax.ppermute(x, axis, pairs)  36.6 us
    all_to_all x1, blocking collectives, layer_block(): lax.all_to_all(latent_out, 'dev', split_axis=1, concat_axis=0, tiled=True)  21.6 us
    dot_general x1, matrix products, expert_block(): jnp.dot(activated, down_weight, preferred_element_type=jnp.float32)  15.2 us
    ppermute x6, starting transfers between devices, from_behind(): return lax.ppermute(x, axis, pairs)  9.44 us
    dot_general x1, matrix products, expert_block(): jnp.dot(expert_rows, gate_weight, preferred_element_type=jnp.float32)  7.47 us
  transfers between devices with their start and end apart: 7, of which 5 were waited for; matrix products, arithmetic and copies ran while one was open for 1% of the time, Pallas kernels for 0%

commit v1 on v0

v1 whole, which is shorter than its diff:
```python
import jax
import jax.numpy as jnp
from jax import lax
from jax.sharding import PartitionSpec as P

EXPERTS = 4
CHUNKS = 2
LANES = 128


def swap(x, by):
    size = lax.axis_size("dev")
    return lax.ppermute(x, "dev", [(i, i ^ by) for i in range(size)])


def sum_scatter(x, rows):
    pairs = lax.axis_size("dev") // 2
    me = lax.axis_index("dev")
    fast, slow = me % 2, me // 2
    blocks = x.reshape(pairs, 2, rows, x.shape[1])
    kept = lax.dynamic_index_in_dim(blocks, fast, 1, False)
    got = swap(lax.dynamic_index_in_dim(blocks, 1 - fast, 1, False), 1)
    paired = (kept.astype(jnp.float32) + got.astype(jnp.float32)).astype(jnp.bfloat16)
    total = lax.dynamic_index_in_dim(paired, slow, 0, False).astype(jnp.float32)
    for by in reversed(range(1, pairs)):
        sent = lax.dynamic_index_in_dim(paired, slow ^ by, 0, False)
        total = total + swap(sent, 2 * by).astype(jnp.float32)
    return total


def gather_rows(x):
    pairs = lax.axis_size("dev") // 2
    column = [x] + [None] * (pairs - 1)
    for by in reversed(range(1, pairs)):
        column[by] = swap(x, 2 * by)
    column = jnp.stack(column, axis=0)
    return jnp.stack([column, swap(column, 1)], axis=0)


def layer_block(
    queries,
    latent_cache,
    cache_length,
    residual,
    norm_gain,
    value_up,
    out_weight,
    gate_weight,
    up_weight,
    down_weight,
    expert_index,
    gate_level,
):
    group_size = lax.axis_size("dev")
    pairs = group_size // 2
    attending = lax.axis_index("sec") < lax.axis_size("sec") - 1
    me = lax.axis_index("dev")
    fast, slow = me % 2, me // 2
    token_count = queries.shape[0]
    latent_width = value_up.shape[1]
    score_scale = (value_up.shape[2] + queries.shape[2] - latent_width) ** (-0.5)
    width = residual.shape[1]
    part = width // CHUNKS

    scores = (
        jnp.einsum("thc,tpc->thp", queries, latent_cache, preferred_element_type=jnp.float32)
        * score_scale
    )
    position = lax.broadcasted_iota(jnp.int32, (1, 1, latent_cache.shape[1]), 2)
    usable = position < cache_length[:, None, None]
    masked = jnp.where(usable, scores, -1e30)
    highest = jnp.max(masked, axis=2, keepdims=True)
    expos = jnp.where(usable, jnp.exp(masked - highest), 0.0)
    weights = (expos / jnp.sum(expos, axis=2, keepdims=True)).astype(jnp.bfloat16)
    latent_out = jnp.einsum(
        "thp,tpc->thc", weights, latent_cache, preferred_element_type=jnp.float32
    )[:, :, :latent_width].astype(jnp.bfloat16)

    by_heads = lax.all_to_all(latent_out, "dev", split_axis=1, concat_axis=0, tiled=True)
    head_out = jnp.einsum(
        "thc,hcv->thv", by_heads, value_up, preferred_element_type=jnp.float32
    ).astype(jnp.bfloat16)
    head_flat = head_out.reshape(head_out.shape[0], -1)
    attended = []
    for i in range(CHUNKS):
        columns = out_weight[:, i * part : (i + 1) * part]
        product = jnp.dot(head_flat, columns, preferred_element_type=jnp.float32)
        attended.append(sum_scatter(product.astype(jnp.bfloat16), token_count))
    attended = jnp.concatenate(attended, axis=1)
    stream = (residual.astype(jnp.float32) + attended).astype(jnp.bfloat16)
    stream_float = stream.astype(jnp.float32)
    mean_square = jnp.mean(stream_float * stream_float, axis=1, keepdims=True)
    normed = (stream_float * lax.rsqrt(mean_square + 1e-06) * norm_gain).astype(jnp.bfloat16)

    levels = gate_level.astype(jnp.float32)
    mix = levels / jnp.sum(levels, axis=1, keepdims=True)
    lane = lax.broadcasted_iota(jnp.int32, (1, 1, LANES), 2)
    mix_of = jnp.sum(
        jnp.where(expert_index[:, :, None] == lane % EXPERTS, mix[:, :, None], 0.0), axis=1
    )
    high = lax.reduce_precision(mix_of, 8, 7)
    mix_row = jnp.where(lane[0] < EXPERTS, high, mix_of - high).astype(jnp.bfloat16)

    rows = []
    for i in range(CHUNKS):
        piece = normed[:, i * part : (i + 1) * part]
        if i == CHUNKS - 1:
            piece = jnp.concatenate([piece, mix_row], axis=1)
        rows.append(gather_rows(piece).reshape(group_size * token_count, -1))
    mix_rows = rows[-1][:, part:].astype(jnp.float32)
    rows[-1] = rows[-1][:, :part]
    rows = jnp.concatenate(rows, axis=1)
    mine = me // (group_size // EXPERTS)
    mix_mine = jnp.sum(
        jnp.where((lane[0] < 2 * EXPERTS) & (lane[0] % EXPERTS == mine), mix_rows, 0.0),
        axis=1,
        keepdims=True,
    )

    gate_hidden = jnp.dot(rows, gate_weight, preferred_element_type=jnp.float32)
    up_hidden = jnp.dot(rows, up_weight, preferred_element_type=jnp.float32)
    activated = (jax.nn.silu(gate_hidden) * up_hidden).astype(jnp.bfloat16)
    order = activated.reshape(2, pairs, token_count, -1)
    mixes = mix_mine.reshape(2, pairs, token_count, 1)
    slow_of = jnp.arange(pairs) ^ slow
    fast_of = jnp.arange(2) ^ fast
    order = jnp.transpose(order[fast_of][:, slow_of], (1, 0, 2, 3)).reshape(rows.shape[0], -1)
    mixes = jnp.transpose(mixes[fast_of][:, slow_of], (1, 0, 2, 3)).reshape(rows.shape[0], 1)
    moe = []
    for i in range(CHUNKS):
        columns = down_weight[:, i * part : (i + 1) * part]
        product = jnp.dot(order, columns, preferred_element_type=jnp.float32) * mixes
        moe.append(sum_scatter(product.astype(jnp.bfloat16), token_count))
    moe = jnp.concatenate(moe, axis=1)
    result = (stream_float + moe).astype(jnp.bfloat16)
    return jnp.where(attending, result, jnp.zeros_like(result))


def solution(mesh):
    placed = (
        P(("sec", "dev"), None, None),
        P(("sec", "dev"), None, None),
        P(("sec", "dev")),
        P(("sec", "dev"), None),
        P(),
        P("dev", None, None),
        P("dev", None),
        P(None, "dev"),
        P(None, "dev"),
        P("dev", None),
        P(("sec", "dev"), None),
        P(("sec", "dev"), None),
    )
    return jax.shard_map(
        layer_block,
        mesh=mesh,
        in_specs=placed,
        out_specs=P(("sec", "dev"), None),
        check_vma=False,
    )
```

time: 339 us -> 130 us (0.38)
  blocking collectives: 154 us -> 0 us
  waiting for transfers between devices: 98.5 us -> 38.2 us
  starting transfers between devices: 9.44 us -> 41.6 us
  between operations: 13.7 us -> 0.51 us
  local copies, waits for them, and re-layouts: 15.2 us -> 4.66 us
    all_to_all x3 -> x0, blocking collectives: 154 us -> none  [the longest x1 66.7 us: layer_block(): lax.all_to_all(spread, 'dev', split_axis=0, concat_axis=0, tiled=True)]
    reduce_scatter x1 -> x0, waiting for transfers between devices: 61.9 us -> none  [layer_block(): lax.psum_scatter(jnp.dot(head_flat, out_weight, preferred_element_type=jn...]
    ppermute x6 -> x24, starting transfers between devices: 9.44 us -> 34.3 us  [swap(): return lax.ppermute(x, 'dev', [(i, i ^ by) for i in range(size)])]
    all_to_all x0 -> x1, waiting for transfers between devices: none -> 14.2 us  [layer_block(): lax.all_to_all(latent_out, 'dev', split_axis=1, concat_axis=0, tiled=True)]
    ppermute x6 -> x24, waiting for transfers between devices: 36.6 us -> 24 us  [swap(): return lax.ppermute(x, 'dev', [(i, i ^ by) for i in range(size)])]
    all_to_all x0 -> x1, starting transfers between devices: none -> 7.28 us  [layer_block(): lax.all_to_all(latent_out, 'dev', split_axis=1, concat_axis=0, tiled=True)]
    reshape x3 -> x0, local copies, waits for them, and re-layouts: 7.1 us -> none  [the longest x1 4.13 us: layer_block(): partial_out.reshape(group_size, last_section, slot_width, width)]
    dot_general x5 -> x6, matrix products: 28.6 us -> 28.6 us  [the longest x2 9.02 us: layer_block(): jnp.dot(order, columns, preferred_element_type=jnp.float32) * mixes]
  transfers between devices with their start and end apart: 7 -> 25, of which waited for: 5 -> 11; matrix products, arithmetic and copies ran while one was open for 1% -> 1% of each run, Pallas kernels for 0% -> 0%
where the time goes in v1:
time: 130 us; the launch traced here: 129 us
  matrix products  41.8 us (32%)
  starting transfers between devices  41.6 us (32%)
  waiting for transfers between devices  38.2 us (29%)
  local copies, waits for them, and re-layouts  4.66 us (4%)
  other arithmetic  2.58 us (2%)
    ppermute x24, starting transfers between devices, swap(): return lax.ppermute(x, 'dev', [(i, i ^ by) for i in range(size)])  34.3 us
    ppermute x24, waiting for transfers between devices, swap(): return lax.ppermute(x, 'dev', [(i, i ^ by) for i in range(size)])  24 us
    all_to_all x1, waiting for transfers between devices, layer_block(): lax.all_to_all(latent_out, 'dev', split_axis=1, concat_axis=0, tiled=True)  14.2 us
    dot_general x2, matrix products, layer_block(): jnp.dot(order, columns, preferred_element_type=jnp.float32) * mixes  9.02 us
    dot_general x2, matrix products, layer_block(): product = jnp.dot(head_flat, columns, preferred_element_type=jnp.float32)  8.98 us
    dot_general x1, matrix products, layer_block(): gate_hidden = jnp.dot(rows, gate_weight, preferred_element_type=jnp.float32)  7.98 us
    all_to_all x1, starting transfers between devices, layer_block(): lax.all_to_all(latent_out, 'dev', split_axis=1, concat_axis=0, tiled=True)  7.28 us
    dot_general x1, matrix products, layer_block(): jnp.einsum('thp,tpc->thc', weights, latent_cache, preferred_element_type=...  6.6 us
  transfers between devices with their start and end apart: 25, of which 11 were waited for; matrix products, arithmetic and copies ran while one was open for 1% of the time, Pallas kernels for 0%

profile of v1, /device:TPU:0, one launch (start us, length us, event | category | flops | bytes accessed | tf_op | source)
XLA Modules:
  0.0 129.4 jit_solution(15851407326788638733)
XLA Ops:
  0.8 6.2 %fusion.71 = (f32[8,64]{1,0:T(8,128)S(1)}, f32[8,64,1024]{2,1,0:T(8,128)S(1)}) fusion(pred[8,1024]{1,0:T(8,128)(4,1)S(1)} %iota_compare_fusion, bf16[8,64,576]{2,1,0:T(8,128)(2,1)} %param.12, bf16[8,1024,576]{1,2,0:T(8,128)(2,1)} %param.13), kind=kOutput, calls=%fused_computation.118 | convolution fusion | flops 606602240 | bytes 12134400 | tf_op jit(solution)/shard_map/sub | solution.py:73
  7.1 6.6 %fusion.30 = bf16[8,64,576]{2,1,0:T(8,128)(2,1)S(1)} fusion(bf16[8,1024,576]{1,2,0:T(8,128)(2,1)} %param.13, f32[8,64,1024]{2,1,0:T(8,128)S(1)} %get-tuple-element.29, f32[8,64]{1,0:T(8,128)S(1)} %get-tuple-element.28), kind=kOutput, calls=%fused_computation.27 | convolution fusion | flops 605028352 | bytes 12126208 | tf_op jit(solution)/shard_map/thp,tpc->thc/dot_general | solution.py:75
  14.8 7.3 %all-to-all-start = ((bf16[8,64,512]{2,0,1:T(8,128)(2,1)}), bf16[8,64,512]{2,0,1:T(8,128)(2,1)S(1)}, u32[]{:S(2)}, u32[]{:S(2)}) async-start(bf16[8,64,512]{2,0,1:T(8,128)(2,1)} %copy.54), calls=%async_computation | async-start | bytes 1048576 | tf_op jit(solution)/shard_map/all_to_all | solution.py:79
  22.4 14.2 %all-to-all-done = bf16[8,64,512]{2,0,1:T(8,128)(2,1)S(1)} async-done(((bf16[8,64,512]{2,0,1:T(8,128)(2,1)}), bf16[8,64,512]{2,0,1:T(8,128)(2,1)S(1)}, u32[]{:S(2)}, u32[]{:S(2)}) %all-to-all-start) | async-done | bytes 524320 | tf_op jit(solution)/shard_map/all_to_all | solution.py:79
  36.9 4.5 %fusion.24 = bf16[64,3584]{1,0:T(8,128)(2,1)S(1)} fusion(bf16[1024,7168]{1,0:T(8,128)(2,1)} %param.18, bf16[8,8,8,128]{3,2,1,0:T(8,128)(2,1)S(1)} %fusion.29), kind=kOutput, calls=%fused_computation.18 | convolution fusion | flops 469991424 | bytes 7929856 | tf_op jit(solution)/shard_map/dot_general | solution.py:87
  41.4 4.5 %fusion.21 = bf16[64,3584]{1,0:T(8,128)(2,1)S(1)} fusion(bf16[1024,7168]{1,0:T(8,128)(2,1)} %param.18, bf16[8,8,8,128]{3,2,1,0:T(8,128)(2,1)S(1)} %fusion.29), kind=kOutput, calls=%fused_computation.17 | convolution fusion | flops 469991424 | bytes 7929856 | tf_op jit(solution)/shard_map/dot_general | solution.py:87
  46.0 1.5 %collective-permute-start.4 = (bf16[4,8,3584]{2,1,0:T(8,128)(2,1)S(1)}, bf16[4,8,3584]{2,1,0:T(8,128)(2,1)S(1)}, u32[]{:S(2)}, u32[]{:S(2)}) collective-permute-start(bf16[4,8,3584]{2,1,0:T(8,128)(2,1)S(1)} %dynamic-slice_bitcast_fusion.2), channel_id=1, source_target_pairs={{0,1},{1,0},{2,3},{3,2},{4,5},{5,4},{6,7},{7,6},{8,9},{9,8},{10,11... | collective-permute-start | bytes 688136 | tf_op jit(solution)/shard_map/ppermute | solution.py:13
  48.1 6.4 %collective-permute-done.4 = bf16[4,8,3584]{2,1,0:T(8,128)(2,1)S(1)} collective-permute-done((bf16[4,8,3584]{2,1,0:T(8,128)(2,1)S(1)}, bf16[4,8,3584]{2,1,0:T(8,128)(2,1)S(1)}, u32[]{:S(2)}, u32[]{:S(2)}) %collective-permute-start.4) | collective-permute-done | bytes 229408 | tf_op jit(solution)/shard_map/ppermute | solution.py:13
  54.7 1.7 %collective-permute-start.6 = (bf16[8,3584]{1,0:T(8,128)(2,1)S(1)}, bf16[8,3584]{1,0:T(8,128)(2,1)S(1)}, u32[]{:S(2)}, u32[]{:S(2)}) collective-permute-start(bf16[8,3584]{1,0:T(8,128)(2,1)S(1)} %get-tuple-element.22), channel_id=1, source_target_pairs={{0,4},{1,5},{2,6},{3,7},{4,0},{5,1},{6,2},{7,3},{8,12},{9,13},{10,... | collective-permute-start | bytes 172040 | tf_op jit(solution)/shard_map/ppermute | solution.py:13
  56.4 2.7 %collective-permute-start.5 = (bf16[8,3584]{1,0:T(8,128)(2,1)S(1)}, bf16[8,3584]{1,0:T(8,128)(2,1)S(1)}, u32[]{:S(2)}, u32[]{:S(2)}) collective-permute-start(bf16[8,3584]{1,0:T(8,128)(2,1)S(1)} %get-tuple-element.20), channel_id=1, source_target_pairs={{0,6},{1,7},{2,4},{3,5},{4,2},{5,3},{6,0},{7,1},{8,14},{9,15},{10,... | collective-permute-start | bytes 172040 | tf_op jit(solution)/shard_map/ppermute | solution.py:13
  59.3 1.7 %collective-permute-start.2 = (bf16[8,3584]{1,0:T(8,128)(2,1)S(1)}, bf16[8,3584]{1,0:T(8,128)(2,1)S(1)}, u32[]{:S(2)}, u32[]{:S(2)}) collective-permute-start(bf16[8,3584]{1,0:T(8,128)(2,1)S(1)} %get-tuple-element.19), channel_id=1, source_target_pairs={{0,4},{1,5},{2,6},{3,7},{4,0},{5,1},{6,2},{7,3},{8,12},{9,13},{10,... | collective-permute-start | bytes 172040 | tf_op jit(solution)/shard_map/ppermute | solution.py:13
  60.9 2.7 %collective-permute-start.1 = (bf16[8,3584]{1,0:T(8,128)(2,1)S(1)}, bf16[8,3584]{1,0:T(8,128)(2,1)S(1)}, u32[]{:S(2)}, u32[]{:S(2)}) collective-permute-start(bf16[8,3584]{1,0:T(8,128)(2,1)S(1)} %get-tuple-element.17), channel_id=1, source_target_pairs={{0,6},{1,7},{2,4},{3,5},{4,2},{5,3},{6,0},{7,1},{8,14},{9,15},{10,... | collective-permute-start | bytes 172040 | tf_op jit(solution)/shard_map/ppermute | solution.py:13
  64.8 2.1 %collective-permute-done.1 = bf16[8,3584]{1,0:T(8,128)(2,1)S(1)} collective-permute-done((bf16[8,3584]{1,0:T(8,128)(2,1)S(1)}, bf16[8,3584]{1,0:T(8,128)(2,1)S(1)}, u32[]{:S(2)}, u32[]{:S(2)}) %collective-permute-start.1) | collective-permute-done | bytes 57376 | tf_op jit(solution)/shard_map/ppermute | solution.py:13
  67.3 2.8 %collective-permute-start.10 = (bf16[8,3584]{1,0:T(8,128)(2,1)S(1)}, bf16[8,3584]{1,0:T(8,128)(2,1)S(1)}, u32[]{:S(2)}, u32[]{:S(2)}) collective-permute-start(bf16[8,3584]{1,0:T(8,128)(2,1)S(1)} %get-tuple-element.25), channel_id=1, source_target_pairs={{0,6},{1,7},{2,4},{3,5},{4,2},{5,3},{6,0},{7,1},{8,14},{9,15},{10,... | collective-permute-start | bytes 172040 | tf_op jit(solution)/shard_map/ppermute | solution.py:13
  70.1 1.7 %collective-permute-start.8 = (bf16[8,3584]{1,0:T(8,128)(2,1)S(1)}, bf16[8,3584]{1,0:T(8,128)(2,1)S(1)}, u32[]{:S(2)}, u32[]{:S(2)}) collective-permute-start(bf16[8,3584]{1,0:T(8,128)(2,1)S(1)} %get-tuple-element.25), channel_id=1, source_target_pairs={{0,2},{1,3},{2,0},{3,1},{4,6},{5,7},{6,4},{7,5},{8,10},{9,11},{10,... | collective-permute-start | bytes 172040 | tf_op jit(solution)/shard_map/ppermute | solution.py:13
  71.7 2.8 %collective-permute-start.14 = (bf16[8,3712]{1,0:T(8,128)(2,1)S(1)}, bf16[8,3712]{1,0:T(8,128)(2,1)S(1)}, u32[]{:S(2)}, u32[]{:S(2)}) collective-permute-start(bf16[8,3712]{1,0:T(8,128)(2,1)S(1)} %get-tuple-element.27), channel_id=1, source_target_pairs={{0,6},{1,7},{2,4},{3,5},{4,2},{5,3},{6,0},{7,1},{8,14},{9,15},{10,... | collective-permute-start | bytes 178184 | tf_op jit(solution)/shard_map/ppermute | solution.py:13
  74.5 1.7 %collective-permute-start.12 = (bf16[8,3712]{1,0:T(8,128)(2,1)S(1)}, bf16[8,3712]{1,0:T(8,128)(2,1)S(1)}, u32[]{:S(2)}, u32[]{:S(2)}) collective-permute-start(bf16[8,3712]{1,0:T(8,128)(2,1)S(1)} %get-tuple-element.27), channel_id=1, source_target_pairs={{0,2},{1,3},{2,0},{3,1},{4,6},{5,7},{6,4},{7,5},{8,10},{9,11},{10,... | collective-permute-start | bytes 178184 | tf_op jit(solution)/shard_map/ppermute | solution.py:13
  76.3 1.8 %collective-permute-start.11 = (bf16[4,8,3584]{2,1,0:T(8,128)(2,1)S(1)}, bf16[4,8,3584]{2,1,0:T(8,128)(2,1)S(1)}, u32[]{:S(2)}, u32[]{:S(2)}) collective-permute-start(bf16[4,8,3584]{2,1,0:T(8,128)(2,1)S(1)} %get-tuple-element.16), channel_id=1, source_target_pairs={{0,1},{1,0},{2,3},{3,2},{4,5},{5,4},{6,7},{7,6},{8,9},{9,8},{10,11... | collective-permute-start | bytes 688136 | tf_op jit(solution)/shard_map/ppermute | solution.py:13
  78.1 1.6 %collective-permute-done.13 = bf16[8,3712]{1,0:T(8,128)(2,1)S(1)} collective-permute-done((bf16[8,3712]{1,0:T(8,128)(2,1)S(1)}, bf16[8,3712]{1,0:T(8,128)(2,1)S(1)}, u32[]{:S(2)}, u32[]{:S(2)}) %collective-permute-start.13) | collective-permute-done | bytes 59424 | tf_op jit(solution)/shard_map/ppermute | solution.py:13
  79.7 1.5 %collective-permute-start.15 = (bf16[4,8,3712]{2,1,0:T(8,128)(2,1)S(1)}, bf16[4,8,3712]{2,1,0:T(8,128)(2,1)S(1)}, u32[]{:S(2)}, u32[]{:S(2)}) collective-permute-start(bf16[4,8,3712]{2,1,0:T(8,128)(2,1)S(1)} %get-tuple-element.8), channel_id=1, source_target_pairs={{0,1},{1,0},{2,3},{3,2},{4,5},{5,4},{6,7},{7,6},{8,9},{9,8},{10,11... | collective-permute-start | bytes 712712 | tf_op jit(solution)/shard_map/ppermute | solution.py:13
  81.2 2.7 %collective-permute-done.11 = bf16[4,8,3584]{2,1,0:T(8,128)(2,1)S(1)} collective-permute-done((bf16[4,8,3584]{2,1,0:T(8,128)(2,1)S(1)}, bf16[4,8,3584]{2,1,0:T(8,128)(2,1)S(1)}, u32[]{:S(2)}, u32[]{:S(2)}) %collective-permute-start.11) | collective-permute-done | bytes 229408 | tf_op jit(solution)/shard_map/ppermute | solution.py:13
  84.0 2.5 %collective-permute-done.15 = bf16[4,8,3712]{2,1,0:T(8,128)(2,1)S(1)} collective-permute-done((bf16[4,8,3712]{2,1,0:T(8,128)(2,1)S(1)}, bf16[4,8,3712]{2,1,0:T(8,128)(2,1)S(1)}, u32[]{:S(2)}, u32[]{:S(2)}) %collective-permute-start.15) | collective-permute-done | bytes 237600 | tf_op jit(solution)/shard_map/ppermute | solution.py:13
  86.8 8.0 %fusion.35 = f32[64,1024]{1,0:T(8,128)S(1)} fusion(bf16[7168,1024]{1,0:T(8,128)(2,1)} %param.19, bf16[64,3584]{1,0:T(8,128)(2,1)S(1)} %slice.48, bf16[64,3584]{1,0:T(8,128)(2,1)S(1)} %bitcast.124), kind=kOutput, calls=%fused_computation.34 | convolution fusion | flops 941359104 | bytes 15859712 | tf_op jit(solution)/shard_map/dot_general | solution.py:120
  95.6 2.7 %fusion.28 = bf16[64,1024]{1,0:T(8,128)(2,1)S(1)} fusion(bf16[7168,1024]{1,0:T(8,128)(2,1)S(1)} %bitcast.123, bf16[64,3584]{1,0:T(8,128)(2,1)S(1)} %slice.48, bf16[64,3584]{1,0:T(8,128)(2,1)S(1)} %bitcast.125, f32[64,1024]{1,0:T(8,128)S(1)} %fusion.35), kind=kOutput, calls=%fused_computation.24 | convolution fusion | flops 941752320 | bytes 15990784 | tf_op jit(solution)/shard_map/dot_general | solution.py:121
  100.7 4.6 %fusion.15 = bf16[64,3584]{1,0:T(8,128)(2,1)S(1)} fusion(bf16[64,1024]{1,0:T(8,128)(2,1)S(1)} %bitcast.140, bf16[1024,7168]{1,0:T(8,128)(2,1)} %param.21, f32[64]{0:T(128)S(1)} %mul.57), kind=kOutput, calls=%fused_computation.15 | convolution fusion | flops 470220800 | bytes 7930112 | tf_op jit(solution)/shard_map/dot_general | solution.py:132
  105.2 4.5 %fusion.18 = bf16[64,3584]{1,0:T(8,128)(2,1)S(1)} fusion(bf16[64,1024]{1,0:T(8,128)(2,1)S(1)} %bitcast.141, bf16[1024,7168]{1,0:T(8,128)(2,1)} %param.21, f32[64]{0:T(128)S(1)} %mul.57), kind=kOutput, calls=%fused_computation.16 | convolution fusion | flops 470220800 | bytes 7930112 | tf_op jit(solution)/shard_map/dot_general | solution.py:132
  109.7 1.7 %collective-permute-start.20 = (bf16[4,8,3584]{2,1,0:T(8,128)(2,1)S(1)}, bf16[4,8,3584]{2,1,0:T(8,128)(2,1)S(1)}, u32[]{:S(2)}, u32[]{:S(2)}) collective-permute-start(bf16[4,8,3584]{2,1,0:T(8,128)(2,1)S(1)} %dynamic-slice_bitcast_fusion), channel_id=1, source_target_pairs={{0,1},{1,0},{2,3},{3,2},{4,5},{5,4},{6,7},{7,6},{8,9},{9,8},{10,11... | collective-permute-start | bytes 688136 | tf_op jit(solution)/shard_map/ppermute | solution.py:13
  111.9 4.6 %collective-permute-done.20 = bf16[4,8,3584]{2,1,0:T(8,128)(2,1)S(1)} collective-permute-done((bf16[4,8,3584]{2,1,0:T(8,128)(2,1)S(1)}, bf16[4,8,3584]{2,1,0:T(8,128)(2,1)S(1)}, u32[]{:S(2)}, u32[]{:S(2)}) %collective-permute-start.20) | collective-permute-done | bytes 229408 | tf_op jit(solution)/shard_map/ppermute | solution.py:13
  118.1 2.9 %collective-permute-start.21 = (bf16[8,3584]{1,0:T(8,128)(2,1)S(1)}, bf16[8,3584]{1,0:T(8,128)(2,1)S(1)}, u32[]{:S(2)}, u32[]{:S(2)}) collective-permute-start(bf16[8,3584]{1,0:T(8,128)(2,1)S(1)} %get-tuple-element.12), channel_id=1, source_target_pairs={{0,6},{1,7},{2,4},{3,5},{4,2},{5,3},{6,0},{7,1},{8,14},{9,15},{10,... | collective-permute-start | bytes 172040 | tf_op jit(solution)/shard_map/ppermute | solution.py:13
  121.2 1.5 %collective-permute-start.18 = (bf16[8,3584]{1,0:T(8,128)(2,1)S(1)}, bf16[8,3584]{1,0:T(8,128)(2,1)S(1)}, u32[]{:S(2)}, u32[]{:S(2)}) collective-permute-start(bf16[8,3584]{1,0:T(8,128)(2,1)S(1)} %get-tuple-element.11), channel_id=1, source_target_pairs={{0,4},{1,5},{2,6},{3,7},{4,0},{5,1},{6,2},{7,3},{8,12},{9,13},{10,... | collective-permute-start | bytes 172040 | tf_op jit(solution)/shard_map/ppermute | solution.py:13
  122.7 2.9 %collective-permute-start.17 = (bf16[8,3584]{1,0:T(8,128)(2,1)S(1)}, bf16[8,3584]{1,0:T(8,128)(2,1)S(1)}, u32[]{:S(2)}, u32[]{:S(2)}) collective-permute-start(bf16[8,3584]{1,0:T(8,128)(2,1)S(1)} %get-tuple-element.9), channel_id=1, source_target_pairs={{0,6},{1,7},{2,4},{3,5},{4,2},{5,3},{6,0},{7,1},{8,14},{9,15},{10,... | collective-permute-start | bytes 172040 | tf_op jit(solution)/shard_map/ppermute | solution.py:13
  126.3 2.3 %collective-permute-done.17 = bf16[8,3584]{1,0:T(8,128)(2,1)S(1)} collective-permute-done((bf16[8,3584]{1,0:T(8,128)(2,1)S(1)}, bf16[8,3584]{1,0:T(8,128)(2,1)S(1)}, u32[]{:S(2)}, u32[]{:S(2)}) %collective-permute-start.17) | collective-permute-done | bytes 57376 | tf_op jit(solution)/shard_map/ppermute | solution.py:13
  (99 shorter events, 12.2 us)
Async XLA Ops:
  0.0 36.6 %copy-start = (bf16[8,512,128]{2,1,0:T(8,128)(2,1)S(1)}, bf16[8,512,128]{2,1,0:T(8,128)(2,1)}, u32[]{:S(2)}) copy-start(bf16[8,512,128]{2,1,0:T(8,128)(2,1)} %param.17) | copy-start | bytes 3145732
  7.0 15.2 %copy-start.4 = (s32[8,2]{0,1:T(2,128)S(1)}, s32[8,2]{0,1:T(2,128)}, u32[]{:S(2)}) copy-start(s32[8,2]{0,1:T(2,128)} %param.23) | copy-start | bytes 196
  7.1 15.2 %copy-start.5 = (s32[8,2]{0,1:T(2,128)S(1)}, s32[8,2]{0,1:T(2,128)}, u32[]{:S(2)}) copy-start(s32[8,2]{0,1:T(2,128)} %param.22) | copy-start | bytes 196
  14.8 21.8 %all-to-all-start = ((bf16[8,64,512]{2,0,1:T(8,128)(2,1)}), bf16[8,64,512]{2,0,1:T(8,128)(2,1)S(1)}, u32[]{:S(2)}, u32[]{:S(2)}) async-start(bf16[8,64,512]{2,0,1:T(8,128)(2,1)} %copy.54), calls=%async_computation | async-start | bytes 1048576 | tf_op jit(solution)/shard_map/all_to_all | solution.py:79
  41.4 25.6 %copy-start.2 = (bf16[8,7168]{1,0:T(8,128)(2,1)S(1)}, bf16[8,7168]{1,0:T(8,128)(2,1)}, u32[]{:S(2)}) copy-start(bf16[8,7168]{1,0:T(8,128)(2,1)} %param.15) | copy-start | bytes 344068
  41.4 25.7 %copy-start.3 = (f32[7168]{0:T(1024)S(1)}, f32[7168]{0:T(1024)}, u32[]{:S(2)}) copy-start(f32[7168]{0:T(1024)} %param.16) | copy-start | bytes 86020
  46.0 8.6 %collective-permute-start.4 = (bf16[4,8,3584]{2,1,0:T(8,128)(2,1)S(1)}, bf16[4,8,3584]{2,1,0:T(8,128)(2,1)S(1)}, u32[]{:S(2)}, u32[]{:S(2)}) collective-permute-start(bf16[4,8,3584]{2,1,0:T(8,128)(2,1)S(1)} %dynamic-slice_bitcast_fusion.2), channel_id=1, source_target_pairs={{0,1},{1,0},{2,3},{3,2},{4,5},{5,4},{6,7},{7,6},{8,9},{9,8},{10,11... | collective-permute-start | bytes 688136 | tf_op jit(solution)/shard_map/ppermute | solution.py:13
  47.5 11.6 %collective-permute-start = (bf16[4,8,3584]{2,1,0:T(8,128)(2,1)S(1)}, bf16[4,8,3584]{2,1,0:T(8,128)(2,1)S(1)}, u32[]{:S(2)}, u32[]{:S(2)}) collective-permute-start(bf16[4,8,3584]{2,1,0:T(8,128)(2,1)S(1)} %dynamic-slice_bitcast_fusion.3), channel_id=1, source_target_pairs={{0,1},{1,0},{2,3},{3,2},{4,5},{5,4},{6,7},{7,6},{8,9},{9,8},{10,11... | collective-permute-start | bytes 688136 | tf_op jit(solution)/shard_map/ppermute | solution.py:13
  54.7 6.3 %collective-permute-start.7 = (bf16[8,3584]{1,0:T(8,128)(2,1)S(1)}, bf16[8,3584]{1,0:T(8,128)(2,1)S(1)}, u32[]{:S(2)}, u32[]{:S(2)}) collective-permute-start(bf16[8,3584]{1,0:T(8,128)(2,1)S(1)} %get-tuple-element.21), channel_id=1, source_target_pairs={{0,2},{1,3},{2,0},{3,1},{4,6},{5,7},{6,4},{7,5},{8,10},{9,11},{10,... | collective-permute-start | bytes 172040 | tf_op jit(solution)/shard_map/ppermute | solution.py:13
  54.7 8.9 %collective-permute-start.6 = (bf16[8,3584]{1,0:T(8,128)(2,1)S(1)}, bf16[8,3584]{1,0:T(8,128)(2,1)S(1)}, u32[]{:S(2)}, u32[]{:S(2)}) collective-permute-start(bf16[8,3584]{1,0:T(8,128)(2,1)S(1)} %get-tuple-element.22), channel_id=1, source_target_pairs={{0,4},{1,5},{2,6},{3,7},{4,0},{5,1},{6,2},{7,3},{8,12},{9,13},{10,... | collective-permute-start | bytes 172040 | tf_op jit(solution)/shard_map/ppermute | solution.py:13
  56.4 7.3 %collective-permute-start.5 = (bf16[8,3584]{1,0:T(8,128)(2,1)S(1)}, bf16[8,3584]{1,0:T(8,128)(2,1)S(1)}, u32[]{:S(2)}, u32[]{:S(2)}) collective-permute-start(bf16[8,3584]{1,0:T(8,128)(2,1)S(1)} %get-tuple-element.20), channel_id=1, source_target_pairs={{0,6},{1,7},{2,4},{3,5},{4,2},{5,3},{6,0},{7,1},{8,14},{9,15},{10,... | collective-permute-start | bytes 172040 | tf_op jit(solution)/shard_map/ppermute | solution.py:13
  59.2 5.0 %collective-permute-start.3 = (bf16[8,3584]{1,0:T(8,128)(2,1)S(1)}, bf16[8,3584]{1,0:T(8,128)(2,1)S(1)}, u32[]{:S(2)}, u32[]{:S(2)}) collective-permute-start(bf16[8,3584]{1,0:T(8,128)(2,1)S(1)} %get-tuple-element.18), channel_id=1, source_target_pairs={{0,2},{1,3},{2,0},{3,1},{4,6},{5,7},{6,4},{7,5},{8,10},{9,11},{10,... | collective-permute-start | bytes 172040 | tf_op jit(solution)/shard_map/ppermute | solution.py:13
  59.3 5.5 %collective-permute-start.2 = (bf16[8,3584]{1,0:T(8,128)(2,1)S(1)}, bf16[8,3584]{1,0:T(8,128)(2,1)S(1)}, u32[]{:S(2)}, u32[]{:S(2)}) collective-permute-start(bf16[8,3584]{1,0:T(8,128)(2,1)S(1)} %get-tuple-element.19), channel_id=1, source_target_pairs={{0,4},{1,5},{2,6},{3,7},{4,0},{5,1},{6,2},{7,3},{8,12},{9,13},{10,... | collective-permute-start | bytes 172040 | tf_op jit(solution)/shard_map/ppermute | solution.py:13
  60.9 6.0 %collective-permute-start.1 = (bf16[8,3584]{1,0:T(8,128)(2,1)S(1)}, bf16[8,3584]{1,0:T(8,128)(2,1)S(1)}, u32[]{:S(2)}, u32[]{:S(2)}) collective-permute-start(bf16[8,3584]{1,0:T(8,128)(2,1)S(1)} %get-tuple-element.17), channel_id=1, source_target_pairs={{0,6},{1,7},{2,4},{3,5},{4,2},{5,3},{6,0},{7,1},{8,14},{9,15},{10,... | collective-permute-start | bytes 172040 | tf_op jit(solution)/shard_map/ppermute | solution.py:13
  67.3 7.3 %collective-permute-start.10 = (bf16[8,3584]{1,0:T(8,128)(2,1)S(1)}, bf16[8,3584]{1,0:T(8,128)(2,1)S(1)}, u32[]{:S(2)}, u32[]{:S(2)}) collective-permute-start(bf16[8,3584]{1,0:T(8,128)(2,1)S(1)} %get-tuple-element.25), channel_id=1, source_target_pairs={{0,6},{1,7},{2,4},{3,5},{4,2},{5,3},{6,0},{7,1},{8,14},{9,15},{10,... | collective-permute-start | bytes 172040 | tf_op jit(solution)/shard_map/ppermute | solution.py:13
  70.1 6.1 %collective-permute-start.9 = (bf16[8,3584]{1,0:T(8,128)(2,1)S(1)}, bf16[8,3584]{1,0:T(8,128)(2,1)S(1)}, u32[]{:S(2)}, u32[]{:S(2)}) collective-permute-start(bf16[8,3584]{1,0:T(8,128)(2,1)S(1)} %get-tuple-element.25), channel_id=1, source_target_pairs={{0,4},{1,5},{2,6},{3,7},{4,0},{5,1},{6,2},{7,3},{8,12},{9,13},{10,... | collective-permute-start | bytes 172040 | tf_op jit(solution)/shard_map/ppermute | solution.py:13
  70.1 6.1 %collective-permute-start.8 = (bf16[8,3584]{1,0:T(8,128)(2,1)S(1)}, bf16[8,3584]{1,0:T(8,128)(2,1)S(1)}, u32[]{:S(2)}, u32[]{:S(2)}) collective-permute-start(bf16[8,3584]{1,0:T(8,128)(2,1)S(1)} %get-tuple-element.25), channel_id=1, source_target_pairs={{0,2},{1,3},{2,0},{3,1},{4,6},{5,7},{6,4},{7,5},{8,10},{9,11},{10,... | collective-permute-start | bytes 172040 | tf_op jit(solution)/shard_map/ppermute | solution.py:13
  71.7 6.3 %collective-permute-start.14 = (bf16[8,3712]{1,0:T(8,128)(2,1)S(1)}, bf16[8,3712]{1,0:T(8,128)(2,1)S(1)}, u32[]{:S(2)}, u32[]{:S(2)}) collective-permute-start(bf16[8,3712]{1,0:T(8,128)(2,1)S(1)} %get-tuple-element.27), channel_id=1, source_target_pairs={{0,6},{1,7},{2,4},{3,5},{4,2},{5,3},{6,0},{7,1},{8,14},{9,15},{10,... | collective-permute-start | bytes 178184 | tf_op jit(solution)/shard_map/ppermute | solution.py:13
  74.5 5.1 %collective-permute-start.13 = (bf16[8,3712]{1,0:T(8,128)(2,1)S(1)}, bf16[8,3712]{1,0:T(8,128)(2,1)S(1)}, u32[]{:S(2)}, u32[]{:S(2)}) collective-permute-start(bf16[8,3712]{1,0:T(8,128)(2,1)S(1)} %get-tuple-element.27), channel_id=1, source_target_pairs={{0,4},{1,5},{2,6},{3,7},{4,0},{5,1},{6,2},{7,3},{8,12},{9,13},{10,... | collective-permute-start | bytes 178184 | tf_op jit(solution)/shard_map/ppermute | solution.py:13
  74.5 5.1 %collective-permute-start.12 = (bf16[8,3712]{1,0:T(8,128)(2,1)S(1)}, bf16[8,3712]{1,0:T(8,128)(2,1)S(1)}, u32[]{:S(2)}, u32[]{:S(2)}) collective-permute-start(bf16[8,3712]{1,0:T(8,128)(2,1)S(1)} %get-tuple-element.27), channel_id=1, source_target_pairs={{0,2},{1,3},{2,0},{3,1},{4,6},{5,7},{6,4},{7,5},{8,10},{9,11},{10,... | collective-permute-start | bytes 178184 | tf_op jit(solution)/shard_map/ppermute | solution.py:13
  76.3 7.7 %collective-permute-start.11 = (bf16[4,8,3584]{2,1,0:T(8,128)(2,1)S(1)}, bf16[4,8,3584]{2,1,0:T(8,128)(2,1)S(1)}, u32[]{:S(2)}, u32[]{:S(2)}) collective-permute-start(bf16[4,8,3584]{2,1,0:T(8,128)(2,1)S(1)} %get-tuple-element.16), channel_id=1, source_target_pairs={{0,1},{1,0},{2,3},{3,2},{4,5},{5,4},{6,7},{7,6},{8,9},{9,8},{10,11... | collective-permute-start | bytes 688136 | tf_op jit(solution)/shard_map/ppermute | solution.py:13
  79.7 6.8 %collective-permute-start.15 = (bf16[4,8,3712]{2,1,0:T(8,128)(2,1)S(1)}, bf16[4,8,3712]{2,1,0:T(8,128)(2,1)S(1)}, u32[]{:S(2)}, u32[]{:S(2)}) collective-permute-start(bf16[4,8,3712]{2,1,0:T(8,128)(2,1)S(1)} %get-tuple-element.8), channel_id=1, source_target_pairs={{0,1},{1,0},{2,3},{3,2},{4,5},{5,4},{6,7},{7,6},{8,9},{9,8},{10,11... | collective-permute-start | bytes 712712 | tf_op jit(solution)/shard_map/ppermute | solution.py:13
  83.9 10.8 %slice-start = ((s8[14680064]{0:T(1024)(128)(4,1)}), s8[2097152]{0:T(1024)(128)(4,1)S(1)}, s32[]{:S(2)}) async-start(s8[14680064]{0:T(1024)(128)(4,1)} %bitcast.122), calls=%async_computation.1 | async-start | bytes 4194304
  100.7 28.7 %copy-start.1 = (bf16[8,512,128]{2,1,0:T(8,128)(2,1)S(1)}, bf16[8,512,128]{2,1,0:T(8,128)(2,1)}, u32[]{:S(2)}) copy-start(bf16[8,512,128]{2,1,0:T(8,128)(2,1)} %param.17) | copy-start | bytes 3145732
  109.7 6.7 %collective-permute-start.20 = (bf16[4,8,3584]{2,1,0:T(8,128)(2,1)S(1)}, bf16[4,8,3584]{2,1,0:T(8,128)(2,1)S(1)}, u32[]{:S(2)}, u32[]{:S(2)}) collective-permute-start(bf16[4,8,3584]{2,1,0:T(8,128)(2,1)S(1)} %dynamic-slice_bitcast_fusion), channel_id=1, source_target_pairs={{0,1},{1,0},{2,3},{3,2},{4,5},{5,4},{6,7},{7,6},{8,9},{9,8},{10,11... | collective-permute-start | bytes 688136 | tf_op jit(solution)/shard_map/ppermute | solution.py:13
  111.5 9.5 %collective-permute-start.16 = (bf16[4,8,3584]{2,1,0:T(8,128)(2,1)S(1)}, bf16[4,8,3584]{2,1,0:T(8,128)(2,1)S(1)}, u32[]{:S(2)}, u32[]{:S(2)}) collective-permute-start(bf16[4,8,3584]{2,1,0:T(8,128)(2,1)S(1)} %dynamic-slice_bitcast_fusion.1), channel_id=1, source_target_pairs={{0,1},{1,0},{2,3},{3,2},{4,5},{5,4},{6,7},{7,6},{8,9},{9,8},{10,11... | collective-permute-start | bytes 688136 | tf_op jit(solution)/shard_map/ppermute | solution.py:13
  116.5 6.1 %collective-permute-start.23 = (bf16[8,3584]{1,0:T(8,128)(2,1)S(1)}, bf16[8,3584]{1,0:T(8,128)(2,1)S(1)}, u32[]{:S(2)}, u32[]{:S(2)}) collective-permute-start(bf16[8,3584]{1,0:T(8,128)(2,1)S(1)} %get-tuple-element.13), channel_id=1, source_target_pairs={{0,2},{1,3},{2,0},{3,1},{4,6},{5,7},{6,4},{7,5},{8,10},{9,11},{10,... | collective-permute-start | bytes 172040 | tf_op jit(solution)/shard_map/ppermute | solution.py:13
  116.6 8.9 %collective-permute-start.22 = (bf16[8,3584]{1,0:T(8,128)(2,1)S(1)}, bf16[8,3584]{1,0:T(8,128)(2,1)S(1)}, u32[]{:S(2)}, u32[]{:S(2)}) collective-permute-start(bf16[8,3584]{1,0:T(8,128)(2,1)S(1)} %get-tuple-element.14), channel_id=1, source_target_pairs={{0,4},{1,5},{2,6},{3,7},{4,0},{5,1},{6,2},{7,3},{8,12},{9,13},{10,... | collective-permute-start | bytes 172040 | tf_op jit(solution)/shard_map/ppermute | solution.py:13
  118.1 7.4 %collective-permute-start.21 = (bf16[8,3584]{1,0:T(8,128)(2,1)S(1)}, bf16[8,3584]{1,0:T(8,128)(2,1)S(1)}, u32[]{:S(2)}, u32[]{:S(2)}) collective-permute-start(bf16[8,3584]{1,0:T(8,128)(2,1)S(1)} %get-tuple-element.12), channel_id=1, source_target_pairs={{0,6},{1,7},{2,4},{3,5},{4,2},{5,3},{6,0},{7,1},{8,14},{9,15},{10,... | collective-permute-start | bytes 172040 | tf_op jit(solution)/shard_map/ppermute | solution.py:13
  121.1 4.5 %collective-permute-start.19 = (bf16[8,3584]{1,0:T(8,128)(2,1)S(1)}, bf16[8,3584]{1,0:T(8,128)(2,1)S(1)}, u32[]{:S(2)}, u32[]{:S(2)}) collective-permute-start(bf16[8,3584]{1,0:T(8,128)(2,1)S(1)} %get-tuple-element.10), channel_id=1, source_target_pairs={{0,2},{1,3},{2,0},{3,1},{4,6},{5,7},{6,4},{7,5},{8,10},{9,11},{10,... | collective-permute-start | bytes 172040 | tf_op jit(solution)/shard_map/ppermute | solution.py:13
  121.2 5.1 %collective-permute-start.18 = (bf16[8,3584]{1,0:T(8,128)(2,1)S(1)}, bf16[8,3584]{1,0:T(8,128)(2,1)S(1)}, u32[]{:S(2)}, u32[]{:S(2)}) collective-permute-start(bf16[8,3584]{1,0:T(8,128)(2,1)S(1)} %get-tuple-element.11), channel_id=1, source_target_pairs={{0,4},{1,5},{2,6},{3,7},{4,0},{5,1},{6,2},{7,3},{8,12},{9,13},{10,... | collective-permute-start | bytes 172040 | tf_op jit(solution)/shard_map/ppermute | solution.py:13
  122.7 6.0 %collective-permute-start.17 = (bf16[8,3584]{1,0:T(8,128)(2,1)S(1)}, bf16[8,3584]{1,0:T(8,128)(2,1)S(1)}, u32[]{:S(2)}, u32[]{:S(2)}) collective-permute-start(bf16[8,3584]{1,0:T(8,128)(2,1)S(1)} %get-tuple-element.9), channel_id=1, source_target_pairs={{0,6},{1,7},{2,4},{3,5},{4,2},{5,3},{6,0},{7,1},{8,14},{9,15},{10,... | collective-permute-start | bytes 172040 | tf_op jit(solution)/shard_map/ppermute | solution.py:13
  (3 other events, 24.9 us)

commit v2 on v1

v2 whole, which is shorter than its diff:
```python
import functools

import jax
import jax.numpy as jnp
from jax import lax
from jax.experimental import pallas as pl
from jax.experimental.pallas import tpu as pltpu
from jax.sharding import PartitionSpec as P

EXPERTS = 4
CHUNKS = 2
LANES = 128


def swap(x, by):
    size = lax.axis_size("dev")
    return lax.ppermute(x, "dev", [(i, i ^ by) for i in range(size)])


def sum_scatter(x, slabs):
    while slabs > 1:
        slabs = slabs // 2
        got = swap(x[:, slabs:], slabs)
        x = (x[:, :slabs].astype(jnp.float32) + got.astype(jnp.float32)).astype(jnp.bfloat16)
    step = lax.axis_size("dev") // x.shape[0]
    total = x[0, 0].astype(jnp.float32)
    for by in reversed(range(1, x.shape[0])):
        total = total + swap(x[by, 0], by * step).astype(jnp.float32)
    return total


def gather_rows(x, slabs):
    column = [x] + [None] * (EXPERTS - 1)
    for by in reversed(range(1, EXPERTS)):
        column[by] = swap(x, by * slabs)
    column = jnp.stack(column, axis=0)[:, None]
    by = 1
    while by < slabs:
        column = jnp.concatenate([column, swap(column, by)], axis=1)
        by = by * 2
    return column


def attend_kernel(scale, groups, place_ref, length_ref, query_ref, cache_ref, out_ref):
    step = pl.program_id(0)
    tokens = query_ref.shape[0]
    heads = query_ref.shape[1]
    latent_width = out_ref.shape[2]
    found = []
    for t in range(tokens):
        scores = lax.dot_general(
            query_ref[t],
            cache_ref[t],
            (((1,), (1,)), ((), ())),
            preferred_element_type=jnp.float32,
        )
        position = lax.broadcasted_iota(jnp.int32, scores.shape, 1)
        usable = position < length_ref[step * tokens + t]
        masked = jnp.where(usable, scores * scale, -1e30)
        highest = jnp.max(masked, axis=1, keepdims=True)
        expos = jnp.where(usable, jnp.exp(masked - highest), 0.0)
        total = jnp.sum(expos, axis=1, keepdims=True)
        summed = jnp.dot(
            expos.astype(jnp.bfloat16),
            cache_ref[t, :, :latent_width],
            preferred_element_type=jnp.float32,
        )
        found.append(summed / total)
    each = heads // groups
    for g in range(groups):
        block = jnp.concatenate([one[g * each : (g + 1) * each] for one in found], axis=0)
        out_ref[g ^ place_ref[0]] = block.astype(jnp.bfloat16)


def attend(queries, latent_cache, cache_length, me, groups, latent_width, scale):
    token_count, heads, key_width = queries.shape
    each = heads // groups
    together = max(2, 16 // each)
    rows = together * each
    return pl.pallas_call(
        functools.partial(attend_kernel, scale, groups),
        out_shape=jax.ShapeDtypeStruct((groups, token_count * each, latent_width), jnp.bfloat16),
        grid_spec=pltpu.PrefetchScalarGridSpec(
            num_scalar_prefetch=2,
            grid=(token_count // together,),
            in_specs=[
                pl.BlockSpec((together, heads, key_width), lambda i, *_: (i, 0, 0)),
                pl.BlockSpec(
                    (together, latent_cache.shape[1], key_width), lambda i, *_: (i, 0, 0)
                ),
            ],
            out_specs=pl.BlockSpec((groups, rows, latent_width), lambda i, *_: (0, i, 0)),
        ),
        compiler_params=pltpu.CompilerParams(vmem_limit_bytes=24 * 1024 * 1024),
        cost_estimate=pl.CostEstimate(
            flops=2 * token_count * heads * latent_cache.shape[1] * (key_width + latent_width),
            bytes_accessed=2 * latent_cache.size,
            transcendentals=token_count * heads * latent_cache.shape[1],
        ),
    )(me.reshape(1), cache_length, queries, latent_cache)


def layer_block(
    queries,
    latent_cache,
    cache_length,
    residual,
    norm_gain,
    value_up,
    out_weight,
    gate_weight,
    up_weight,
    down_weight,
    expert_index,
    gate_level,
):
    group_size = lax.axis_size("dev")
    slabs = group_size // EXPERTS
    attending = lax.axis_index("sec") < lax.axis_size("sec") - 1
    me = lax.axis_index("dev")
    token_count = queries.shape[0]
    latent_width = value_up.shape[1]
    score_scale = (value_up.shape[2] + queries.shape[2] - latent_width) ** (-0.5)
    width = residual.shape[1]
    part = width // CHUNKS

    latent_out = attend(
        queries, latent_cache, cache_length, me, group_size, latent_width, score_scale
    )
    arrived = [latent_out[0]] + [None] * (group_size - 1)
    for by in reversed(range(1, group_size)):
        arrived[by] = swap(latent_out[by], by)
    by_heads = jnp.stack(arrived, axis=0).reshape(
        group_size * token_count, value_up.shape[0], latent_width
    )
    head_out = jnp.einsum(
        "thc,hcv->thv", by_heads, value_up, preferred_element_type=jnp.float32
    ).astype(jnp.bfloat16)
    head_flat = head_out.reshape(head_out.shape[0], -1)
    product = jnp.dot(head_flat, out_weight, preferred_element_type=jnp.float32)
    product = product.astype(jnp.bfloat16).reshape(EXPERTS, slabs, token_count, width)
    attended = [
        sum_scatter(product[..., i * part : (i + 1) * part], slabs) for i in range(CHUNKS)
    ]
    attended = jnp.concatenate(attended, axis=1)
    stream = (residual.astype(jnp.float32) + attended).astype(jnp.bfloat16)
    stream_float = stream.astype(jnp.float32)
    mean_square = jnp.mean(stream_float * stream_float, axis=1, keepdims=True)
    normed = (stream_float * lax.rsqrt(mean_square + 1e-06) * norm_gain).astype(jnp.bfloat16)

    levels = gate_level.astype(jnp.float32)
    mix = levels / jnp.sum(levels, axis=1, keepdims=True)
    lane = lax.broadcasted_iota(jnp.int32, (1, 1, LANES), 2)
    mix_of = jnp.sum(
        jnp.where(expert_index[:, :, None] == lane % EXPERTS, mix[:, :, None], 0.0), axis=1
    )
    high = lax.reduce_precision(mix_of, 8, 7)
    mix_row = jnp.where(lane[0] < EXPERTS, high, mix_of - high).astype(jnp.bfloat16)

    rows = []
    for i in range(CHUNKS):
        piece = normed[:, i * part : (i + 1) * part]
        if i == CHUNKS - 1:
            piece = jnp.concatenate([piece, mix_row], axis=1)
        rows.append(gather_rows(piece, slabs).reshape(group_size * token_count, -1))
    mix_rows = rows[-1][:, part:].astype(jnp.float32)
    rows[-1] = rows[-1][:, :part]
    rows = jnp.concatenate(rows, axis=1)
    mine = me // slabs
    mix_mine = jnp.sum(
        jnp.where((lane[0] < 2 * EXPERTS) & (lane[0] % EXPERTS == mine), mix_rows, 0.0),
        axis=1,
        keepdims=True,
    )

    gate_hidden = jnp.dot(rows, gate_weight, preferred_element_type=jnp.float32)
    up_hidden = jnp.dot(rows, up_weight, preferred_element_type=jnp.float32)
    activated = (jax.nn.silu(gate_hidden) * up_hidden).astype(jnp.bfloat16)
    product = jnp.dot(activated, down_weight, preferred_element_type=jnp.float32) * mix_mine
    product = product.astype(jnp.bfloat16).reshape(EXPERTS, slabs, token_count, width)
    moe = [sum_scatter(product[..., i * part : (i + 1) * part], slabs) for i in range(CHUNKS)]
    moe = jnp.concatenate(moe, axis=1)
    result = (stream_float + moe).astype(jnp.bfloat16)
    return jnp.where(attending, result, jnp.zeros_like(result))


def solution(mesh):
    placed = (
        P(("sec", "dev"), None, None),
        P(("sec", "dev"), None, None),
        P(("sec", "dev")),
        P(("sec", "dev"), None),
        P(),
        P("dev", None, None),
        P("dev", None),
        P(None, "dev"),
        P(None, "dev"),
        P("dev", None),
        P(("sec", "dev"), None),
        P(("sec", "dev"), None),
    )
    return jax.shard_map(
        layer_block,
        mesh=mesh,
        in_specs=placed,
        out_specs=P(("sec", "dev"), None),
        check_vma=False,
    )
```

time: 130 us -> 142 us (1.092)
  matrix products: 41.8 us -> 25.8 us
  local copies, waits for them, and re-layouts: 4.66 us -> 18.5 us
  Pallas kernels: 0 us -> 7.13 us
  starting transfers between devices: 41.6 us -> 48.1 us
  waiting for transfers between devices: 38.2 us -> 40.1 us
    unnamed x20 -> x33, local copies, waits for them, and re-layouts: 0.87 us -> 18.3 us
    ppermute x24 -> x31, waiting for transfers between devices: 24 us -> 40.1 us  [swap(): return lax.ppermute(x, 'dev', [(i, i ^ by) for i in range(size)])]
    all_to_all x1 -> x0, waiting for transfers between devices: 14.2 us -> none  [layer_block(): lax.all_to_all(latent_out, 'dev', split_axis=1, concat_axis=0, tiled=True)]
    ppermute x24 -> x31, starting transfers between devices: 34.3 us -> 48.1 us  [swap(): return lax.ppermute(x, 'dev', [(i, i ^ by) for i in range(size)])]
    all_to_all x1 -> x0, starting transfers between devices: 7.28 us -> none  [layer_block(): lax.all_to_all(latent_out, 'dev', split_axis=1, concat_axis=0, tiled=True)]
    pallas_call x0 -> x1, Pallas kernels: none -> 7.13 us  [attend(): pl.pallas_call(functools.partial(attend_kernel, scale, groups), out_shape...]
    sub x1 -> x0, matrix products: 6.22 us -> none  [layer_block(): expos = jnp.where(usable, jnp.exp(masked - highest), 0.0)]
    dot_general x1, matrix products: 7.98 us -> 2.73 us  [layer_block(): gate_hidden = jnp.dot(rows, gate_weight, preferred_element_type=jnp.float32)]
  transfers between devices with their start and end apart: 25 -> 31, of which waited for: 11 -> 15; matrix products, arithmetic and copies ran while one was open for 1% -> 0% of each run, Pallas kernels for 0% -> 0%
where the time goes in v2:
time: 142 us
  starting transfers between devices  48.1 us (34%)
  waiting for transfers between devices  40.1 us (28%)
  matrix products  25.8 us (18%)
  local copies, waits for them, and re-layouts  18.5 us (13%)
  Pallas kernels  7.13 us (5%)
  other arithmetic  1.71 us (1%)
    ppermute x31, starting transfers between devices, swap(): return lax.ppermute(x, 'dev', [(i, i ^ by) for i in range(size)])  48.1 us
    ppermute x31, waiting for transfers between devices, swap(): return lax.ppermute(x, 'dev', [(i, i ^ by) for i in range(size)])  40.1 us
    unnamed x33, local copies, waits for them, and re-layouts  18.3 us
    dot_general x1, matrix products, layer_block(): jnp.dot(activated, down_weight, preferred_element_type=jnp.float32)  14.6 us
    dot_general x1, matrix products, layer_block(): product = jnp.dot(head_flat, out_weight, preferred_element_type=jnp.float32)  8.11 us
    pallas_call x1, Pallas kernels, attend(): pl.pallas_call(functools.partial(attend_kernel, scale, groups), out_shape...  7.13 us
  transfers between devices with their start and end apart: 31, of which 15 were waited for; matrix products, arithmetic and copies ran while one was open for 0% of the time, Pallas kernels for 0%

profile of v2, /device:TPU:0, one launch (start us, length us, event | category | flops | bytes accessed | tf_op | source)
XLA Modules:
  0.0 141.8 jit_solution(14500218637585087119)
XLA Ops:
  0.0 14.2 %copy.23.cache_ref = bf16[8,1024,576]{2,1,0:T(8,128)(2,1)} copy(bf16[8,1024,576]{1,2,0:T(8,128)(2,1)} %param.13) | data formatting | bytes 18874368 | tf_op args[1]
  14.3 4.0 %copy-done.2 = bf16[8,1024,576]{2,1,0:T(8,128)(2,1)S(1)} copy-done((bf16[8,1024,576]{2,1,0:T(8,128)(2,1)S(1)}, bf16[8,1024,576]{2,1,0:T(8,128)(2,1)}, u32[]{:S(2)}) %copy-start.2) | copy-done | bytes 9437208
  18.2 7.1 %shard_map.118 = bf16[8,64,512]{2,1,0:T(8,128)(2,1)S(1)} custom-call(s32[1]{0:T(128)} %bitcast.place_ref, s32[8]{0:T(128)S(1)} %copy-done.4, bf16[8,64,576]{2,1,0:T(8,128)(2,1)S(1)} %copy-done.3, bf16[8,1024,576]{2,1,0:T(8,128)(2,1)S(1)} %copy-done.2), custom_call_target="tpu_custom_call" | custom-call | flops 1140850688 | bytes 9437184 | tf_op jit(solution)/shard_map/pallas_call | solution.py:80
  25.4 3.0 %collective-permute-start = (bf16[64,512]{1,0:T(8,128)(2,1)S(1)}, bf16[64,512]{1,0:T(8,128)(2,1)S(1)}, u32[]{:S(2)}, u32[]{:S(2)}) collective-permute-start(bf16[64,512]{1,0:T(8,128)(2,1)S(1)} %get-tuple-element.21), channel_id=1, source_target_pairs={{0,1},{1,0},{2,3},{3,2},{4,5},{5,4},{6,7},{7,6},{8,9},{9,8},{10,11... | collective-permute-start | bytes 196616 | tf_op jit(solution)/shard_map/ppermute | solution.py:17
  28.5 1.6 %collective-permute-start.1 = (bf16[64,512]{1,0:T(8,128)(2,1)S(1)}, bf16[64,512]{1,0:T(8,128)(2,1)S(1)}, u32[]{:S(2)}, u32[]{:S(2)}) collective-permute-start(bf16[64,512]{1,0:T(8,128)(2,1)S(1)} %get-tuple-element.20), channel_id=1, source_target_pairs={{0,2},{1,3},{2,0},{3,1},{4,6},{5,7},{6,4},{7,5},{8,10},{9,11},{10,... | collective-permute-start | bytes 196616 | tf_op jit(solution)/shard_map/ppermute | solution.py:17
  30.1 3.0 %collective-permute-start.3 = (bf16[64,512]{1,0:T(8,128)(2,1)S(1)}, bf16[64,512]{1,0:T(8,128)(2,1)S(1)}, u32[]{:S(2)}, u32[]{:S(2)}) collective-permute-start(bf16[64,512]{1,0:T(8,128)(2,1)S(1)} %get-tuple-element.18), channel_id=1, source_target_pairs={{0,4},{1,5},{2,6},{3,7},{4,0},{5,1},{6,2},{7,3},{8,12},{9,13},{10,... | collective-permute-start | bytes 196616 | tf_op jit(solution)/shard_map/ppermute | solution.py:17
  34.5 3.7 %collective-permute-start.5 = (bf16[64,512]{1,0:T(8,128)(2,1)S(1)}, bf16[64,512]{1,0:T(8,128)(2,1)S(1)}, u32[]{:S(2)}, u32[]{:S(2)}) collective-permute-start(bf16[64,512]{1,0:T(8,128)(2,1)S(1)} %get-tuple-element.16), channel_id=1, source_target_pairs={{0,6},{1,7},{2,4},{3,5},{4,2},{5,3},{6,0},{7,1},{8,14},{9,15},{10,... | collective-permute-start | bytes 196616 | tf_op jit(solution)/shard_map/ppermute | solution.py:17
  38.3 5.0 %collective-permute-done.4 = bf16[64,512]{1,0:T(8,128)(2,1)S(1)} collective-permute-done((bf16[64,512]{1,0:T(8,128)(2,1)S(1)}, bf16[64,512]{1,0:T(8,128)(2,1)S(1)}, u32[]{:S(2)}, u32[]{:S(2)}) %collective-permute-start.4) | collective-permute-done | bytes 65568 | tf_op jit(solution)/shard_map/ppermute | solution.py:17
  43.3 2.0 %collective-permute-done.6 = bf16[64,512]{1,0:T(8,128)(2,1)S(1)} collective-permute-done((bf16[64,512]{1,0:T(8,128)(2,1)S(1)}, bf16[64,512]{1,0:T(8,128)(2,1)S(1)}, u32[]{:S(2)}, u32[]{:S(2)}) %collective-permute-start.6) | collective-permute-done | bytes 65568 | tf_op jit(solution)/shard_map/ppermute | solution.py:17
  45.7 8.1 %convolution_convert_fusion = bf16[64,7168]{1,0:T(8,128)(2,1)S(1)} fusion(bf16[1024,7168]{1,0:T(8,128)(2,1)} %param.18, bf16[8,8,8,128]{3,2,1,0:T(8,128)(2,1)S(1)} %fusion.2), kind=kOutput, calls=%fused_computation.2 | convolution fusion | flops 939982848 | bytes 15728640 | tf_op jit(solution)/shard_map/dot_general | solution.py:140
  56.0 4.9 %collective-permute-done.11 = bf16[4,1,8,3584]{3,2,1,0:T(8,128)(2,1)S(1)} collective-permute-done((bf16[4,1,8,3584]{3,2,1,0:T(8,128)(2,1)S(1)}, bf16[4,1,8,3584]{3,2,1,0:T(8,128)(2,1)S(1)}, u32[]{:S(2)}, u32[]{:S(2)}) %collective-permute-start.11) | collective-permute-done | bytes 229408 | tf_op jit(solution)/shard_map/ppermute | solution.py:17
  60.9 2.5 %collective-permute-done.7 = bf16[4,1,8,3584]{3,2,1,0:T(8,128)(2,1)S(1)} collective-permute-done((bf16[4,1,8,3584]{3,2,1,0:T(8,128)(2,1)S(1)}, bf16[4,1,8,3584]{3,2,1,0:T(8,128)(2,1)S(1)}, u32[]{:S(2)}, u32[]{:S(2)}) %collective-permute-start.7) | collective-permute-done | bytes 229408 | tf_op jit(solution)/shard_map/ppermute | solution.py:17
  63.5 3.9 %collective-permute-start.10 = (bf16[8,3584]{1,0:T(8,128)(2,1)S(1)}, bf16[8,3584]{1,0:T(8,128)(2,1)S(1)}, u32[]{:S(2)}, u32[]{:S(2)}) collective-permute-start(bf16[8,3584]{1,0:T(8,128)(2,1)S(1)} %get-tuple-element.30), channel_id=1, source_target_pairs={{0,2},{1,3},{2,0},{3,1},{4,6},{5,7},{6,4},{7,5},{8,10},{9,11},{10,... | collective-permute-start | bytes 172040 | tf_op jit(solution)/shard_map/ppermute | solution.py:17
  67.4 2.6 %collective-permute-start.8 = (bf16[8,3584]{1,0:T(8,128)(2,1)S(1)}, bf16[8,3584]{1,0:T(8,128)(2,1)S(1)}, u32[]{:S(2)}, u32[]{:S(2)}) collective-permute-start(bf16[8,3584]{1,0:T(8,128)(2,1)S(1)} %get-tuple-element.29), channel_id=1, source_target_pairs={{0,6},{1,7},{2,4},{3,5},{4,2},{5,3},{6,0},{7,1},{8,14},{9,15},{10,... | collective-permute-start | bytes 172040 | tf_op jit(solution)/shard_map/ppermute | solution.py:17
  70.0 1.6 %collective-permute-start.12 = (bf16[8,3584]{1,0:T(8,128)(2,1)S(1)}, bf16[8,3584]{1,0:T(8,128)(2,1)S(1)}, u32[]{:S(2)}, u32[]{:S(2)}) collective-permute-start(bf16[8,3584]{1,0:T(8,128)(2,1)S(1)} %get-tuple-element.32), channel_id=1, source_target_pairs={{0,6},{1,7},{2,4},{3,5},{4,2},{5,3},{6,0},{7,1},{8,14},{9,15},{10,... | collective-permute-start | bytes 172040 | tf_op jit(solution)/shard_map/ppermute | solution.py:17
  71.6 1.7 %collective-permute-start.13 = (bf16[8,3584]{1,0:T(8,128)(2,1)S(1)}, bf16[8,3584]{1,0:T(8,128)(2,1)S(1)}, u32[]{:S(2)}, u32[]{:S(2)}) collective-permute-start(bf16[8,3584]{1,0:T(8,128)(2,1)S(1)} %get-tuple-element.34), channel_id=1, source_target_pairs={{0,4},{1,5},{2,6},{3,7},{4,0},{5,1},{6,2},{7,3},{8,12},{9,13},{10,... | collective-permute-start | bytes 172040 | tf_op jit(solution)/shard_map/ppermute | solution.py:17
  74.5 2.5 %collective-permute-done.9 = bf16[8,3584]{1,0:T(8,128)(2,1)S(1)} collective-permute-done((bf16[8,3584]{1,0:T(8,128)(2,1)S(1)}, bf16[8,3584]{1,0:T(8,128)(2,1)S(1)}, u32[]{:S(2)}, u32[]{:S(2)}) %collective-permute-start.9) | collective-permute-done | bytes 57376 | tf_op jit(solution)/shard_map/ppermute | solution.py:17
  77.1 2.2 %collective-permute-done.13 = bf16[8,3584]{1,0:T(8,128)(2,1)S(1)} collective-permute-done((bf16[8,3584]{1,0:T(8,128)(2,1)S(1)}, bf16[8,3584]{1,0:T(8,128)(2,1)S(1)}, u32[]{:S(2)}, u32[]{:S(2)}) %collective-permute-start.13) | collective-permute-done | bytes 57376 | tf_op jit(solution)/shard_map/ppermute | solution.py:17
  79.7 3.2 %collective-permute-start.16 = (bf16[8,3584]{1,0:T(8,128)(2,1)S(1)}, bf16[8,3584]{1,0:T(8,128)(2,1)S(1)}, u32[]{:S(2)}, u32[]{:S(2)}) collective-permute-start(bf16[8,3584]{1,0:T(8,128)(2,1)S(1)} %get-tuple-element.37), channel_id=1, source_target_pairs={{0,4},{1,5},{2,6},{3,7},{4,0},{5,1},{6,2},{7,3},{8,12},{9,13},{10,... | collective-permute-start | bytes 172040 | tf_op jit(solution)/shard_map/ppermute | solution.py:17
  84.1 3.2 %collective-permute-start.20 = (bf16[8,3712]{1,0:T(8,128)(2,1)S(1)}, bf16[8,3712]{1,0:T(8,128)(2,1)S(1)}, u32[]{:S(2)}, u32[]{:S(2)}) collective-permute-start(bf16[8,3712]{1,0:T(8,128)(2,1)S(1)} %get-tuple-element.39), channel_id=1, source_target_pairs={{0,4},{1,5},{2,6},{3,7},{4,0},{5,1},{6,2},{7,3},{8,12},{9,13},{10,... | collective-permute-start | bytes 178184 | tf_op jit(solution)/shard_map/ppermute | solution.py:17
  90.0 1.9 %collective-permute-done.20 = bf16[8,3712]{1,0:T(8,128)(2,1)S(1)} collective-permute-done((bf16[8,3712]{1,0:T(8,128)(2,1)S(1)}, bf16[8,3712]{1,0:T(8,128)(2,1)S(1)}, u32[]{:S(2)}, u32[]{:S(2)}) %collective-permute-start.20) | collective-permute-done | bytes 59424 | tf_op jit(solution)/shard_map/ppermute | solution.py:17
  94.2 3.2 %collective-permute-done.18 = bf16[4,1,8,3584]{3,2,1,0:T(8,128)(2,1)S(1)} collective-permute-done((bf16[4,1,8,3584]{3,2,1,0:T(8,128)(2,1)S(1)}, bf16[4,1,8,3584]{3,2,1,0:T(8,128)(2,1)S(1)}, u32[]{:S(2)}, u32[]{:S(2)}) %collective-permute-start.18) | collective-permute-done | bytes 229408 | tf_op jit(solution)/shard_map/ppermute | solution.py:17
  97.4 2.7 %collective-permute-done.22 = bf16[4,1,8,3712]{3,2,0,1:T(8,128)(2,1)S(1)} collective-permute-done((bf16[4,1,8,3712]{3,2,0,1:T(8,128)(2,1)S(1)}, bf16[4,1,8,3712]{3,2,0,1:T(8,128)(2,1)S(1)}, u32[]{:S(2)}, u32[]{:S(2)}) %collective-permute-start.22) | collective-permute-done | bytes 237600 | tf_op jit(solution)/shard_map/ppermute | solution.py:17
  100.5 2.7 %fusion.3 = f32[64,1024]{1,0:T(8,128)S(1)} fusion(bf16[7168,1024]{1,0:T(8,128)(2,1)S(1)} %bitcast.104, bf16[64,3584]{1,0:T(8,128)(2,1)S(1)} %slice.178, bf16[64,3584]{1,0:T(8,128)(2,1)S(1)} %bitcast.105), kind=kOutput, calls=%fused_computation.8 | convolution fusion | flops 941359104 | bytes 15859712 | tf_op jit(solution)/shard_map/dot_general | solution.py:176
  103.2 14.6 %fusion = bf16[64,7168]{1,0:T(8,128)(2,1)S(1)} fusion(bf16[1024,7168]{1,0:T(8,128)(2,1)} %param.21, f32[64]{0:T(128)S(1)} %select_reduce_fusion, bf16[7168,1024]{1,0:T(8,128)(2,1)} %param.20, bf16[64,3584]{1,0:T(8,128)(2,1)S(1)} %slice.178, bf16[64,3584]{1,0:T(8,128)(2,1)S(1)} %bitcast.106, f32[64,1024]{1,0:T(8,128)S(1)} %fusion.3), kind=kOutput, calls=%fused_computation.1 | convolution fusion | flops 1882193920 | bytes 31457536 | tf_op jit(solution)/shard_map/dot_general | solution.py:179
  119.9 5.7 %collective-permute-done.23 = bf16[4,1,8,3584]{3,2,1,0:T(8,128)(2,1)S(1)} collective-permute-done((bf16[4,1,8,3584]{3,2,1,0:T(8,128)(2,1)S(1)}, bf16[4,1,8,3584]{3,2,1,0:T(8,128)(2,1)S(1)}, u32[]{:S(2)}, u32[]{:S(2)}) %collective-permute-start.23) | collective-permute-done | bytes 229408 | tf_op jit(solution)/shard_map/ppermute | solution.py:17
  125.7 2.5 %collective-permute-done.27 = bf16[4,1,8,3584]{3,2,1,0:T(8,128)(2,1)S(1)} collective-permute-done((bf16[4,1,8,3584]{3,2,1,0:T(8,128)(2,1)S(1)}, bf16[4,1,8,3584]{3,2,1,0:T(8,128)(2,1)S(1)}, u32[]{:S(2)}, u32[]{:S(2)}) %collective-permute-start.27) | collective-permute-done | bytes 229408 | tf_op jit(solution)/shard_map/ppermute | solution.py:17
  128.3 1.6 %collective-permute-start.24 = (bf16[8,3584]{1,0:T(8,128)(2,1)S(1)}, bf16[8,3584]{1,0:T(8,128)(2,1)S(1)}, u32[]{:S(2)}, u32[]{:S(2)}) collective-permute-start(bf16[8,3584]{1,0:T(8,128)(2,1)S(1)} %get-tuple-element.23), channel_id=1, source_target_pairs={{0,6},{1,7},{2,4},{3,5},{4,2},{5,3},{6,0},{7,1},{8,14},{9,15},{10,... | collective-permute-start | bytes 172040 | tf_op jit(solution)/shard_map/ppermute | solution.py:17
  129.9 2.3 %collective-permute-start.25 = (bf16[8,3584]{1,0:T(8,128)(2,1)S(1)}, bf16[8,3584]{1,0:T(8,128)(2,1)S(1)}, u32[]{:S(2)}, u32[]{:S(2)}) collective-permute-start(bf16[8,3584]{1,0:T(8,128)(2,1)S(1)} %get-tuple-element.25), channel_id=1, source_target_pairs={{0,4},{1,5},{2,6},{3,7},{4,0},{5,1},{6,2},{7,3},{8,12},{9,13},{10,... | collective-permute-start | bytes 172040 | tf_op jit(solution)/shard_map/ppermute | solution.py:17
  132.7 1.6 %collective-permute-start.28 = (bf16[8,3584]{1,0:T(8,128)(2,1)S(1)}, bf16[8,3584]{1,0:T(8,128)(2,1)S(1)}, u32[]{:S(2)}, u32[]{:S(2)}) collective-permute-start(bf16[8,3584]{1,0:T(8,128)(2,1)S(1)} %get-tuple-element.26), channel_id=1, source_target_pairs={{0,6},{1,7},{2,4},{3,5},{4,2},{5,3},{6,0},{7,1},{8,14},{9,15},{10,... | collective-permute-start | bytes 172040 | tf_op jit(solution)/shard_map/ppermute | solution.py:17
  135.8 2.2 %collective-permute-start.30 = (bf16[8,3584]{1,0:T(8,128)(2,1)S(1)}, bf16[8,3584]{1,0:T(8,128)(2,1)S(1)}, u32[]{:S(2)}, u32[]{:S(2)}) collective-permute-start(bf16[8,3584]{1,0:T(8,128)(2,1)S(1)} %get-tuple-element.27), channel_id=1, source_target_pairs={{0,2},{1,3},{2,0},{3,1},{4,6},{5,7},{6,4},{7,5},{8,10},{9,11},{10,... | collective-permute-start | bytes 172040 | tf_op jit(solution)/shard_map/ppermute | solution.py:17
  137.9 2.0 %collective-permute-done.25 = bf16[8,3584]{1,0:T(8,128)(2,1)S(1)} collective-permute-done((bf16[8,3584]{1,0:T(8,128)(2,1)S(1)}, bf16[8,3584]{1,0:T(8,128)(2,1)S(1)}, u32[]{:S(2)}, u32[]{:S(2)}) %collective-permute-start.25) | collective-permute-done | bytes 57376 | tf_op jit(solution)/shard_map/ppermute | solution.py:17
  (103 shorter events, 18.4 us)
Async XLA Ops:
  25.4 9.0 %collective-permute-start = (bf16[64,512]{1,0:T(8,128)(2,1)S(1)}, bf16[64,512]{1,0:T(8,128)(2,1)S(1)}, u32[]{:S(2)}, u32[]{:S(2)}) collective-permute-start(bf16[64,512]{1,0:T(8,128)(2,1)S(1)} %get-tuple-element.21), channel_id=1, source_target_pairs={{0,1},{1,0},{2,3},{3,2},{4,5},{5,4},{6,7},{7,6},{8,9},{9,8},{10,11... | collective-permute-start | bytes 196616 | tf_op jit(solution)/shard_map/ppermute | solution.py:17
  28.5 9.7 %collective-permute-start.1 = (bf16[64,512]{1,0:T(8,128)(2,1)S(1)}, bf16[64,512]{1,0:T(8,128)(2,1)S(1)}, u32[]{:S(2)}, u32[]{:S(2)}) collective-permute-start(bf16[64,512]{1,0:T(8,128)(2,1)S(1)} %get-tuple-element.20), channel_id=1, source_target_pairs={{0,2},{1,3},{2,0},{3,1},{4,6},{5,7},{6,4},{7,5},{8,10},{9,11},{10,... | collective-permute-start | bytes 196616 | tf_op jit(solution)/shard_map/ppermute | solution.py:17
  30.1 8.2 %collective-permute-start.2 = (bf16[64,512]{1,0:T(8,128)(2,1)S(1)}, bf16[64,512]{1,0:T(8,128)(2,1)S(1)}, u32[]{:S(2)}, u32[]{:S(2)}) collective-permute-start(bf16[64,512]{1,0:T(8,128)(2,1)S(1)} %get-tuple-element.19), channel_id=1, source_target_pairs={{0,3},{1,2},{2,1},{3,0},{4,7},{5,6},{6,5},{7,4},{8,11},{9,10},{10,... | collective-permute-start | bytes 196616 | tf_op jit(solution)/shard_map/ppermute | solution.py:17
  30.1 8.2 %collective-permute-start.3 = (bf16[64,512]{1,0:T(8,128)(2,1)S(1)}, bf16[64,512]{1,0:T(8,128)(2,1)S(1)}, u32[]{:S(2)}, u32[]{:S(2)}) collective-permute-start(bf16[64,512]{1,0:T(8,128)(2,1)S(1)} %get-tuple-element.18), channel_id=1, source_target_pairs={{0,4},{1,5},{2,6},{3,7},{4,0},{5,1},{6,2},{7,3},{8,12},{9,13},{10,... | collective-permute-start | bytes 196616 | tf_op jit(solution)/shard_map/ppermute | solution.py:17
  33.0 10.2 %collective-permute-start.4 = (bf16[64,512]{1,0:T(8,128)(2,1)S(1)}, bf16[64,512]{1,0:T(8,128)(2,1)S(1)}, u32[]{:S(2)}, u32[]{:S(2)}) collective-permute-start(bf16[64,512]{1,0:T(8,128)(2,1)S(1)} %get-tuple-element.17), channel_id=1, source_target_pairs={{0,5},{1,4},{2,7},{3,6},{4,1},{5,0},{6,3},{7,2},{8,13},{9,12},{10,... | collective-permute-start | bytes 196616 | tf_op jit(solution)/shard_map/ppermute | solution.py:17
  34.5 8.8 %collective-permute-start.5 = (bf16[64,512]{1,0:T(8,128)(2,1)S(1)}, bf16[64,512]{1,0:T(8,128)(2,1)S(1)}, u32[]{:S(2)}, u32[]{:S(2)}) collective-permute-start(bf16[64,512]{1,0:T(8,128)(2,1)S(1)} %get-tuple-element.16), channel_id=1, source_target_pairs={{0,6},{1,7},{2,4},{3,5},{4,2},{5,3},{6,0},{7,1},{8,14},{9,15},{10,... | collective-permute-start | bytes 196616 | tf_op jit(solution)/shard_map/ppermute | solution.py:17
  38.2 7.1 %collective-permute-start.6 = (bf16[64,512]{1,0:T(8,128)(2,1)S(1)}, bf16[64,512]{1,0:T(8,128)(2,1)S(1)}, u32[]{:S(2)}, u32[]{:S(2)}) collective-permute-start(bf16[64,512]{1,0:T(8,128)(2,1)S(1)} %get-tuple-element.15), channel_id=1, source_target_pairs={{0,7},{1,6},{2,5},{3,4},{4,3},{5,2},{6,1},{7,0},{8,15},{9,14},{10,... | collective-permute-start | bytes 196616 | tf_op jit(solution)/shard_map/ppermute | solution.py:17
  45.3 55.1 %slice-start = ((s8[14680064]{0:T(1024)(128)(4,1)}), s8[4194304]{0:T(1024)(128)(4,1)S(1)}, s32[]{:S(2)}) async-start(s8[14680064]{0:T(1024)(128)(4,1)} %bitcast.103), calls=%async_computation | async-start | bytes 8388608
  53.9 7.0 %collective-permute-start.11 = (bf16[4,1,8,3584]{3,2,1,0:T(8,128)(2,1)S(1)}, bf16[4,1,8,3584]{3,2,1,0:T(8,128)(2,1)S(1)}, u32[]{:S(2)}, u32[]{:S(2)}) collective-permute-start(bf16[4,1,8,3584]{3,2,1,0:T(8,128)(2,1)S(1)} %get-tuple-element.14), channel_id=1, source_target_pairs={{0,1},{1,0},{2,3},{3,2},{4,5},{5,4},{6,7},{7,6},{8,9},{9,8},{10,11... | collective-permute-start | bytes 688136 | tf_op jit(solution)/shard_map/ppermute | solution.py:17
  54.4 8.9 %collective-permute-start.7 = (bf16[4,1,8,3584]{3,2,1,0:T(8,128)(2,1)S(1)}, bf16[4,1,8,3584]{3,2,1,0:T(8,128)(2,1)S(1)}, u32[]{:S(2)}, u32[]{:S(2)}) collective-permute-start(bf16[4,1,8,3584]{3,2,1,0:T(8,128)(2,1)S(1)} %get-tuple-element.13), channel_id=1, source_target_pairs={{0,1},{1,0},{2,3},{3,2},{4,5},{5,4},{6,7},{7,6},{8,9},{9,8},{10,11... | collective-permute-start | bytes 688136 | tf_op jit(solution)/shard_map/ppermute | solution.py:17
  63.5 9.8 %collective-permute-start.10 = (bf16[8,3584]{1,0:T(8,128)(2,1)S(1)}, bf16[8,3584]{1,0:T(8,128)(2,1)S(1)}, u32[]{:S(2)}, u32[]{:S(2)}) collective-permute-start(bf16[8,3584]{1,0:T(8,128)(2,1)S(1)} %get-tuple-element.30), channel_id=1, source_target_pairs={{0,2},{1,3},{2,0},{3,1},{4,6},{5,7},{6,4},{7,5},{8,10},{9,11},{10,... | collective-permute-start | bytes 172040 | tf_op jit(solution)/shard_map/ppermute | solution.py:17
  67.4 7.1 %collective-permute-start.8 = (bf16[8,3584]{1,0:T(8,128)(2,1)S(1)}, bf16[8,3584]{1,0:T(8,128)(2,1)S(1)}, u32[]{:S(2)}, u32[]{:S(2)}) collective-permute-start(bf16[8,3584]{1,0:T(8,128)(2,1)S(1)} %get-tuple-element.29), channel_id=1, source_target_pairs={{0,6},{1,7},{2,4},{3,5},{4,2},{5,3},{6,0},{7,1},{8,14},{9,15},{10,... | collective-permute-start | bytes 172040 | tf_op jit(solution)/shard_map/ppermute | solution.py:17
  70.0 7.0 %collective-permute-start.9 = (bf16[8,3584]{1,0:T(8,128)(2,1)S(1)}, bf16[8,3584]{1,0:T(8,128)(2,1)S(1)}, u32[]{:S(2)}, u32[]{:S(2)}) collective-permute-start(bf16[8,3584]{1,0:T(8,128)(2,1)S(1)} %get-tuple-element.31), channel_id=1, source_target_pairs={{0,4},{1,5},{2,6},{3,7},{4,0},{5,1},{6,2},{7,3},{8,12},{9,13},{10,... | collective-permute-start | bytes 172040 | tf_op jit(solution)/shard_map/ppermute | solution.py:17
  70.0 7.0 %collective-permute-start.12 = (bf16[8,3584]{1,0:T(8,128)(2,1)S(1)}, bf16[8,3584]{1,0:T(8,128)(2,1)S(1)}, u32[]{:S(2)}, u32[]{:S(2)}) collective-permute-start(bf16[8,3584]{1,0:T(8,128)(2,1)S(1)} %get-tuple-element.32), channel_id=1, source_target_pairs={{0,6},{1,7},{2,4},{3,5},{4,2},{5,3},{6,0},{7,1},{8,14},{9,15},{10,... | collective-permute-start | bytes 172040 | tf_op jit(solution)/shard_map/ppermute | solution.py:17
  71.6 7.6 %collective-permute-start.13 = (bf16[8,3584]{1,0:T(8,128)(2,1)S(1)}, bf16[8,3584]{1,0:T(8,128)(2,1)S(1)}, u32[]{:S(2)}, u32[]{:S(2)}) collective-permute-start(bf16[8,3584]{1,0:T(8,128)(2,1)S(1)} %get-tuple-element.34), channel_id=1, source_target_pairs={{0,4},{1,5},{2,6},{3,7},{4,0},{5,1},{6,2},{7,3},{8,12},{9,13},{10,... | collective-permute-start | bytes 172040 | tf_op jit(solution)/shard_map/ppermute | solution.py:17
  73.3 5.9 %collective-permute-start.14 = (bf16[8,3584]{1,0:T(8,128)(2,1)S(1)}, bf16[8,3584]{1,0:T(8,128)(2,1)S(1)}, u32[]{:S(2)}, u32[]{:S(2)}) collective-permute-start(bf16[8,3584]{1,0:T(8,128)(2,1)S(1)} %get-tuple-element.33), channel_id=1, source_target_pairs={{0,2},{1,3},{2,0},{3,1},{4,6},{5,7},{6,4},{7,5},{8,10},{9,11},{10,... | collective-permute-start | bytes 172040 | tf_op jit(solution)/shard_map/ppermute | solution.py:17
  79.6 7.7 %collective-permute-start.15 = (bf16[8,3584]{1,0:T(8,128)(2,1)S(1)}, bf16[8,3584]{1,0:T(8,128)(2,1)S(1)}, u32[]{:S(2)}, u32[]{:S(2)}) collective-permute-start(bf16[8,3584]{1,0:T(8,128)(2,1)S(1)} %get-tuple-element.37), channel_id=1, source_target_pairs={{0,2},{1,3},{2,0},{3,1},{4,6},{5,7},{6,4},{7,5},{8,10},{9,11},{10,... | collective-permute-start | bytes 172040 | tf_op jit(solution)/shard_map/ppermute | solution.py:17
  79.7 8.8 %collective-permute-start.16 = (bf16[8,3584]{1,0:T(8,128)(2,1)S(1)}, bf16[8,3584]{1,0:T(8,128)(2,1)S(1)}, u32[]{:S(2)}, u32[]{:S(2)}) collective-permute-start(bf16[8,3584]{1,0:T(8,128)(2,1)S(1)} %get-tuple-element.37), channel_id=1, source_target_pairs={{0,4},{1,5},{2,6},{3,7},{4,0},{5,1},{6,2},{7,3},{8,12},{9,13},{10,... | collective-permute-start | bytes 172040 | tf_op jit(solution)/shard_map/ppermute | solution.py:17
  82.9 6.1 %collective-permute-start.17 = (bf16[8,3584]{1,0:T(8,128)(2,1)S(1)}, bf16[8,3584]{1,0:T(8,128)(2,1)S(1)}, u32[]{:S(2)}, u32[]{:S(2)}) collective-permute-start(bf16[8,3584]{1,0:T(8,128)(2,1)S(1)} %get-tuple-element.37), channel_id=1, source_target_pairs={{0,6},{1,7},{2,4},{3,5},{4,2},{5,3},{6,0},{7,1},{8,14},{9,15},{10,... | collective-permute-start | bytes 172040 | tf_op jit(solution)/shard_map/ppermute | solution.py:17
  84.1 5.9 %collective-permute-start.19 = (bf16[8,3712]{1,0:T(8,128)(2,1)S(1)}, bf16[8,3712]{1,0:T(8,128)(2,1)S(1)}, u32[]{:S(2)}, u32[]{:S(2)}) collective-permute-start(bf16[8,3712]{1,0:T(8,128)(2,1)S(1)} %get-tuple-element.39), channel_id=1, source_target_pairs={{0,2},{1,3},{2,0},{3,1},{4,6},{5,7},{6,4},{7,5},{8,10},{9,11},{10,... | collective-permute-start | bytes 178184 | tf_op jit(solution)/shard_map/ppermute | solution.py:17
  84.1 7.7 %collective-permute-start.20 = (bf16[8,3712]{1,0:T(8,128)(2,1)S(1)}, bf16[8,3712]{1,0:T(8,128)(2,1)S(1)}, u32[]{:S(2)}, u32[]{:S(2)}) collective-permute-start(bf16[8,3712]{1,0:T(8,128)(2,1)S(1)} %get-tuple-element.39), channel_id=1, source_target_pairs={{0,4},{1,5},{2,6},{3,7},{4,0},{5,1},{6,2},{7,3},{8,12},{9,13},{10,... | collective-permute-start | bytes 178184 | tf_op jit(solution)/shard_map/ppermute | solution.py:17
  87.3 6.0 %collective-permute-start.21 = (bf16[8,3712]{1,0:T(8,128)(2,1)S(1)}, bf16[8,3712]{1,0:T(8,128)(2,1)S(1)}, u32[]{:S(2)}, u32[]{:S(2)}) collective-permute-start(bf16[8,3712]{1,0:T(8,128)(2,1)S(1)} %get-tuple-element.39), channel_id=1, source_target_pairs={{0,6},{1,7},{2,4},{3,5},{4,2},{5,3},{6,0},{7,1},{8,14},{9,15},{10,... | collective-permute-start | bytes 178184 | tf_op jit(solution)/shard_map/ppermute | solution.py:17
  89.0 8.4 %collective-permute-start.18 = (bf16[4,1,8,3584]{3,2,1,0:T(8,128)(2,1)S(1)}, bf16[4,1,8,3584]{3,2,1,0:T(8,128)(2,1)S(1)}, u32[]{:S(2)}, u32[]{:S(2)}) collective-permute-start(bf16[4,1,8,3584]{3,2,1,0:T(8,128)(2,1)S(1)} %maximum_bitcast_fusion.1), channel_id=1, source_target_pairs={{0,1},{1,0},{2,3},{3,2},{4,5},{5,4},{6,7},{7,6},{8,9},{9,8},{10,11... | collective-permute-start | bytes 688136 | tf_op jit(solution)/shard_map/ppermute | solution.py:17
  93.4 6.8 %collective-permute-start.22 = (bf16[4,1,8,3712]{3,2,0,1:T(8,128)(2,1)S(1)}, bf16[4,1,8,3712]{3,2,0,1:T(8,128)(2,1)S(1)}, u32[]{:S(2)}, u32[]{:S(2)}) collective-permute-start(bf16[4,1,8,3712]{3,2,0,1:T(8,128)(2,1)S(1)} %maximum_bitcast_fusion), channel_id=1, source_target_pairs={{0,1},{1,0},{2,3},{3,2},{4,5},{5,4},{6,7},{7,6},{8,9},{9,8},{10,11... | collective-permute-start | bytes 712712 | tf_op jit(solution)/shard_map/ppermute | solution.py:17
  117.8 7.8 %collective-permute-start.23 = (bf16[4,1,8,3584]{3,2,1,0:T(8,128)(2,1)S(1)}, bf16[4,1,8,3584]{3,2,1,0:T(8,128)(2,1)S(1)}, u32[]{:S(2)}, u32[]{:S(2)}) collective-permute-start(bf16[4,1,8,3584]{3,2,1,0:T(8,128)(2,1)S(1)} %get-tuple-element.9), channel_id=1, source_target_pairs={{0,1},{1,0},{2,3},{3,2},{4,5},{5,4},{6,7},{7,6},{8,9},{9,8},{10,11... | collective-permute-start | bytes 688136 | tf_op jit(solution)/shard_map/ppermute | solution.py:17
  118.8 9.3 %collective-permute-start.27 = (bf16[4,1,8,3584]{3,2,1,0:T(8,128)(2,1)S(1)}, bf16[4,1,8,3584]{3,2,1,0:T(8,128)(2,1)S(1)}, u32[]{:S(2)}, u32[]{:S(2)}) collective-permute-start(bf16[4,1,8,3584]{3,2,1,0:T(8,128)(2,1)S(1)} %get-tuple-element.10), channel_id=1, source_target_pairs={{0,1},{1,0},{2,3},{3,2},{4,5},{5,4},{6,7},{7,6},{8,9},{9,8},{10,11... | collective-permute-start | bytes 688136 | tf_op jit(solution)/shard_map/ppermute | solution.py:17
  128.3 7.5 %collective-permute-start.24 = (bf16[8,3584]{1,0:T(8,128)(2,1)S(1)}, bf16[8,3584]{1,0:T(8,128)(2,1)S(1)}, u32[]{:S(2)}, u32[]{:S(2)}) collective-permute-start(bf16[8,3584]{1,0:T(8,128)(2,1)S(1)} %get-tuple-element.23), channel_id=1, source_target_pairs={{0,6},{1,7},{2,4},{3,5},{4,2},{5,3},{6,0},{7,1},{8,14},{9,15},{10,... | collective-permute-start | bytes 172040 | tf_op jit(solution)/shard_map/ppermute | solution.py:17
  129.9 10.1 %collective-permute-start.25 = (bf16[8,3584]{1,0:T(8,128)(2,1)S(1)}, bf16[8,3584]{1,0:T(8,128)(2,1)S(1)}, u32[]{:S(2)}, u32[]{:S(2)}) collective-permute-start(bf16[8,3584]{1,0:T(8,128)(2,1)S(1)} %get-tuple-element.25), channel_id=1, source_target_pairs={{0,4},{1,5},{2,6},{3,7},{4,0},{5,1},{6,2},{7,3},{8,12},{9,13},{10,... | collective-permute-start | bytes 172040 | tf_op jit(solution)/shard_map/ppermute | solution.py:17
  132.2 7.7 %collective-permute-start.26 = (bf16[8,3584]{1,0:T(8,128)(2,1)S(1)}, bf16[8,3584]{1,0:T(8,128)(2,1)S(1)}, u32[]{:S(2)}, u32[]{:S(2)}) collective-permute-start(bf16[8,3584]{1,0:T(8,128)(2,1)S(1)} %get-tuple-element.24), channel_id=1, source_target_pairs={{0,2},{1,3},{2,0},{3,1},{4,6},{5,7},{6,4},{7,5},{8,10},{9,11},{10,... | collective-permute-start | bytes 172040 | tf_op jit(solution)/shard_map/ppermute | solution.py:17
  132.7 7.2 %collective-permute-start.28 = (bf16[8,3584]{1,0:T(8,128)(2,1)S(1)}, bf16[8,3584]{1,0:T(8,128)(2,1)S(1)}, u32[]{:S(2)}, u32[]{:S(2)}) collective-permute-start(bf16[8,3584]{1,0:T(8,128)(2,1)S(1)} %get-tuple-element.26), channel_id=1, source_target_pairs={{0,6},{1,7},{2,4},{3,5},{4,2},{5,3},{6,0},{7,1},{8,14},{9,15},{10,... | collective-permute-start | bytes 172040 | tf_op jit(solution)/shard_map/ppermute | solution.py:17
  134.3 6.7 %collective-permute-start.29 = (bf16[8,3584]{1,0:T(8,128)(2,1)S(1)}, bf16[8,3584]{1,0:T(8,128)(2,1)S(1)}, u32[]{:S(2)}, u32[]{:S(2)}) collective-permute-start(bf16[8,3584]{1,0:T(8,128)(2,1)S(1)} %get-tuple-element.28), channel_id=1, source_target_pairs={{0,4},{1,5},{2,6},{3,7},{4,0},{5,1},{6,2},{7,3},{8,12},{9,13},{10,... | collective-permute-start | bytes 172040 | tf_op jit(solution)/shard_map/ppermute | solution.py:17
  135.8 5.3 %collective-permute-start.30 = (bf16[8,3584]{1,0:T(8,128)(2,1)S(1)}, bf16[8,3584]{1,0:T(8,128)(2,1)S(1)}, u32[]{:S(2)}, u32[]{:S(2)}) collective-permute-start(bf16[8,3584]{1,0:T(8,128)(2,1)S(1)} %get-tuple-element.27), channel_id=1, source_target_pairs={{0,2},{1,3},{2,0},{3,1},{4,6},{5,7},{6,4},{7,5},{8,10},{9,11},{10,... | collective-permute-start | bytes 172040 | tf_op jit(solution)/shard_map/ppermute | solution.py:17
  (12 other events, 449.6 us)

commit v3 on v2

--- a/solution.py
+++ b/solution.py
@@ -41,63 +41,193 @@
     return column
 
 
-def attend_kernel(scale, groups, place_ref, length_ref, query_ref, cache_ref, out_ref):
-    step = pl.program_id(0)
-    tokens = query_ref.shape[0]
-    heads = query_ref.shape[1]
+def streamed(x):
+    return pltpu.with_memory_space_constraint(x, pltpu.HBM)
+
+
+def attend_kernel(
+    scale,
+    groups,
+    together,
+    place_ref,
+    length_ref,
+    query_hbm,
+    cache_hbm,
+    out_ref,
+    query_ref,
+    cache_ref,
+    query_sem,
+    cache_sem,
+):
+    tokens, heads, _ = query_ref.shape
     latent_width = out_ref.shape[2]
+    each = heads // groups
+    query_copy = pltpu.make_async_copy(query_hbm, query_ref, query_sem)
+    query_copy.start()
+    copies = []
+    for t in range(tokens):
+        copy = pltpu.make_async_copy(cache_hbm.at[t], cache_ref.at[t], cache_sem.at[t])
+        copy.start()
+        copies.append(copy)
+    query_copy.wait()
+
+    def scores_of(t):
+        copies[t].wait()
+        return jnp.dot(query_ref[t], cache_ref[t], preferred_element_type=jnp.float32)
+
+    scores = scores_of(0)
     found = []
     for t in range(tokens):
-        scores = lax.dot_general(
-            query_ref[t],
-            cache_ref[t],
-            (((1,), (1,)), ((), ())),
-            preferred_element_type=jnp.float32,
-        )
+        later = scores_of(t + 1) if t + 1 < tokens else None
         position = lax.broadcasted_iota(jnp.int32, scores.shape, 1)
-        usable = position < length_ref[step * tokens + t]
+        usable = position < length_ref[t]
         masked = jnp.where(usable, scores * scale, -1e30)
         highest = jnp.max(masked, axis=1, keepdims=True)
         expos = jnp.where(usable, jnp.exp(masked - highest), 0.0)
         total = jnp.sum(expos, axis=1, keepdims=True)
-        summed = jnp.dot(
+        summed = lax.dot_general(
             expos.astype(jnp.bfloat16),
-            cache_ref[t, :, :latent_width],
+            cache_ref[t, :latent_width],
+            (((1,), (1,)), ((), ())),
             preferred_element_type=jnp.float32,
         )
         found.append(summed / total)
-    each = heads // groups
-    for g in range(groups):
-        block = jnp.concatenate([one[g * each : (g + 1) * each] for one in found], axis=0)
-        out_ref[g ^ place_ref[0]] = block.astype(jnp.bfloat16)
+        if len(found) == together:
+            first = (t + 1 - together) * each
+            for g in range(groups):
+                block = jnp.concatenate([one[g * each : (g + 1) * each] for one in found], axis=0)
+                out_ref[g ^ place_ref[0], first : first + block.shape[0]] = block.astype(
+                    jnp.bfloat16
+                )
+            found = []
+        scores = later
 
 
 def attend(queries, latent_cache, cache_length, me, groups, latent_width, scale):
     token_count, heads, key_width = queries.shape
+    length = latent_cache.shape[1]
     each = heads // groups
-    together = max(2, 16 // each)
-    rows = together * each
+    together = max(1, 16 // each)
     return pl.pallas_call(
-        functools.partial(attend_kernel, scale, groups),
+        functools.partial(attend_kernel, scale, groups, together),
         out_shape=jax.ShapeDtypeStruct((groups, token_count * each, latent_width), jnp.bfloat16),
-        grid_spec=pltpu.PrefetchScalarGridSpec(
-            num_scalar_prefetch=2,
-            grid=(token_count // together,),
-            in_specs=[
-                pl.BlockSpec((together, heads, key_width), lambda i, *_: (i, 0, 0)),
-                pl.BlockSpec(
-                    (together, latent_cache.shape[1], key_width), lambda i, *_: (i, 0, 0)
-                ),
-            ],
-            out_specs=pl.BlockSpec((groups, rows, latent_width), lambda i, *_: (0, i, 0)),
+        in_specs=[pl.BlockSpec(memory_space=pltpu.SMEM)] * 2
+        + [pl.BlockSpec(memory_space=pl.ANY)] * 2,
+        out_specs=pl.BlockSpec(memory_space=pltpu.VMEM),
+        scratch_shapes=[
+            pltpu.VMEM(queries.shape, queries.dtype),
+            pltpu.VMEM((token_count, key_width, length), latent_cache.dtype),
+            pltpu.SemaphoreType.DMA,
+            pltpu.SemaphoreType.DMA((token_count,)),
+        ],
+        compiler_params=pltpu.CompilerParams(vmem_limit_bytes=20 * 1024 * 1024),
+        cost_estimate=pl.CostEstimate(
+            flops=2 * token_count * heads * length * (key_width + latent_width),
+            bytes_accessed=2 * latent_cache.size,
+            transcendentals=token_count * heads * length,
         ),
+    )(
+        me.reshape(1), cache_length, streamed(queries), streamed(jnp.swapaxes(latent_cache, 1, 2))
+    )
+
+
+DEPTH = 256
+
+
+def project_kernel(first, rows_ref, scale_ref, weight_hbm, out_ref, weight_ref, total_ref, sem):
+    depth, count = weight_ref.shape
+    copies = []
+    for i in range(depth // DEPTH):
+        part = pl.ds(i * DEPTH, DEPTH)
+        copy = pltpu.make_async_copy(
+            weight_hbm.at[part, pl.ds(first, count)], weight_ref.at[part], sem.at[i]
+        )
+        copy.start()
+        copies.append(copy)
+    for i, copy in enumerate(copies):
+        copy.wait()
+        part = pl.ds(i * DEPTH, DEPTH)
+        product = jnp.dot(
+            rows_ref[:, part], weight_ref[part, :], preferred_element_type=jnp.float32
+        )
+        if i > 0:
+            product = product + total_ref[...]
+        if i < len(copies) - 1:
+            total_ref[...] = product
+        else:
+            out_ref[...] = (product * scale_ref[...]).astype(out_ref.dtype)
+
+
+def project(rows, scale, weight, first, count):
+    depth = weight.shape[0]
+    vmem = pl.BlockSpec(memory_space=pltpu.VMEM)
+    return pl.pallas_call(
+        functools.partial(project_kernel, first),
+        out_shape=jax.ShapeDtypeStruct((rows.shape[0], count), jnp.bfloat16),
+        in_specs=[vmem, vmem, pl.BlockSpec(memory_space=pl.ANY)],
+        out_specs=vmem,
+        scratch_shapes=[
+            pltpu.VMEM((depth, count), weight.dtype),
+            pltpu.VMEM((rows.shape[0], count), jnp.float32),
+            pltpu.SemaphoreType.DMA((depth // DEPTH,)),
+        ],
+        compiler_params=pltpu.CompilerParams(vmem_limit_bytes=20 * 1024 * 1024),
+        cost_estimate=pl.CostEstimate(
+            flops=2 * rows.shape[0] * depth * count,
+            bytes_accessed=2 * depth * count,
+            transcendentals=0,
+        ),
+    )(rows, scale, streamed(weight))
+
+
+def hidden_kernel(
+    first, rows_ref, gate_hbm, up_hbm, gate_in, up_in, gate_out, up_out, gate_ref, up_ref, sem
+):
+    count = gate_ref.shape[0]
+    copies = []
+    for i in range(count // STEP):
+        for k, (source, target) in enumerate(((gate_hbm, gate_ref), (up_hbm, up_ref))):
+            copy = pltpu.make_async_copy(
+                source.at[pl.ds(first + i * STEP, STEP)],
+                target.at[pl.ds(i * STEP, STEP)],
+                sem.at[k, i],
+            )
+            copy.start()
+            copies.append(copy)
+    for i in range(count // STEP):
+        part = pl.ds(i * STEP, STEP)
+        for k, (weight, before, after) in enumerate(
+            ((gate_ref, gate_in, gate_out), (up_ref, up_in, up_out))
+        ):
+            copies[2 * i + k].wait()
+            product = jnp.dot(
+                rows_ref[:, part], weight[part, :], preferred_element_type=jnp.float32
+            )
+            after[...] = product + (before if i == 0 else after)[...]
+
+
+STEP = 512
+
+
+def hidden(rows, gate_weight, up_weight, gate, up, first, count):
+    width = gate_weight.shape[1]
+    shape = (rows.shape[0], width)
+    vmem = pl.BlockSpec(memory_space=pltpu.VMEM)
+    hbm = pl.BlockSpec(memory_space=pl.ANY)
+    return pl.pallas_call(
+        functools.partial(hidden_kernel, first),
+        out_shape=[jax.ShapeDtypeStruct(shape, jnp.float32)] * 2,
+        in_specs=[vmem, hbm, hbm, vmem, vmem],
+        out_specs=[vmem] * 2,
+        scratch_shapes=[pltpu.VMEM((count, width), gate_weight.dtype)] * 2
+        + [pltpu.SemaphoreType.DMA((2, count // STEP))],
         compiler_params=pltpu.CompilerParams(vmem_limit_bytes=24 * 1024 * 1024),
         cost_estimate=pl.CostEstimate(
-            flops=2 * token_count * heads * latent_cache.shape[1] * (key_width + latent_width),
-            bytes_accessed=2 * latent_cache.size,
-            transcendentals=token_count * heads * latent_cache.shape[1],
+            flops=4 * rows.shape[0] * width * count,
+            bytes_accessed=4 * width * count,
+            transcendentals=0,
         ),
-    )(me.reshape(1), cache_length, queries, latent_cache)
+    )(rows, streamed(gate_weight), streamed(up_weight), gate, up)
 
 
 def layer_block(
@@ -137,11 +267,11 @@
         "thc,hcv->thv", by_heads, value_up, preferred_element_type=jnp.float32
     ).astype(jnp.bfloat16)
     head_flat = head_out.reshape(head_out.shape[0], -1)
-    product = jnp.dot(head_flat, out_weight, preferred_element_type=jnp.float32)
-    product = product.astype(jnp.bfloat16).reshape(EXPERTS, slabs, token_count, width)
-    attended = [
-        sum_scatter(product[..., i * part : (i + 1) * part], slabs) for i in range(CHUNKS)
-    ]
+    ones = jnp.ones((head_flat.shape[0], 1), jnp.float32)
+    attended = []
+    for i in range(CHUNKS):
+        product = project(head_flat, ones, out_weight, i * part, part)
+        attended.append(sum_scatter(product.reshape(EXPERTS, slabs, token_count, part), slabs))
     attended = jnp.concatenate(attended, axis=1)
     stream = (residual.astype(jnp.float32) + attended).astype(jnp.bfloat16)
     stream_float = stream.astype(jnp.float32)
@@ -165,7 +295,6 @@
         rows.append(gather_rows(piece, slabs).reshape(group_size * token_count, -1))
     mix_rows = rows[-1][:, part:].astype(jnp.float32)
     rows[-1] = rows[-1][:, :part]
-    rows = jnp.concatenate(rows, axis=1)
     mine = me // slabs
     mix_mine = jnp.sum(
         jnp.where((lane[0] < 2 * EXPERTS) & (lane[0] % EXPERTS == mine), mix_rows, 0.0),
@@ -173,12 +302,14 @@
         keepdims=True,
     )
 
-    gate_hidden = jnp.dot(rows, gate_weight, preferred_element_type=jnp.float32)
-    up_hidden = jnp.dot(rows, up_weight, preferred_element_type=jnp.float32)
-    activated = (jax.nn.silu(gate_hidden) * up_hidden).astype(jnp.bfloat16)
-    product = jnp.dot(activated, down_weight, preferred_element_type=jnp.float32) * mix_mine
-    product = product.astype(jnp.bfloat16).reshape(EXPERTS, slabs, token_count, width)
-    moe = [sum_scatter(product[..., i * part : (i + 1) * part], slabs) for i in range(CHUNKS)]
+    gate = up = jnp.zeros((rows[0].shape[0], gate_weight.shape[1]), jnp.float32)
+    for i in range(CHUNKS):
+        gate, up = hidden(rows[i], gate_weight, up_weight, gate, up, i * part, part)
+    activated = (jax.nn.silu(gate) * up).astype(jnp.bfloat16)
+    moe = []
+    for i in range(CHUNKS):
+        product = project(activated, mix_mine, down_weight, i * part, part)
+        moe.append(sum_scatter(product.reshape(EXPERTS, slabs, token_count, part), slabs))
     moe = jnp.concatenate(moe, axis=1)
     result = (stream_float + moe).astype(jnp.bfloat16)
     return jnp.where(attending, result, jnp.zeros_like(result))

time: 142 us -> 113 us (0.80)
  Pallas kernels: 7.13 us -> 35.5 us
  matrix products: 25.8 us -> 0.38 us
  local copies, waits for them, and re-layouts: 18.5 us -> 1.23 us
  waiting for transfers between devices: 40.1 us -> 23.3 us
  other arithmetic: 1.71 us -> 3.83 us
    pallas_call x1 -> x7, Pallas kernels: 7.13 us -> 35.5 us  [the longest x4 14.6 us: project(): pl.pallas_call(functools.partial(project_kernel, first), out_shape=jax.Sh...]
    dot_general x3 -> x0, matrix products: 25.4 us -> none  [the longest x1 14.6 us: layer_block(): jnp.dot(activated, down_weight, preferred_element_type=jnp.float32)]
    unnamed x33 -> x16, local copies, waits for them, and re-layouts: 18.3 us -> 0.8 us
    ppermute x31, waiting for transfers between devices: 40.1 us -> 23.3 us  [swap(): return lax.ppermute(x, 'dev', [(i, i ^ by) for i in range(size)])]
  transfers between devices with their start and end apart: 31 -> 31, of which waited for: 15 -> 15; matrix products, arithmetic and copies ran while one was open for 0% -> 2% of each run, Pallas kernels for 0% -> 11%
where the time goes in v3:
time: 113 us
  starting transfers between devices  48.1 us (43%)
  Pallas kernels  35.5 us (31%)
  waiting for transfers between devices  23.3 us (21%)
  other arithmetic  3.83 us (3%)
  local copies, waits for them, and re-layouts  1.23 us (1%)
    ppermute x31, starting transfers between devices, swap(): return lax.ppermute(x, 'dev', [(i, i ^ by) for i in range(size)])  48.1 us
    ppermute x31, waiting for transfers between devices, swap(): return lax.ppermute(x, 'dev', [(i, i ^ by) for i in range(size)])  23.3 us
    pallas_call x4, Pallas kernels, project(): pl.pallas_call(functools.partial(project_kernel, first), out_shape=jax.Sh...  14.6 us
    pallas_call x2, Pallas kernels, hidden(): pl.pallas_call(functools.partial(hidden_kernel, first), out_shape=[jax.Sh...  11.3 us
    pallas_call x1, Pallas kernels, attend(): pl.pallas_call(functools.partial(attend_kernel, scale, groups, together),...  9.56 us
  transfers between devices with their start and end apart: 31, of which 15 were waited for; matrix products, arithmetic and copies ran while one was open for 2% of the time, Pallas kernels for 11%

profile of v3, /device:TPU:0, one launch (start us, length us, event | category | flops | bytes accessed | tf_op | source)
XLA Modules:
  0.0 112.8 jit_solution(11040712441626520504)
XLA Ops:
  0.7 9.6 %shard_map.118 = bf16[8,64,512]{2,1,0:T(8,128)(2,1)S(1)} custom-call(s32[1]{0:T(128)} %bitcast.place_ref, s32[8]{0:T(128)S(1)} %copy-done.2, bf16[8,64,576]{2,1,0:T(8,128)(2,1)} %query_hbm.1, bf16[8,576,1024]{2,1,0:T(8,128)(2,1)} %bitcast.114), custom_call_target="tpu_custom_call" | custom-call | flops 1140850688 | bytes 9437184 | tf_op jit(solution)/shard_map/pallas_call | solution.py:111
  10.4 6.1 %collective-permute-start.6 = (bf16[64,512]{1,0:T(8,128)(2,1)S(1)}, bf16[64,512]{1,0:T(8,128)(2,1)S(1)}, u32[]{:S(2)}, u32[]{:S(2)}) collective-permute-start(bf16[64,512]{1,0:T(8,128)(2,1)S(1)} %get-tuple-element.15), channel_id=1, source_target_pairs={{0,7},{1,6},{2,5},{3,4},{4,3},{5,2},{6,1},{7,0},{8,15},{9,14},{10,... | collective-permute-start | bytes 196616 | tf_op jit(solution)/shard_map/ppermute | solution.py:17
  17.4 2.0 %collective-permute-start.3 = (bf16[64,512]{1,0:T(8,128)(2,1)S(1)}, bf16[64,512]{1,0:T(8,128)(2,1)S(1)}, u32[]{:S(2)}, u32[]{:S(2)}) collective-permute-start(bf16[64,512]{1,0:T(8,128)(2,1)S(1)} %get-tuple-element.18), channel_id=1, source_target_pairs={{0,4},{1,5},{2,6},{3,7},{4,0},{5,1},{6,2},{7,3},{8,12},{9,13},{10,... | collective-permute-start | bytes 196616 | tf_op jit(solution)/shard_map/ppermute | solution.py:17
  19.4 1.6 %collective-permute-start = (bf16[64,512]{1,0:T(8,128)(2,1)S(1)}, bf16[64,512]{1,0:T(8,128)(2,1)S(1)}, u32[]{:S(2)}, u32[]{:S(2)}) collective-permute-start(bf16[64,512]{1,0:T(8,128)(2,1)S(1)} %get-tuple-element.21), channel_id=1, source_target_pairs={{0,1},{1,0},{2,3},{3,2},{4,5},{5,4},{6,7},{7,6},{8,9},{9,8},{10,11... | collective-permute-start | bytes 196616 | tf_op jit(solution)/shard_map/ppermute | solution.py:17
  25.1 3.2 %collective-permute-done.1 = bf16[64,512]{1,0:T(8,128)(2,1)S(1)} collective-permute-done((bf16[64,512]{1,0:T(8,128)(2,1)S(1)}, bf16[64,512]{1,0:T(8,128)(2,1)S(1)}, u32[]{:S(2)}, u32[]{:S(2)}) %collective-permute-start.1) | collective-permute-done | bytes 65568 | tf_op jit(solution)/shard_map/ppermute | solution.py:17
  28.3 2.4 %collective-permute-start.2 = (bf16[64,512]{1,0:T(8,128)(2,1)S(1)}, bf16[64,512]{1,0:T(8,128)(2,1)S(1)}, u32[]{:S(2)}, u32[]{:S(2)}) collective-permute-start(bf16[64,512]{1,0:T(8,128)(2,1)S(1)} %get-tuple-element.19), channel_id=1, source_target_pairs={{0,3},{1,2},{2,1},{3,0},{4,7},{5,6},{6,5},{7,4},{8,11},{9,10},{10,... | collective-permute-start | bytes 196616 | tf_op jit(solution)/shard_map/ppermute | solution.py:17
  30.7 2.8 %collective-permute-done.2 = bf16[64,512]{1,0:T(8,128)(2,1)S(1)} collective-permute-done((bf16[64,512]{1,0:T(8,128)(2,1)S(1)}, bf16[64,512]{1,0:T(8,128)(2,1)S(1)}, u32[]{:S(2)}, u32[]{:S(2)}) %collective-permute-start.2) | collective-permute-done | bytes 65568 | tf_op jit(solution)/shard_map/ppermute | solution.py:17
  34.0 3.7 %shard_map.120 = bf16[64,3584]{1,0:T(8,128)(2,1)S(1)} custom-call(bf16[64,1024]{1,0:T(8,128)(2,1)S(1)} %bitcast.112, f32[64,1]{1,0:T(8,128)S(1)} %broadcast_in_dim.55.scale_ref, bf16[1024,7168]{1,0:T(8,128)(2,1)} %weight_hbm.5), custom_call_target="tpu_custom_call" | custom-call | flops 469762048 | bytes 7340032 | tf_op jit(solution)/shard_map/pallas_call | solution.py:164
  37.7 1.5 %collective-permute-start.11 = (bf16[4,1,8,3584]{3,2,1,0:T(8,128)(2,1)S(1)}, bf16[4,1,8,3584]{3,2,1,0:T(8,128)(2,1)S(1)}, u32[]{:S(2)}, u32[]{:S(2)}) collective-permute-start(bf16[4,1,8,3584]{3,2,1,0:T(8,128)(2,1)S(1)} %slice.159), channel_id=1, source_target_pairs={{0,1},{1,0},{2,3},{3,2},{4,5},{5,4},{6,7},{7,6},{8,9},{9,8},{10,11... | collective-permute-start | bytes 688136 | tf_op jit(solution)/shard_map/ppermute | solution.py:17
  39.2 3.6 %shard_map.119 = bf16[64,3584]{1,0:T(8,128)(2,1)S(1)} custom-call(bf16[64,1024]{1,0:T(8,128)(2,1)S(1)} %bitcast.113, f32[64,1]{1,0:T(8,128)S(1)} %broadcast_in_dim.55.scale_ref, bf16[1024,7168]{1,0:T(8,128)(2,1)} %weight_hbm.5), custom_call_target="tpu_custom_call" | custom-call | flops 469762048 | bytes 7340032 | tf_op jit(solution)/shard_map/pallas_call | solution.py:164
  43.6 2.6 %collective-permute-done.11 = bf16[4,1,8,3584]{3,2,1,0:T(8,128)(2,1)S(1)} collective-permute-done((bf16[4,1,8,3584]{3,2,1,0:T(8,128)(2,1)S(1)}, bf16[4,1,8,3584]{3,2,1,0:T(8,128)(2,1)S(1)}, u32[]{:S(2)}, u32[]{:S(2)}) %collective-permute-start.11) | collective-permute-done | bytes 229408 | tf_op jit(solution)/shard_map/ppermute | solution.py:17
  46.2 4.1 %collective-permute-start.12 = (bf16[8,3584]{1,0:T(8,128)(2,1)S(1)}, bf16[8,3584]{1,0:T(8,128)(2,1)S(1)}, u32[]{:S(2)}, u32[]{:S(2)}) collective-permute-start(bf16[8,3584]{1,0:T(8,128)(2,1)S(1)} %get-tuple-element.32), channel_id=1, source_target_pairs={{0,6},{1,7},{2,4},{3,5},{4,2},{5,3},{6,0},{7,1},{8,14},{9,15},{10,... | collective-permute-start | bytes 172040 | tf_op jit(solution)/shard_map/ppermute | solution.py:17
  51.1 3.8 %collective-permute-start.8 = (bf16[8,3584]{1,0:T(8,128)(2,1)S(1)}, bf16[8,3584]{1,0:T(8,128)(2,1)S(1)}, u32[]{:S(2)}, u32[]{:S(2)}) collective-permute-start(bf16[8,3584]{1,0:T(8,128)(2,1)S(1)} %get-tuple-element.29), channel_id=1, source_target_pairs={{0,6},{1,7},{2,4},{3,5},{4,2},{5,3},{6,0},{7,1},{8,14},{9,15},{10,... | collective-permute-start | bytes 172040 | tf_op jit(solution)/shard_map/ppermute | solution.py:17
  56.1 1.5 %collective-permute-done.8 = bf16[8,3584]{1,0:T(8,128)(2,1)S(1)} collective-permute-done((bf16[8,3584]{1,0:T(8,128)(2,1)S(1)}, bf16[8,3584]{1,0:T(8,128)(2,1)S(1)}, u32[]{:S(2)}, u32[]{:S(2)}) %collective-permute-start.8) | collective-permute-done | bytes 57376 | tf_op jit(solution)/shard_map/ppermute | solution.py:17
  57.6 1.7 %collective-permute-done.10 = bf16[8,3584]{1,0:T(8,128)(2,1)S(1)} collective-permute-done((bf16[8,3584]{1,0:T(8,128)(2,1)S(1)}, bf16[8,3584]{1,0:T(8,128)(2,1)S(1)}, u32[]{:S(2)}, u32[]{:S(2)}) %collective-permute-start.10) | collective-permute-done | bytes 57376 | tf_op jit(solution)/shard_map/ppermute | solution.py:17
  59.3 1.3 %collective-permute-done.9 = bf16[8,3584]{1,0:T(8,128)(2,1)S(1)} collective-permute-done((bf16[8,3584]{1,0:T(8,128)(2,1)S(1)}, bf16[8,3584]{1,0:T(8,128)(2,1)S(1)}, u32[]{:S(2)}, u32[]{:S(2)}) %collective-permute-start.9) | collective-permute-done | bytes 57376 | tf_op jit(solution)/shard_map/ppermute | solution.py:17
  61.0 1.4 %collective-permute-start.20 = (bf16[8,3584]{1,0:T(8,128)(2,1)S(1)}, bf16[8,3584]{1,0:T(8,128)(2,1)S(1)}, u32[]{:S(2)}, u32[]{:S(2)}) collective-permute-start(bf16[8,3584]{1,0:T(8,128)(2,1)S(1)} %get-tuple-element.36), channel_id=1, source_target_pairs={{0,4},{1,5},{2,6},{3,7},{4,0},{5,1},{6,2},{7,3},{8,12},{9,13},{10,... | collective-permute-start | bytes 172040 | tf_op jit(solution)/shard_map/ppermute | solution.py:17
  62.4 3.7 %collective-permute-start.19 = (bf16[8,3584]{1,0:T(8,128)(2,1)S(1)}, bf16[8,3584]{1,0:T(8,128)(2,1)S(1)}, u32[]{:S(2)}, u32[]{:S(2)}) collective-permute-start(bf16[8,3584]{1,0:T(8,128)(2,1)S(1)} %get-tuple-element.36), channel_id=1, source_target_pairs={{0,2},{1,3},{2,0},{3,1},{4,6},{5,7},{6,4},{7,5},{8,10},{9,11},{10,... | collective-permute-start | bytes 172040 | tf_op jit(solution)/shard_map/ppermute | solution.py:17
  66.1 1.5 %collective-permute-start.16 = (bf16[8,3712]{1,0:T(8,128)(2,1)S(1)}, bf16[8,3712]{1,0:T(8,128)(2,1)S(1)}, u32[]{:S(2)}, u32[]{:S(2)}) collective-permute-start(bf16[8,3712]{1,0:T(8,128)(2,1)S(1)} %get-tuple-element.39), channel_id=1, source_target_pairs={{0,4},{1,5},{2,6},{3,7},{4,0},{5,1},{6,2},{7,3},{8,12},{9,13},{10,... | collective-permute-start | bytes 178184 | tf_op jit(solution)/shard_map/ppermute | solution.py:17
  67.6 2.9 %collective-permute-start.15 = (bf16[8,3712]{1,0:T(8,128)(2,1)S(1)}, bf16[8,3712]{1,0:T(8,128)(2,1)S(1)}, u32[]{:S(2)}, u32[]{:S(2)}) collective-permute-start(bf16[8,3712]{1,0:T(8,128)(2,1)S(1)} %get-tuple-element.39), channel_id=1, source_target_pairs={{0,2},{1,3},{2,0},{3,1},{4,6},{5,7},{6,4},{7,5},{8,10},{9,11},{10,... | collective-permute-start | bytes 178184 | tf_op jit(solution)/shard_map/ppermute | solution.py:17
  70.6 1.5 %collective-permute-done.21 = bf16[8,3584]{1,0:T(8,128)(2,1)S(1)} collective-permute-done((bf16[8,3584]{1,0:T(8,128)(2,1)S(1)}, bf16[8,3584]{1,0:T(8,128)(2,1)S(1)}, u32[]{:S(2)}, u32[]{:S(2)}) %collective-permute-start.21) | collective-permute-done | bytes 57376 | tf_op jit(solution)/shard_map/ppermute | solution.py:17
  73.0 3.5 %collective-permute-done.17 = bf16[8,3712]{1,0:T(8,128)(2,1)S(1)} collective-permute-done((bf16[8,3712]{1,0:T(8,128)(2,1)S(1)}, bf16[8,3712]{1,0:T(8,128)(2,1)S(1)}, u32[]{:S(2)}, u32[]{:S(2)}) %collective-permute-start.17) | collective-permute-done | bytes 59424 | tf_op jit(solution)/shard_map/ppermute | solution.py:17
  78.3 5.6 %shard_map.121 = (f32[64,1024]{1,0:T(8,128)S(1)}, f32[64,1024]{1,0:T(8,128)S(1)}) custom-call(bf16[64,3584]{1,0:T(8,128)(2,1)S(1)} %bitcast.111, bf16[7168,1024]{1,0:T(8,128)(2,1)} %gate_hbm.3, bf16[7168,1024]{1,0:T(8,128)(2,1)} %up_hbm.3, f32[64,1024]{1,0:T(8,128)S(1)} %broadcast_in_dim.61.gate_in.up_in, f32[64,1024]{1,0:T(8,128)S(1)} %broadcast_in_dim.61.gate_in.up_in), custom_call_target="tpu_custom_call" | custom-call | flops 939524096 | bytes 14680064 | tf_op jit(solution)/shard_map/pallas_call | solution.py:217
  84.3 5.7 %shard_map.122 = (f32[64,1024]{1,0:T(8,128)S(1)}, f32[64,1024]{1,0:T(8,128)S(1)}) custom-call(bf16[64,3584]{1,0:T(8,128)(2,1)S(1)} %slice.165.rows_ref, bf16[7168,1024]{1,0:T(8,128)(2,1)} %gate_hbm.3, bf16[7168,1024]{1,0:T(8,128)(2,1)} %up_hbm.3, f32[64,1024]{1,0:T(8,128)S(1)} %get-tuple-element.9.gate_in, f32[64,1024]{1,0:T(8,128)S(1)} %get-tuple-element.10.up_in), custom_call_target="tpu_custom_call" | custom-call | flops 939524096 | bytes 14680064 | tf_op jit(solution)/shard_map/pallas_call | solution.py:217
  90.1 3.7 %shard_map.124 = bf16[64,3584]{1,0:T(8,128)(2,1)S(1)} custom-call(bf16[64,1024]{1,0:T(8,128)(2,1)S(1)} %multiply_convert_fusion.rows_ref, f32[64,1]{1,0:T(8,128)S(1)} %copy.25.scale_ref, bf16[1024,7168]{1,0:T(8,128)(2,1)} %weight_hbm.7), custom_call_target="tpu_custom_call" | custom-call | flops 469762048 | bytes 7340032 | tf_op jit(solution)/shard_map/pallas_call | solution.py:164
  94.7 3.6 %shard_map.123 = bf16[64,3584]{1,0:T(8,128)(2,1)S(1)} custom-call(bf16[64,1024]{1,0:T(8,128)(2,1)S(1)} %multiply_convert_fusion.rows_ref, f32[64,1]{1,0:T(8,128)S(1)} %copy.25.scale_ref, bf16[1024,7168]{1,0:T(8,128)(2,1)} %weight_hbm.7), custom_call_target="tpu_custom_call" | custom-call | flops 469762048 | bytes 7340032 | tf_op jit(solution)/shard_map/pallas_call | solution.py:164
  98.4 1.2 %collective-permute-start.23 = (bf16[4,1,8,3584]{3,2,1,0:T(8,128)(2,1)S(1)}, bf16[4,1,8,3584]{3,2,1,0:T(8,128)(2,1)S(1)}, u32[]{:S(2)}, u32[]{:S(2)}) collective-permute-start(bf16[4,1,8,3584]{3,2,1,0:T(8,128)(2,1)S(1)} %slice.169), channel_id=1, source_target_pairs={{0,1},{1,0},{2,3},{3,2},{4,5},{5,4},{6,7},{7,6},{8,9},{9,8},{10,11... | collective-permute-start | bytes 688136 | tf_op jit(solution)/shard_map/ppermute | solution.py:17
  100.0 2.4 %collective-permute-start.28 = (bf16[8,3584]{1,0:T(8,128)(2,1)S(1)}, bf16[8,3584]{1,0:T(8,128)(2,1)S(1)}, u32[]{:S(2)}, u32[]{:S(2)}) collective-permute-start(bf16[8,3584]{1,0:T(8,128)(2,1)S(1)} %get-tuple-element.26), channel_id=1, source_target_pairs={{0,6},{1,7},{2,4},{3,5},{4,2},{5,3},{6,0},{7,1},{8,14},{9,15},{10,... | collective-permute-start | bytes 172040 | tf_op jit(solution)/shard_map/ppermute | solution.py:17
  102.4 2.1 %collective-permute-start.29 = (bf16[8,3584]{1,0:T(8,128)(2,1)S(1)}, bf16[8,3584]{1,0:T(8,128)(2,1)S(1)}, u32[]{:S(2)}, u32[]{:S(2)}) collective-permute-start(bf16[8,3584]{1,0:T(8,128)(2,1)S(1)} %get-tuple-element.28), channel_id=1, source_target_pairs={{0,4},{1,5},{2,6},{3,7},{4,0},{5,1},{6,2},{7,3},{8,12},{9,13},{10,... | collective-permute-start | bytes 172040 | tf_op jit(solution)/shard_map/ppermute | solution.py:17
  104.6 2.4 %collective-permute-start.24 = (bf16[8,3584]{1,0:T(8,128)(2,1)S(1)}, bf16[8,3584]{1,0:T(8,128)(2,1)S(1)}, u32[]{:S(2)}, u32[]{:S(2)}) collective-permute-start(bf16[8,3584]{1,0:T(8,128)(2,1)S(1)} %get-tuple-element.23), channel_id=1, source_target_pairs={{0,6},{1,7},{2,4},{3,5},{4,2},{5,3},{6,0},{7,1},{8,14},{9,15},{10,... | collective-permute-start | bytes 172040 | tf_op jit(solution)/shard_map/ppermute | solution.py:17
  107.0 2.1 %collective-permute-start.25 = (bf16[8,3584]{1,0:T(8,128)(2,1)S(1)}, bf16[8,3584]{1,0:T(8,128)(2,1)S(1)}, u32[]{:S(2)}, u32[]{:S(2)}) collective-permute-start(bf16[8,3584]{1,0:T(8,128)(2,1)S(1)} %get-tuple-element.25), channel_id=1, source_target_pairs={{0,4},{1,5},{2,6},{3,7},{4,0},{5,1},{6,2},{7,3},{8,12},{9,13},{10,... | collective-permute-start | bytes 172040 | tf_op jit(solution)/shard_map/ppermute | solution.py:17
  109.1 1.5 %collective-permute-done.24 = bf16[8,3584]{1,0:T(8,128)(2,1)S(1)} collective-permute-done((bf16[8,3584]{1,0:T(8,128)(2,1)S(1)}, bf16[8,3584]{1,0:T(8,128)(2,1)S(1)}, u32[]{:S(2)}, u32[]{:S(2)}) %collective-permute-start.24) | collective-permute-done | bytes 57376 | tf_op jit(solution)/shard_map/ppermute | solution.py:17
  (98 shorter events, 16.0 us)
Async XLA Ops:
  0.0 33.6 %copy-start = (bf16[8,512,128]{2,1,0:T(8,128)(2,1)S(1)}, bf16[8,512,128]{2,1,0:T(8,128)(2,1)}, u32[]{:S(2)}) copy-start(bf16[8,512,128]{2,1,0:T(8,128)(2,1)} %param.17) | copy-start | bytes 3145732
  10.4 23.2 %collective-permute-start.6 = (bf16[64,512]{1,0:T(8,128)(2,1)S(1)}, bf16[64,512]{1,0:T(8,128)(2,1)S(1)}, u32[]{:S(2)}, u32[]{:S(2)}) collective-permute-start(bf16[64,512]{1,0:T(8,128)(2,1)S(1)} %get-tuple-element.15), channel_id=1, source_target_pairs={{0,7},{1,6},{2,5},{3,4},{4,3},{5,2},{6,1},{7,0},{8,15},{9,14},{10,... | collective-permute-start | bytes 196616 | tf_op jit(solution)/shard_map/ppermute | solution.py:17
  16.4 17.1 %collective-permute-start.5 = (bf16[64,512]{1,0:T(8,128)(2,1)S(1)}, bf16[64,512]{1,0:T(8,128)(2,1)S(1)}, u32[]{:S(2)}, u32[]{:S(2)}) collective-permute-start(bf16[64,512]{1,0:T(8,128)(2,1)S(1)} %get-tuple-element.16), channel_id=1, source_target_pairs={{0,6},{1,7},{2,4},{3,5},{4,2},{5,3},{6,0},{7,1},{8,14},{9,15},{10,... | collective-permute-start | bytes 196616 | tf_op jit(solution)/shard_map/ppermute | solution.py:17
  16.7 16.8 %collective-permute-start.4 = (bf16[64,512]{1,0:T(8,128)(2,1)S(1)}, bf16[64,512]{1,0:T(8,128)(2,1)S(1)}, u32[]{:S(2)}, u32[]{:S(2)}) collective-permute-start(bf16[64,512]{1,0:T(8,128)(2,1)S(1)} %get-tuple-element.17), channel_id=1, source_target_pairs={{0,5},{1,4},{2,7},{3,6},{4,1},{5,0},{6,3},{7,2},{8,13},{9,12},{10,... | collective-permute-start | bytes 196616 | tf_op jit(solution)/shard_map/ppermute | solution.py:17
  17.4 16.1 %collective-permute-start.3 = (bf16[64,512]{1,0:T(8,128)(2,1)S(1)}, bf16[64,512]{1,0:T(8,128)(2,1)S(1)}, u32[]{:S(2)}, u32[]{:S(2)}) collective-permute-start(bf16[64,512]{1,0:T(8,128)(2,1)S(1)} %get-tuple-element.18), channel_id=1, source_target_pairs={{0,4},{1,5},{2,6},{3,7},{4,0},{5,1},{6,2},{7,3},{8,12},{9,13},{10,... | collective-permute-start | bytes 196616 | tf_op jit(solution)/shard_map/ppermute | solution.py:17
  19.4 4.5 %collective-permute-start = (bf16[64,512]{1,0:T(8,128)(2,1)S(1)}, bf16[64,512]{1,0:T(8,128)(2,1)S(1)}, u32[]{:S(2)}, u32[]{:S(2)}) collective-permute-start(bf16[64,512]{1,0:T(8,128)(2,1)S(1)} %get-tuple-element.21), channel_id=1, source_target_pairs={{0,1},{1,0},{2,3},{3,2},{4,5},{5,4},{6,7},{7,6},{8,9},{9,8},{10,11... | collective-permute-start | bytes 196616 | tf_op jit(solution)/shard_map/ppermute | solution.py:17
  23.9 4.4 %collective-permute-start.1 = (bf16[64,512]{1,0:T(8,128)(2,1)S(1)}, bf16[64,512]{1,0:T(8,128)(2,1)S(1)}, u32[]{:S(2)}, u32[]{:S(2)}) collective-permute-start(bf16[64,512]{1,0:T(8,128)(2,1)S(1)} %get-tuple-element.20), channel_id=1, source_target_pairs={{0,2},{1,3},{2,0},{3,1},{4,6},{5,7},{6,4},{7,5},{8,10},{9,11},{10,... | collective-permute-start | bytes 196616 | tf_op jit(solution)/shard_map/ppermute | solution.py:17
  28.3 5.2 %collective-permute-start.2 = (bf16[64,512]{1,0:T(8,128)(2,1)S(1)}, bf16[64,512]{1,0:T(8,128)(2,1)S(1)}, u32[]{:S(2)}, u32[]{:S(2)}) collective-permute-start(bf16[64,512]{1,0:T(8,128)(2,1)S(1)} %get-tuple-element.19), channel_id=1, source_target_pairs={{0,3},{1,2},{2,1},{3,0},{4,7},{5,6},{6,5},{7,4},{8,11},{9,10},{10,... | collective-permute-start | bytes 196616 | tf_op jit(solution)/shard_map/ppermute | solution.py:17
  37.7 8.4 %collective-permute-start.11 = (bf16[4,1,8,3584]{3,2,1,0:T(8,128)(2,1)S(1)}, bf16[4,1,8,3584]{3,2,1,0:T(8,128)(2,1)S(1)}, u32[]{:S(2)}, u32[]{:S(2)}) collective-permute-start(bf16[4,1,8,3584]{3,2,1,0:T(8,128)(2,1)S(1)} %slice.159), channel_id=1, source_target_pairs={{0,1},{1,0},{2,3},{3,2},{4,5},{5,4},{6,7},{7,6},{8,9},{9,8},{10,11... | collective-permute-start | bytes 688136 | tf_op jit(solution)/shard_map/ppermute | solution.py:17
  42.9 8.1 %collective-permute-start.7 = (bf16[4,1,8,3584]{3,2,1,0:T(8,128)(2,1)S(1)}, bf16[4,1,8,3584]{3,2,1,0:T(8,128)(2,1)S(1)}, u32[]{:S(2)}, u32[]{:S(2)}) collective-permute-start(bf16[4,1,8,3584]{3,2,1,0:T(8,128)(2,1)S(1)} %slice.153), channel_id=1, source_target_pairs={{0,1},{1,0},{2,3},{3,2},{4,5},{5,4},{6,7},{7,6},{8,9},{9,8},{10,11... | collective-permute-start | bytes 688136 | tf_op jit(solution)/shard_map/ppermute | solution.py:17
  46.2 8.7 %collective-permute-start.12 = (bf16[8,3584]{1,0:T(8,128)(2,1)S(1)}, bf16[8,3584]{1,0:T(8,128)(2,1)S(1)}, u32[]{:S(2)}, u32[]{:S(2)}) collective-permute-start(bf16[8,3584]{1,0:T(8,128)(2,1)S(1)} %get-tuple-element.32), channel_id=1, source_target_pairs={{0,6},{1,7},{2,4},{3,5},{4,2},{5,3},{6,0},{7,1},{8,14},{9,15},{10,... | collective-permute-start | bytes 172040 | tf_op jit(solution)/shard_map/ppermute | solution.py:17
  50.4 5.2 %collective-permute-start.14 = (bf16[8,3584]{1,0:T(8,128)(2,1)S(1)}, bf16[8,3584]{1,0:T(8,128)(2,1)S(1)}, u32[]{:S(2)}, u32[]{:S(2)}) collective-permute-start(bf16[8,3584]{1,0:T(8,128)(2,1)S(1)} %get-tuple-element.33), channel_id=1, source_target_pairs={{0,2},{1,3},{2,0},{3,1},{4,6},{5,7},{6,4},{7,5},{8,10},{9,11},{10,... | collective-permute-start | bytes 172040 | tf_op jit(solution)/shard_map/ppermute | solution.py:17
  50.4 5.7 %collective-permute-start.13 = (bf16[8,3584]{1,0:T(8,128)(2,1)S(1)}, bf16[8,3584]{1,0:T(8,128)(2,1)S(1)}, u32[]{:S(2)}, u32[]{:S(2)}) collective-permute-start(bf16[8,3584]{1,0:T(8,128)(2,1)S(1)} %get-tuple-element.34), channel_id=1, source_target_pairs={{0,4},{1,5},{2,6},{3,7},{4,0},{5,1},{6,2},{7,3},{8,12},{9,13},{10,... | collective-permute-start | bytes 172040 | tf_op jit(solution)/shard_map/ppermute | solution.py:17
  51.1 6.5 %collective-permute-start.8 = (bf16[8,3584]{1,0:T(8,128)(2,1)S(1)}, bf16[8,3584]{1,0:T(8,128)(2,1)S(1)}, u32[]{:S(2)}, u32[]{:S(2)}) collective-permute-start(bf16[8,3584]{1,0:T(8,128)(2,1)S(1)} %get-tuple-element.29), channel_id=1, source_target_pairs={{0,6},{1,7},{2,4},{3,5},{4,2},{5,3},{6,0},{7,1},{8,14},{9,15},{10,... | collective-permute-start | bytes 172040 | tf_op jit(solution)/shard_map/ppermute | solution.py:17
  54.9 4.4 %collective-permute-start.10 = (bf16[8,3584]{1,0:T(8,128)(2,1)S(1)}, bf16[8,3584]{1,0:T(8,128)(2,1)S(1)}, u32[]{:S(2)}, u32[]{:S(2)}) collective-permute-start(bf16[8,3584]{1,0:T(8,128)(2,1)S(1)} %get-tuple-element.30), channel_id=1, source_target_pairs={{0,2},{1,3},{2,0},{3,1},{4,6},{5,7},{6,4},{7,5},{8,10},{9,11},{10,... | collective-permute-start | bytes 172040 | tf_op jit(solution)/shard_map/ppermute | solution.py:17
  54.9 5.7 %collective-permute-start.9 = (bf16[8,3584]{1,0:T(8,128)(2,1)S(1)}, bf16[8,3584]{1,0:T(8,128)(2,1)S(1)}, u32[]{:S(2)}, u32[]{:S(2)}) collective-permute-start(bf16[8,3584]{1,0:T(8,128)(2,1)S(1)} %get-tuple-element.31), channel_id=1, source_target_pairs={{0,4},{1,5},{2,6},{3,7},{4,0},{5,1},{6,2},{7,3},{8,12},{9,13},{10,... | collective-permute-start | bytes 172040 | tf_op jit(solution)/shard_map/ppermute | solution.py:17
  61.0 9.6 %collective-permute-start.20 = (bf16[8,3584]{1,0:T(8,128)(2,1)S(1)}, bf16[8,3584]{1,0:T(8,128)(2,1)S(1)}, u32[]{:S(2)}, u32[]{:S(2)}) collective-permute-start(bf16[8,3584]{1,0:T(8,128)(2,1)S(1)} %get-tuple-element.36), channel_id=1, source_target_pairs={{0,4},{1,5},{2,6},{3,7},{4,0},{5,1},{6,2},{7,3},{8,12},{9,13},{10,... | collective-permute-start | bytes 172040 | tf_op jit(solution)/shard_map/ppermute | solution.py:17
  62.4 8.3 %collective-permute-start.19 = (bf16[8,3584]{1,0:T(8,128)(2,1)S(1)}, bf16[8,3584]{1,0:T(8,128)(2,1)S(1)}, u32[]{:S(2)}, u32[]{:S(2)}) collective-permute-start(bf16[8,3584]{1,0:T(8,128)(2,1)S(1)} %get-tuple-element.36), channel_id=1, source_target_pairs={{0,2},{1,3},{2,0},{3,1},{4,6},{5,7},{6,4},{7,5},{8,10},{9,11},{10,... | collective-permute-start | bytes 172040 | tf_op jit(solution)/shard_map/ppermute | solution.py:17
  66.1 6.0 %collective-permute-start.21 = (bf16[8,3584]{1,0:T(8,128)(2,1)S(1)}, bf16[8,3584]{1,0:T(8,128)(2,1)S(1)}, u32[]{:S(2)}, u32[]{:S(2)}) collective-permute-start(bf16[8,3584]{1,0:T(8,128)(2,1)S(1)} %get-tuple-element.36), channel_id=1, source_target_pairs={{0,6},{1,7},{2,4},{3,5},{4,2},{5,3},{6,0},{7,1},{8,14},{9,15},{10,... | collective-permute-start | bytes 172040 | tf_op jit(solution)/shard_map/ppermute | solution.py:17
  66.1 6.9 %collective-permute-start.16 = (bf16[8,3712]{1,0:T(8,128)(2,1)S(1)}, bf16[8,3712]{1,0:T(8,128)(2,1)S(1)}, u32[]{:S(2)}, u32[]{:S(2)}) collective-permute-start(bf16[8,3712]{1,0:T(8,128)(2,1)S(1)} %get-tuple-element.39), channel_id=1, source_target_pairs={{0,4},{1,5},{2,6},{3,7},{4,0},{5,1},{6,2},{7,3},{8,12},{9,13},{10,... | collective-permute-start | bytes 178184 | tf_op jit(solution)/shard_map/ppermute | solution.py:17
  67.6 5.4 %collective-permute-start.15 = (bf16[8,3712]{1,0:T(8,128)(2,1)S(1)}, bf16[8,3712]{1,0:T(8,128)(2,1)S(1)}, u32[]{:S(2)}, u32[]{:S(2)}) collective-permute-start(bf16[8,3712]{1,0:T(8,128)(2,1)S(1)} %get-tuple-element.39), channel_id=1, source_target_pairs={{0,2},{1,3},{2,0},{3,1},{4,6},{5,7},{6,4},{7,5},{8,10},{9,11},{10,... | collective-permute-start | bytes 178184 | tf_op jit(solution)/shard_map/ppermute | solution.py:17
  70.6 6.0 %collective-permute-start.17 = (bf16[8,3712]{1,0:T(8,128)(2,1)S(1)}, bf16[8,3712]{1,0:T(8,128)(2,1)S(1)}, u32[]{:S(2)}, u32[]{:S(2)}) collective-permute-start(bf16[8,3712]{1,0:T(8,128)(2,1)S(1)} %get-tuple-element.39), channel_id=1, source_target_pairs={{0,6},{1,7},{2,4},{3,5},{4,2},{5,3},{6,0},{7,1},{8,14},{9,15},{10,... | collective-permute-start | bytes 178184 | tf_op jit(solution)/shard_map/ppermute | solution.py:17
  72.1 6.1 %collective-permute-start.22 = (bf16[4,1,8,3584]{3,2,0,1:T(8,128)(2,1)S(1)}, bf16[4,1,8,3584]{3,2,0,1:T(8,128)(2,1)S(1)}, u32[]{:S(2)}, u32[]{:S(2)}) collective-permute-start(bf16[4,1,8,3584]{3,2,0,1:T(8,128)(2,1)S(1)} %maximum_bitcast_fusion.1), channel_id=1, source_target_pairs={{0,1},{1,0},{2,3},{3,2},{4,5},{5,4},{6,7},{7,6},{8,9},{9,8},{10,11... | collective-permute-start | bytes 688136 | tf_op jit(solution)/shard_map/ppermute | solution.py:17
  76.6 7.3 %collective-permute-start.18 = (bf16[4,1,8,3712]{3,2,0,1:T(8,128)(2,1)S(1)}, bf16[4,1,8,3712]{3,2,0,1:T(8,128)(2,1)S(1)}, u32[]{:S(2)}, u32[]{:S(2)}) collective-permute-start(bf16[4,1,8,3712]{3,2,0,1:T(8,128)(2,1)S(1)} %maximum_bitcast_fusion), channel_id=1, source_target_pairs={{0,1},{1,0},{2,3},{3,2},{4,5},{5,4},{6,7},{7,6},{8,9},{9,8},{10,11... | collective-permute-start | bytes 712712 | tf_op jit(solution)/shard_map/ppermute | solution.py:17
  93.8 6.1 %collective-permute-start.27 = (bf16[4,1,8,3584]{3,2,1,0:T(8,128)(2,1)S(1)}, bf16[4,1,8,3584]{3,2,1,0:T(8,128)(2,1)S(1)}, u32[]{:S(2)}, u32[]{:S(2)}) collective-permute-start(bf16[4,1,8,3584]{3,2,1,0:T(8,128)(2,1)S(1)} %slice.175), channel_id=1, source_target_pairs={{0,1},{1,0},{2,3},{3,2},{4,5},{5,4},{6,7},{7,6},{8,9},{9,8},{10,11... | collective-permute-start | bytes 688136 | tf_op jit(solution)/shard_map/ppermute | solution.py:17
  98.4 6.1 %collective-permute-start.23 = (bf16[4,1,8,3584]{3,2,1,0:T(8,128)(2,1)S(1)}, bf16[4,1,8,3584]{3,2,1,0:T(8,128)(2,1)S(1)}, u32[]{:S(2)}, u32[]{:S(2)}) collective-permute-start(bf16[4,1,8,3584]{3,2,1,0:T(8,128)(2,1)S(1)} %slice.169), channel_id=1, source_target_pairs={{0,1},{1,0},{2,3},{3,2},{4,5},{5,4},{6,7},{7,6},{8,9},{9,8},{10,11... | collective-permute-start | bytes 688136 | tf_op jit(solution)/shard_map/ppermute | solution.py:17
  100.0 7.0 %collective-permute-start.28 = (bf16[8,3584]{1,0:T(8,128)(2,1)S(1)}, bf16[8,3584]{1,0:T(8,128)(2,1)S(1)}, u32[]{:S(2)}, u32[]{:S(2)}) collective-permute-start(bf16[8,3584]{1,0:T(8,128)(2,1)S(1)} %get-tuple-element.26), channel_id=1, source_target_pairs={{0,6},{1,7},{2,4},{3,5},{4,2},{5,3},{6,0},{7,1},{8,14},{9,15},{10,... | collective-permute-start | bytes 172040 | tf_op jit(solution)/shard_map/ppermute | solution.py:17
  102.4 6.7 %collective-permute-start.30 = (bf16[8,3584]{1,0:T(8,128)(2,1)S(1)}, bf16[8,3584]{1,0:T(8,128)(2,1)S(1)}, u32[]{:S(2)}, u32[]{:S(2)}) collective-permute-start(bf16[8,3584]{1,0:T(8,128)(2,1)S(1)} %get-tuple-element.27), channel_id=1, source_target_pairs={{0,2},{1,3},{2,0},{3,1},{4,6},{5,7},{6,4},{7,5},{8,10},{9,11},{10,... | collective-permute-start | bytes 172040 | tf_op jit(solution)/shard_map/ppermute | solution.py:17
  102.4 6.7 %collective-permute-start.29 = (bf16[8,3584]{1,0:T(8,128)(2,1)S(1)}, bf16[8,3584]{1,0:T(8,128)(2,1)S(1)}, u32[]{:S(2)}, u32[]{:S(2)}) collective-permute-start(bf16[8,3584]{1,0:T(8,128)(2,1)S(1)} %get-tuple-element.28), channel_id=1, source_target_pairs={{0,4},{1,5},{2,6},{3,7},{4,0},{5,1},{6,2},{7,3},{8,12},{9,13},{10,... | collective-permute-start | bytes 172040 | tf_op jit(solution)/shard_map/ppermute | solution.py:17
  104.6 6.0 %collective-permute-start.24 = (bf16[8,3584]{1,0:T(8,128)(2,1)S(1)}, bf16[8,3584]{1,0:T(8,128)(2,1)S(1)}, u32[]{:S(2)}, u32[]{:S(2)}) collective-permute-start(bf16[8,3584]{1,0:T(8,128)(2,1)S(1)} %get-tuple-element.23), channel_id=1, source_target_pairs={{0,6},{1,7},{2,4},{3,5},{4,2},{5,3},{6,0},{7,1},{8,14},{9,15},{10,... | collective-permute-start | bytes 172040 | tf_op jit(solution)/shard_map/ppermute | solution.py:17
  107.0 4.3 %collective-permute-start.26 = (bf16[8,3584]{1,0:T(8,128)(2,1)S(1)}, bf16[8,3584]{1,0:T(8,128)(2,1)S(1)}, u32[]{:S(2)}, u32[]{:S(2)}) collective-permute-start(bf16[8,3584]{1,0:T(8,128)(2,1)S(1)} %get-tuple-element.24), channel_id=1, source_target_pairs={{0,2},{1,3},{2,0},{3,1},{4,6},{5,7},{6,4},{7,5},{8,10},{9,11},{10,... | collective-permute-start | bytes 172040 | tf_op jit(solution)/shard_map/ppermute | solution.py:17
  107.0 5.1 %collective-permute-start.25 = (bf16[8,3584]{1,0:T(8,128)(2,1)S(1)}, bf16[8,3584]{1,0:T(8,128)(2,1)S(1)}, u32[]{:S(2)}, u32[]{:S(2)}) collective-permute-start(bf16[8,3584]{1,0:T(8,128)(2,1)S(1)} %get-tuple-element.25), channel_id=1, source_target_pairs={{0,4},{1,5},{2,6},{3,7},{4,0},{5,1},{6,2},{7,3},{8,12},{9,13},{10,... | collective-permute-start | bytes 172040 | tf_op jit(solution)/shard_map/ppermute | solution.py:17
  (4 other events, 77.0 us)

commit v4 on v3

--- a/solution.py
+++ b/solution.py
@@ -29,6 +29,19 @@
     return total
 
 
+def exchange(x, earlier):
+    if earlier is not None:
+        x, _ = lax.optimization_barrier((x, earlier))
+    slabs = x.shape[1]
+    column = [x[0]] + [None] * (EXPERTS - 1)
+    for by in reversed(range(1, EXPERTS)):
+        column[by] = swap(x[by], by * slabs)
+    column_first = column[EXPERTS - 1]
+    column = jnp.stack(column, axis=0)
+    both = [column[:, 0]] + [swap(column[:, by], by) for by in range(1, slabs)]
+    return jnp.stack(both, axis=1), column_first
+
+
 def gather_rows(x, slabs):
     column = [x] + [None] * (EXPERTS - 1)
     for by in reversed(range(1, EXPERTS)):
@@ -45,14 +58,19 @@
     return pltpu.with_memory_space_constraint(x, pltpu.HBM)
 
 
+ATTEND_WINDOW = 4
+
+
 def attend_kernel(
     scale,
     groups,
     together,
+    first_token,
     place_ref,
     length_ref,
     query_hbm,
     cache_hbm,
+    _,
     out_ref,
     query_ref,
     cache_ref,
@@ -62,17 +80,21 @@
     tokens, heads, _ = query_ref.shape
     latent_width = out_ref.shape[2]
     each = heads // groups
-    query_copy = pltpu.make_async_copy(query_hbm, query_ref, query_sem)
+    chosen = pl.ds(first_token, tokens)
+    query_copy = pltpu.make_async_copy(query_hbm.at[chosen], query_ref, query_sem)
     query_copy.start()
-    copies = []
-    for t in range(tokens):
-        copy = pltpu.make_async_copy(cache_hbm.at[t], cache_ref.at[t], cache_sem.at[t])
+    copies = [
+        pltpu.make_async_copy(cache_hbm.at[first_token + t], cache_ref.at[t], cache_sem.at[t])
+        for t in range(tokens)
+    ]
+    for copy in copies[:ATTEND_WINDOW]:
         copy.start()
-        copies.append(copy)
     query_copy.wait()
 
     def scores_of(t):
         copies[t].wait()
+        if t + ATTEND_WINDOW < tokens:
+            copies[t + ATTEND_WINDOW].start()
         return jnp.dot(query_ref[t], cache_ref[t], preferred_element_type=jnp.float32)
 
     scores = scores_of(0)
@@ -80,7 +102,7 @@
     for t in range(tokens):
         later = scores_of(t + 1) if t + 1 < tokens else None
         position = lax.broadcasted_iota(jnp.int32, scores.shape, 1)
-        usable = position < length_ref[t]
+        usable = position < length_ref[first_token + t]
         masked = jnp.where(usable, scores * scale, -1e30)
         highest = jnp.max(masked, axis=1, keepdims=True)
         expos = jnp.where(usable, jnp.exp(masked - highest), 0.0)
@@ -103,19 +125,19 @@
         scores = later
 
 
-def attend(queries, latent_cache, cache_length, me, groups, latent_width, scale):
-    token_count, heads, key_width = queries.shape
+def attend(queries, latent_cache, cache_length, me, groups, latent_width, scale, first, token_count, after):
+    _, heads, key_width = queries.shape
     length = latent_cache.shape[1]
     each = heads // groups
     together = max(1, 16 // each)
     return pl.pallas_call(
-        functools.partial(attend_kernel, scale, groups, together),
+        functools.partial(attend_kernel, scale, groups, together, first),
         out_shape=jax.ShapeDtypeStruct((groups, token_count * each, latent_width), jnp.bfloat16),
         in_specs=[pl.BlockSpec(memory_space=pltpu.SMEM)] * 2
-        + [pl.BlockSpec(memory_space=pl.ANY)] * 2,
+        + [pl.BlockSpec(memory_space=pl.ANY)] * 3,
         out_specs=pl.BlockSpec(memory_space=pltpu.VMEM),
         scratch_shapes=[
-            pltpu.VMEM(queries.shape, queries.dtype),
+            pltpu.VMEM((token_count, heads, key_width), queries.dtype),
             pltpu.VMEM((token_count, key_width, length), latent_cache.dtype),
             pltpu.SemaphoreType.DMA,
             pltpu.SemaphoreType.DMA((token_count,)),
@@ -123,15 +145,20 @@
         compiler_params=pltpu.CompilerParams(vmem_limit_bytes=20 * 1024 * 1024),
         cost_estimate=pl.CostEstimate(
             flops=2 * token_count * heads * length * (key_width + latent_width),
-            bytes_accessed=2 * latent_cache.size,
+            bytes_accessed=2 * token_count * key_width * length,
             transcendentals=token_count * heads * length,
         ),
     )(
-        me.reshape(1), cache_length, streamed(queries), streamed(jnp.swapaxes(latent_cache, 1, 2))
+        me.reshape(1),
+        cache_length,
+        streamed(queries),
+        streamed(jnp.swapaxes(latent_cache, 1, 2)),
+        after,
     )
 
 
 DEPTH = 256
+WINDOW = 16
 
 
 def project_kernel(first, rows_ref, scale_ref, weight_hbm, out_ref, weight_ref, total_ref, sem):
@@ -142,10 +169,13 @@
         copy = pltpu.make_async_copy(
             weight_hbm.at[part, pl.ds(first, count)], weight_ref.at[part], sem.at[i]
         )
+        copies.append(copy)
+    for copy in copies[:WINDOW]:
         copy.start()
-        copies.append(copy)
     for i, copy in enumerate(copies):
         copy.wait()
+        if i + WINDOW < len(copies):
+            copies[i + WINDOW].start()
         part = pl.ds(i * DEPTH, DEPTH)
         product = jnp.dot(
             rows_ref[:, part], weight_ref[part, :], preferred_element_type=jnp.float32
@@ -192,14 +222,18 @@
                 target.at[pl.ds(i * STEP, STEP)],
                 sem.at[k, i],
             )
-            copy.start()
             copies.append(copy)
+    ahead = 2 * HIDDEN_WINDOW
+    for copy in copies[:ahead]:
+        copy.start()
     for i in range(count // STEP):
         part = pl.ds(i * STEP, STEP)
         for k, (weight, before, after) in enumerate(
             ((gate_ref, gate_in, gate_out), (up_ref, up_in, up_out))
         ):
             copies[2 * i + k].wait()
+            if 2 * i + k + ahead < len(copies):
+                copies[2 * i + k + ahead].start()
             product = jnp.dot(
                 rows_ref[:, part], weight[part, :], preferred_element_type=jnp.float32
             )
@@ -207,6 +241,7 @@
 
 
 STEP = 512
+HIDDEN_WINDOW = 16
 
 
 def hidden(rows, gate_weight, up_weight, gate, up, first, count):
@@ -254,14 +289,31 @@
     width = residual.shape[1]
     part = width // CHUNKS
 
-    latent_out = attend(
-        queries, latent_cache, cache_length, me, group_size, latent_width, score_scale
-    )
-    arrived = [latent_out[0]] + [None] * (group_size - 1)
-    for by in reversed(range(1, group_size)):
-        arrived[by] = swap(latent_out[by], by)
-    by_heads = jnp.stack(arrived, axis=0).reshape(
-        group_size * token_count, value_up.shape[0], latent_width
+    each = queries.shape[1] // group_size
+    last = max(1, 16 // each)
+    parts = [(0, token_count - last), (token_count - last, last)]
+    pieces = []
+    latent_out, hop = cache_length, None
+    for first, count in parts:
+        if count == 0:
+            continue
+        latent_out = attend(
+            queries,
+            latent_cache,
+            cache_length,
+            me,
+            group_size,
+            latent_width,
+            score_scale,
+            first,
+            count,
+            latent_out,
+        )
+        sent = latent_out.reshape(EXPERTS, slabs, count * each, latent_width)
+        arrived, hop = exchange(sent, hop)
+        pieces.append(arrived.reshape(group_size, count, each, latent_width))
+    by_heads = jnp.concatenate(pieces, axis=1).reshape(
+        group_size * token_count, each, latent_width
     )
     head_out = jnp.einsum(
         "thc,hcv->thv", by_heads, value_up, preferred_element_type=jnp.float32

time: 113 us -> 107 us (0.947)
  starting transfers between devices: 48.1 us -> 45.1 us
  waiting for transfers between devices: 23.3 us -> 20.7 us
  other arithmetic: 3.83 us -> 1.97 us
    ppermute x31 -> x32, starting transfers between devices: 48.1 us -> 45.1 us  [swap(): return lax.ppermute(x, 'dev', [(i, i ^ by) for i in range(size)])]
    ppermute x31 -> x32, waiting for transfers between devices: 23.3 us -> 20.7 us  [swap(): return lax.ppermute(x, 'dev', [(i, i ^ by) for i in range(size)])]
    pallas_call x1 -> x2, Pallas kernels: 9.56 us -> 10 us  [attend(): pl.pallas_call(functools.partial(attend_kernel, scale, groups, together,...]
  transfers between devices with their start and end apart: 31 -> 32, of which waited for: 15 -> 14; matrix products, arithmetic and copies ran while one was open for 2% -> 1% of each run, Pallas kernels for 11% -> 15%
where the time goes in v4:
time: 107 us
  starting transfers between devices  45.1 us (42%)
  Pallas kernels  36.1 us (34%)
  waiting for transfers between devices  20.7 us (19%)
  other arithmetic  1.97 us (2%)
  local copies, waits for them, and re-layouts  1.91 us (2%)
    ppermute x32, starting transfers between devices, swap(): return lax.ppermute(x, 'dev', [(i, i ^ by) for i in range(size)])  45.1 us
    ppermute x32, waiting for transfers between devices, swap(): return lax.ppermute(x, 'dev', [(i, i ^ by) for i in range(size)])  20.7 us
    pallas_call x4, Pallas kernels, project(): pl.pallas_call(functools.partial(project_kernel, first), out_shape=jax.Sh...  14.6 us
    pallas_call x2, Pallas kernels, hidden(): pl.pallas_call(functools.partial(hidden_kernel, first), out_shape=[jax.Sh...  11.5 us
    pallas_call x2, Pallas kernels, attend(): pl.pallas_call(functools.partial(attend_kernel, scale, groups, together,...  10 us
  transfers between devices with their start and end apart: 32, of which 14 were waited for; matrix products, arithmetic and copies ran while one was open for 1% of the time, Pallas kernels for 15%

profile of v4, /device:TPU:0, one launch (start us, length us, event | category | flops | bytes accessed | tf_op | source)
XLA Modules:
  0.0 106.6 jit_solution(15650440855236264067)
XLA Ops:
  0.8 6.8 %shard_map.118._ = bf16[8,48,512]{2,1,0:T(8,128)(2,1)S(1)} custom-call(s32[1]{0:T(128)} %bitcast.place_ref, s32[8]{0:T(128)S(1)} %copy-done.2, bf16[8,64,576]{2,1,0:T(8,128)(2,1)} %query_hbm.3, bf16[8,576,1024]{2,1,0:T(8,128)(2,1)} %bitcast.122, s32[8]{0:T(128)S(1)} %copy-done.2), custom_call_target="tpu_custom_call" | custom-call | flops 855638016 | bytes 7077888 | tf_op jit(solution)/shard_map/pallas_call | solution.py:133
  7.6 5.1 %collective-permute-start.2 = (bf16[2,48,512]{2,1,0:T(8,128)(2,1)S(1)}, bf16[2,48,512]{2,1,0:T(8,128)(2,1)S(1)}, u32[]{:S(2)}, u32[]{:S(2)}) collective-permute-start(bf16[2,48,512]{2,1,0:T(8,128)(2,1)S(1)} %get-tuple-element.20), channel_id=1, source_target_pairs={{0,6},{1,7},{2,4},{3,5},{4,2},{5,3},{6,0},{7,1},{8,14},{9,15},{10,... | collective-permute-start | bytes 294920 | tf_op jit(solution)/shard_map/ppermute | solution.py:17
  14.0 3.2 %shard_map.119 = bf16[8,16,512]{2,1,0:T(8,128)(2,1)S(1)} custom-call(s32[1]{0:T(128)} %bitcast.place_ref, s32[8]{0:T(128)S(1)} %copy-done.3, bf16[8,64,576]{2,1,0:T(8,128)(2,1)} %query_hbm.3, bf16[8,576,1024]{2,1,0:T(8,128)(2,1)} %bitcast.123, bf16[8,48,512]{2,1,0:T(8,128)(2,1)S(1)} %shard_map.118._), custom_call_target="tpu_custom_call" | custom-call | flops 285212672 | bytes 2359296 | tf_op jit(solution)/shard_map/pallas_call | solution.py:133
  17.4 3.8 %collective-permute-start.6 = (bf16[2,16,512]{2,1,0:T(8,128)(2,1)S(1)}, bf16[2,16,512]{2,1,0:T(8,128)(2,1)S(1)}, u32[]{:S(2)}, u32[]{:S(2)}) collective-permute-start(bf16[2,16,512]{2,1,0:T(8,128)(2,1)S(1)} %get-tuple-element.38), channel_id=1, source_target_pairs={{0,6},{1,7},{2,4},{3,5},{4,2},{5,3},{6,0},{7,1},{8,14},{9,15},{10,... | collective-permute-start | bytes 98312 | tf_op jit(solution)/shard_map/ppermute | solution.py:17
  22.2 1.6 %collective-permute-start.3 = (bf16[4,48,512]{2,1,0:T(8,128)(2,1)S(1)}, bf16[4,48,512]{2,1,0:T(8,128)(2,1)S(1)}, u32[]{:S(2)}, u32[]{:S(2)}) collective-permute-start(bf16[4,48,512]{2,1,0:T(8,128)(2,1)S(1)} %get-tuple-element.18), channel_id=1, source_target_pairs={{0,1},{1,0},{2,3},{3,2},{4,5},{5,4},{6,7},{7,6},{8,9},{9,8},{10,11... | collective-permute-start | bytes 589832 | tf_op jit(solution)/shard_map/ppermute | solution.py:17
  23.8 2.3 %collective-permute-done.5 = bf16[2,16,512]{2,1,0:T(8,128)(2,1)S(1)} collective-permute-done((bf16[2,16,512]{2,1,0:T(8,128)(2,1)S(1)}, bf16[2,16,512]{2,1,0:T(8,128)(2,1)S(1)}, u32[]{:S(2)}, u32[]{:S(2)}) %collective-permute-start.5) | collective-permute-done | bytes 32800 | tf_op jit(solution)/shard_map/ppermute | solution.py:17
  26.2 1.6 %collective-permute-start.7 = (bf16[4,16,512]{2,1,0:T(8,128)(2,1)S(1)}, bf16[4,16,512]{2,1,0:T(8,128)(2,1)S(1)}, u32[]{:S(2)}, u32[]{:S(2)}) collective-permute-start(bf16[4,16,512]{2,1,0:T(8,128)(2,1)S(1)} %get-tuple-element.36), channel_id=1, source_target_pairs={{0,1},{1,0},{2,3},{3,2},{4,5},{5,4},{6,7},{7,6},{8,9},{9,8},{10,11... | collective-permute-start | bytes 196616 | tf_op jit(solution)/shard_map/ppermute | solution.py:17
  27.8 2.7 %collective-permute-done.7 = bf16[4,16,512]{2,1,0:T(8,128)(2,1)S(1)} collective-permute-done((bf16[4,16,512]{2,1,0:T(8,128)(2,1)S(1)}, bf16[4,16,512]{2,1,0:T(8,128)(2,1)S(1)}, u32[]{:S(2)}, u32[]{:S(2)}) %collective-permute-start.7) | collective-permute-done | bytes 65568 | tf_op jit(solution)/shard_map/ppermute | solution.py:17
  31.2 3.7 %shard_map.121 = bf16[64,3584]{1,0:T(8,128)(2,1)S(1)} custom-call(bf16[64,1024]{1,0:T(8,128)(2,1)S(1)} %bitcast.119, f32[64,1]{1,0:T(8,128)S(1)} %broadcast_in_dim.55.scale_ref, bf16[1024,7168]{1,0:T(8,128)(2,1)} %weight_hbm.5), custom_call_target="tpu_custom_call" | custom-call | flops 469762048 | bytes 7340032 | tf_op jit(solution)/shard_map/pallas_call | solution.py:194
  34.9 1.6 %collective-permute-start.12 = (bf16[4,1,8,3584]{3,2,1,0:T(8,128)(2,1)S(1)}, bf16[4,1,8,3584]{3,2,1,0:T(8,128)(2,1)S(1)}, u32[]{:S(2)}, u32[]{:S(2)}) collective-permute-start(bf16[4,1,8,3584]{3,2,1,0:T(8,128)(2,1)S(1)} %slice.182), channel_id=1, source_target_pairs={{0,1},{1,0},{2,3},{3,2},{4,5},{5,4},{6,7},{7,6},{8,9},{9,8},{10,11... | collective-permute-start | bytes 688136 | tf_op jit(solution)/shard_map/ppermute | solution.py:17
  36.5 3.6 %shard_map.120 = bf16[64,3584]{1,0:T(8,128)(2,1)S(1)} custom-call(bf16[64,1024]{1,0:T(8,128)(2,1)S(1)} %bitcast.120, f32[64,1]{1,0:T(8,128)S(1)} %broadcast_in_dim.55.scale_ref, bf16[1024,7168]{1,0:T(8,128)(2,1)} %weight_hbm.5), custom_call_target="tpu_custom_call" | custom-call | flops 469762048 | bytes 7340032 | tf_op jit(solution)/shard_map/pallas_call | solution.py:194
  42.0 3.5 %collective-permute-start.13 = (bf16[8,3584]{1,0:T(8,128)(2,1)S(1)}, bf16[8,3584]{1,0:T(8,128)(2,1)S(1)}, u32[]{:S(2)}, u32[]{:S(2)}) collective-permute-start(bf16[8,3584]{1,0:T(8,128)(2,1)S(1)} %get-tuple-element.32), channel_id=1, source_target_pairs={{0,6},{1,7},{2,4},{3,5},{4,2},{5,3},{6,0},{7,1},{8,14},{9,15},{10,... | collective-permute-start | bytes 172040 | tf_op jit(solution)/shard_map/ppermute | solution.py:17
  46.6 3.5 %collective-permute-start.9 = (bf16[8,3584]{1,0:T(8,128)(2,1)S(1)}, bf16[8,3584]{1,0:T(8,128)(2,1)S(1)}, u32[]{:S(2)}, u32[]{:S(2)}) collective-permute-start(bf16[8,3584]{1,0:T(8,128)(2,1)S(1)} %get-tuple-element.29), channel_id=1, source_target_pairs={{0,6},{1,7},{2,4},{3,5},{4,2},{5,3},{6,0},{7,1},{8,14},{9,15},{10,... | collective-permute-start | bytes 172040 | tf_op jit(solution)/shard_map/ppermute | solution.py:17
  51.3 1.5 %collective-permute-done.9 = bf16[8,3584]{1,0:T(8,128)(2,1)S(1)} collective-permute-done((bf16[8,3584]{1,0:T(8,128)(2,1)S(1)}, bf16[8,3584]{1,0:T(8,128)(2,1)S(1)}, u32[]{:S(2)}, u32[]{:S(2)}) %collective-permute-start.9) | collective-permute-done | bytes 57376 | tf_op jit(solution)/shard_map/ppermute | solution.py:17
  52.8 1.5 %collective-permute-done.11 = bf16[8,3584]{1,0:T(8,128)(2,1)S(1)} collective-permute-done((bf16[8,3584]{1,0:T(8,128)(2,1)S(1)}, bf16[8,3584]{1,0:T(8,128)(2,1)S(1)}, u32[]{:S(2)}, u32[]{:S(2)}) %collective-permute-start.11) | collective-permute-done | bytes 57376 | tf_op jit(solution)/shard_map/ppermute | solution.py:17
  54.3 2.4 %collective-permute-done.10 = bf16[8,3584]{1,0:T(8,128)(2,1)S(1)} collective-permute-done((bf16[8,3584]{1,0:T(8,128)(2,1)S(1)}, bf16[8,3584]{1,0:T(8,128)(2,1)S(1)}, u32[]{:S(2)}, u32[]{:S(2)}) %collective-permute-start.10) | collective-permute-done | bytes 57376 | tf_op jit(solution)/shard_map/ppermute | solution.py:17
  57.5 2.3 %collective-permute-start.20 = (bf16[8,3584]{1,0:T(8,128)(2,1)S(1)}, bf16[8,3584]{1,0:T(8,128)(2,1)S(1)}, u32[]{:S(2)}, u32[]{:S(2)}) collective-permute-start(bf16[8,3584]{1,0:T(8,128)(2,1)S(1)} %get-tuple-element.42), channel_id=1, source_target_pairs={{0,2},{1,3},{2,0},{3,1},{4,6},{5,7},{6,4},{7,5},{8,10},{9,11},{10,... | collective-permute-start | bytes 172040 | tf_op jit(solution)/shard_map/ppermute | solution.py:17
  59.8 1.7 %collective-permute-start.22 = (bf16[8,3584]{1,0:T(8,128)(2,1)S(1)}, bf16[8,3584]{1,0:T(8,128)(2,1)S(1)}, u32[]{:S(2)}, u32[]{:S(2)}) collective-permute-start(bf16[8,3584]{1,0:T(8,128)(2,1)S(1)} %get-tuple-element.42), channel_id=1, source_target_pairs={{0,6},{1,7},{2,4},{3,5},{4,2},{5,3},{6,0},{7,1},{8,14},{9,15},{10,... | collective-permute-start | bytes 172040 | tf_op jit(solution)/shard_map/ppermute | solution.py:17
  61.6 2.7 %collective-permute-start.16 = (bf16[8,3712]{1,0:T(8,128)(2,1)S(1)}, bf16[8,3712]{1,0:T(8,128)(2,1)S(1)}, u32[]{:S(2)}, u32[]{:S(2)}) collective-permute-start(bf16[8,3712]{1,0:T(8,128)(2,1)S(1)} %get-tuple-element.45), channel_id=1, source_target_pairs={{0,2},{1,3},{2,0},{3,1},{4,6},{5,7},{6,4},{7,5},{8,10},{9,11},{10,... | collective-permute-start | bytes 178184 | tf_op jit(solution)/shard_map/ppermute | solution.py:17
  64.3 1.7 %collective-permute-start.18 = (bf16[8,3712]{1,0:T(8,128)(2,1)S(1)}, bf16[8,3712]{1,0:T(8,128)(2,1)S(1)}, u32[]{:S(2)}, u32[]{:S(2)}) collective-permute-start(bf16[8,3712]{1,0:T(8,128)(2,1)S(1)} %get-tuple-element.45), channel_id=1, source_target_pairs={{0,6},{1,7},{2,4},{3,5},{4,2},{5,3},{6,0},{7,1},{8,14},{9,15},{10,... | collective-permute-start | bytes 178184 | tf_op jit(solution)/shard_map/ppermute | solution.py:17
  67.1 3.2 %collective-permute-done.18 = bf16[8,3712]{1,0:T(8,128)(2,1)S(1)} collective-permute-done((bf16[8,3712]{1,0:T(8,128)(2,1)S(1)}, bf16[8,3712]{1,0:T(8,128)(2,1)S(1)}, u32[]{:S(2)}, u32[]{:S(2)}) %collective-permute-start.18) | collective-permute-done | bytes 59424 | tf_op jit(solution)/shard_map/ppermute | solution.py:17
  70.4 1.7 %collective-permute-done.23 = bf16[4,1,8,3584]{3,2,0,1:T(8,128)(2,1)S(1)} collective-permute-done((bf16[4,1,8,3584]{3,2,0,1:T(8,128)(2,1)S(1)}, bf16[4,1,8,3584]{3,2,0,1:T(8,128)(2,1)S(1)}, u32[]{:S(2)}, u32[]{:S(2)}) %collective-permute-start.23) | collective-permute-done | bytes 229408 | tf_op jit(solution)/shard_map/ppermute | solution.py:17
  72.2 5.6 %shard_map.122 = (f32[64,1024]{1,0:T(8,128)S(1)}, f32[64,1024]{1,0:T(8,128)S(1)}) custom-call(bf16[64,3584]{1,0:T(8,128)(2,1)S(1)} %bitcast.118, bf16[7168,1024]{1,0:T(8,128)(2,1)} %gate_hbm.3, bf16[7168,1024]{1,0:T(8,128)(2,1)} %up_hbm.3, f32[64,1024]{1,0:T(8,128)S(1)} %broadcast_in_dim.61.gate_in.up_in, f32[64,1024]{1,0:T(8,128)S(1)} %broadcast_in_dim.61.gate_in.up_in), custom_call_target="tpu_custom_call" | custom-call | flops 939524096 | bytes 14680064 | tf_op jit(solution)/shard_map/pallas_call | solution.py:252
  78.2 5.8 %shard_map.123 = (f32[64,1024]{1,0:T(8,128)S(1)}, f32[64,1024]{1,0:T(8,128)S(1)}) custom-call(bf16[64,3584]{1,0:T(8,128)(2,1)S(1)} %slice.188.rows_ref, bf16[7168,1024]{1,0:T(8,128)(2,1)} %gate_hbm.3, bf16[7168,1024]{1,0:T(8,128)(2,1)} %up_hbm.3, f32[64,1024]{1,0:T(8,128)S(1)} %get-tuple-element.11.gate_in, f32[64,1024]{1,0:T(8,128)S(1)} %get-tuple-element.12.up_in), custom_call_target="tpu_custom_call" | custom-call | flops 939524096 | bytes 14680064 | tf_op jit(solution)/shard_map/pallas_call | solution.py:252
  84.2 3.7 %shard_map.125 = bf16[64,3584]{1,0:T(8,128)(2,1)S(1)} custom-call(bf16[64,1024]{1,0:T(8,128)(2,1)S(1)} %multiply_convert_fusion.rows_ref, f32[64,1]{1,0:T(8,128)S(1)} %copy.46.scale_ref, bf16[1024,7168]{1,0:T(8,128)(2,1)} %weight_hbm.7), custom_call_target="tpu_custom_call" | custom-call | flops 469762048 | bytes 7340032 | tf_op jit(solution)/shard_map/pallas_call | solution.py:194
  88.3 3.6 %shard_map.124 = bf16[64,3584]{1,0:T(8,128)(2,1)S(1)} custom-call(bf16[64,1024]{1,0:T(8,128)(2,1)S(1)} %multiply_convert_fusion.rows_ref, f32[64,1]{1,0:T(8,128)S(1)} %copy.46.scale_ref, bf16[1024,7168]{1,0:T(8,128)(2,1)} %weight_hbm.7), custom_call_target="tpu_custom_call" | custom-call | flops 469762048 | bytes 7340032 | tf_op jit(solution)/shard_map/pallas_call | solution.py:194
  92.0 1.8 %collective-permute-start.24 = (bf16[4,1,8,3584]{3,2,1,0:T(8,128)(2,1)S(1)}, bf16[4,1,8,3584]{3,2,1,0:T(8,128)(2,1)S(1)}, u32[]{:S(2)}, u32[]{:S(2)}) collective-permute-start(bf16[4,1,8,3584]{3,2,1,0:T(8,128)(2,1)S(1)} %slice.192), channel_id=1, source_target_pairs={{0,1},{1,0},{2,3},{3,2},{4,5},{5,4},{6,7},{7,6},{8,9},{9,8},{10,11... | collective-permute-start | bytes 688136 | tf_op jit(solution)/shard_map/ppermute | solution.py:17
  94.1 2.2 %collective-permute-start.29 = (bf16[8,3584]{1,0:T(8,128)(2,1)S(1)}, bf16[8,3584]{1,0:T(8,128)(2,1)S(1)}, u32[]{:S(2)}, u32[]{:S(2)}) collective-permute-start(bf16[8,3584]{1,0:T(8,128)(2,1)S(1)} %get-tuple-element.26), channel_id=1, source_target_pairs={{0,6},{1,7},{2,4},{3,5},{4,2},{5,3},{6,0},{7,1},{8,14},{9,15},{10,... | collective-permute-start | bytes 172040 | tf_op jit(solution)/shard_map/ppermute | solution.py:17
  96.3 2.2 %collective-permute-start.30 = (bf16[8,3584]{1,0:T(8,128)(2,1)S(1)}, bf16[8,3584]{1,0:T(8,128)(2,1)S(1)}, u32[]{:S(2)}, u32[]{:S(2)}) collective-permute-start(bf16[8,3584]{1,0:T(8,128)(2,1)S(1)} %get-tuple-element.28), channel_id=1, source_target_pairs={{0,4},{1,5},{2,6},{3,7},{4,0},{5,1},{6,2},{7,3},{8,12},{9,13},{10,... | collective-permute-start | bytes 172040 | tf_op jit(solution)/shard_map/ppermute | solution.py:17
  98.6 2.2 %collective-permute-start.25 = (bf16[8,3584]{1,0:T(8,128)(2,1)S(1)}, bf16[8,3584]{1,0:T(8,128)(2,1)S(1)}, u32[]{:S(2)}, u32[]{:S(2)}) collective-permute-start(bf16[8,3584]{1,0:T(8,128)(2,1)S(1)} %get-tuple-element.23), channel_id=1, source_target_pairs={{0,6},{1,7},{2,4},{3,5},{4,2},{5,3},{6,0},{7,1},{8,14},{9,15},{10,... | collective-permute-start | bytes 172040 | tf_op jit(solution)/shard_map/ppermute | solution.py:17
  100.8 2.2 %collective-permute-start.26 = (bf16[8,3584]{1,0:T(8,128)(2,1)S(1)}, bf16[8,3584]{1,0:T(8,128)(2,1)S(1)}, u32[]{:S(2)}, u32[]{:S(2)}) collective-permute-start(bf16[8,3584]{1,0:T(8,128)(2,1)S(1)} %get-tuple-element.25), channel_id=1, source_target_pairs={{0,4},{1,5},{2,6},{3,7},{4,0},{5,1},{6,2},{7,3},{8,12},{9,13},{10,... | collective-permute-start | bytes 172040 | tf_op jit(solution)/shard_map/ppermute | solution.py:17
  103.1 1.6 %collective-permute-done.25 = bf16[8,3584]{1,0:T(8,128)(2,1)S(1)} collective-permute-done((bf16[8,3584]{1,0:T(8,128)(2,1)S(1)}, bf16[8,3584]{1,0:T(8,128)(2,1)S(1)}, u32[]{:S(2)}, u32[]{:S(2)}) %collective-permute-start.25) | collective-permute-done | bytes 57376 | tf_op jit(solution)/shard_map/ppermute | solution.py:17
  (109 shorter events, 13.4 us)
Async XLA Ops:
  7.6 9.8 %collective-permute-start.2 = (bf16[2,48,512]{2,1,0:T(8,128)(2,1)S(1)}, bf16[2,48,512]{2,1,0:T(8,128)(2,1)S(1)}, u32[]{:S(2)}, u32[]{:S(2)}) collective-permute-start(bf16[2,48,512]{2,1,0:T(8,128)(2,1)S(1)} %get-tuple-element.20), channel_id=1, source_target_pairs={{0,6},{1,7},{2,4},{3,5},{4,2},{5,3},{6,0},{7,1},{8,14},{9,15},{10,... | collective-permute-start | bytes 294920 | tf_op jit(solution)/shard_map/ppermute | solution.py:17
  12.7 9.5 %collective-permute-start.1 = (bf16[2,48,512]{2,1,0:T(8,128)(2,1)S(1)}, bf16[2,48,512]{2,1,0:T(8,128)(2,1)S(1)}, u32[]{:S(2)}, u32[]{:S(2)}) collective-permute-start(bf16[2,48,512]{2,1,0:T(8,128)(2,1)S(1)} %get-tuple-element.21), channel_id=1, source_target_pairs={{0,4},{1,5},{2,6},{3,7},{4,0},{5,1},{6,2},{7,3},{8,12},{9,13},{10,... | collective-permute-start | bytes 294920 | tf_op jit(solution)/shard_map/ppermute | solution.py:17
  12.7 9.5 %collective-permute-start = (bf16[2,48,512]{2,1,0:T(8,128)(2,1)S(1)}, bf16[2,48,512]{2,1,0:T(8,128)(2,1)S(1)}, u32[]{:S(2)}, u32[]{:S(2)}) collective-permute-start(bf16[2,48,512]{2,1,0:T(8,128)(2,1)S(1)} %get-tuple-element.22), channel_id=1, source_target_pairs={{0,2},{1,3},{2,0},{3,1},{4,6},{5,7},{6,4},{7,5},{8,10},{9,11},{10,... | collective-permute-start | bytes 294920 | tf_op jit(solution)/shard_map/ppermute | solution.py:17
  17.4 6.4 %collective-permute-start.6 = (bf16[2,16,512]{2,1,0:T(8,128)(2,1)S(1)}, bf16[2,16,512]{2,1,0:T(8,128)(2,1)S(1)}, u32[]{:S(2)}, u32[]{:S(2)}) collective-permute-start(bf16[2,16,512]{2,1,0:T(8,128)(2,1)S(1)} %get-tuple-element.38), channel_id=1, source_target_pairs={{0,6},{1,7},{2,4},{3,5},{4,2},{5,3},{6,0},{7,1},{8,14},{9,15},{10,... | collective-permute-start | bytes 98312 | tf_op jit(solution)/shard_map/ppermute | solution.py:17
  21.2 4.9 %collective-permute-start.5 = (bf16[2,16,512]{2,1,0:T(8,128)(2,1)S(1)}, bf16[2,16,512]{2,1,0:T(8,128)(2,1)S(1)}, u32[]{:S(2)}, u32[]{:S(2)}) collective-permute-start(bf16[2,16,512]{2,1,0:T(8,128)(2,1)S(1)} %get-tuple-element.39), channel_id=1, source_target_pairs={{0,4},{1,5},{2,6},{3,7},{4,0},{5,1},{6,2},{7,3},{8,12},{9,13},{10,... | collective-permute-start | bytes 98312 | tf_op jit(solution)/shard_map/ppermute | solution.py:17
  21.9 4.3 %collective-permute-start.4 = (bf16[2,16,512]{2,1,0:T(8,128)(2,1)S(1)}, bf16[2,16,512]{2,1,0:T(8,128)(2,1)S(1)}, u32[]{:S(2)}, u32[]{:S(2)}) collective-permute-start(bf16[2,16,512]{2,1,0:T(8,128)(2,1)S(1)} %get-tuple-element.40), channel_id=1, source_target_pairs={{0,2},{1,3},{2,0},{3,1},{4,6},{5,7},{6,4},{7,5},{8,10},{9,11},{10,... | collective-permute-start | bytes 98312 | tf_op jit(solution)/shard_map/ppermute | solution.py:17
  22.2 8.3 %collective-permute-start.3 = (bf16[4,48,512]{2,1,0:T(8,128)(2,1)S(1)}, bf16[4,48,512]{2,1,0:T(8,128)(2,1)S(1)}, u32[]{:S(2)}, u32[]{:S(2)}) collective-permute-start(bf16[4,48,512]{2,1,0:T(8,128)(2,1)S(1)} %get-tuple-element.18), channel_id=1, source_target_pairs={{0,1},{1,0},{2,3},{3,2},{4,5},{5,4},{6,7},{7,6},{8,9},{9,8},{10,11... | collective-permute-start | bytes 589832 | tf_op jit(solution)/shard_map/ppermute | solution.py:17
  26.2 4.3 %collective-permute-start.7 = (bf16[4,16,512]{2,1,0:T(8,128)(2,1)S(1)}, bf16[4,16,512]{2,1,0:T(8,128)(2,1)S(1)}, u32[]{:S(2)}, u32[]{:S(2)}) collective-permute-start(bf16[4,16,512]{2,1,0:T(8,128)(2,1)S(1)} %get-tuple-element.36), channel_id=1, source_target_pairs={{0,1},{1,0},{2,3},{3,2},{4,5},{5,4},{6,7},{7,6},{8,9},{9,8},{10,11... | collective-permute-start | bytes 196616 | tf_op jit(solution)/shard_map/ppermute | solution.py:17
  34.9 7.1 %collective-permute-start.12 = (bf16[4,1,8,3584]{3,2,1,0:T(8,128)(2,1)S(1)}, bf16[4,1,8,3584]{3,2,1,0:T(8,128)(2,1)S(1)}, u32[]{:S(2)}, u32[]{:S(2)}) collective-permute-start(bf16[4,1,8,3584]{3,2,1,0:T(8,128)(2,1)S(1)} %slice.182), channel_id=1, source_target_pairs={{0,1},{1,0},{2,3},{3,2},{4,5},{5,4},{6,7},{7,6},{8,9},{9,8},{10,11... | collective-permute-start | bytes 688136 | tf_op jit(solution)/shard_map/ppermute | solution.py:17
  40.1 6.4 %collective-permute-start.8 = (bf16[4,1,8,3584]{3,2,1,0:T(8,128)(2,1)S(1)}, bf16[4,1,8,3584]{3,2,1,0:T(8,128)(2,1)S(1)}, u32[]{:S(2)}, u32[]{:S(2)}) collective-permute-start(bf16[4,1,8,3584]{3,2,1,0:T(8,128)(2,1)S(1)} %slice.176), channel_id=1, source_target_pairs={{0,1},{1,0},{2,3},{3,2},{4,5},{5,4},{6,7},{7,6},{8,9},{9,8},{10,11... | collective-permute-start | bytes 688136 | tf_op jit(solution)/shard_map/ppermute | solution.py:17
  42.0 8.1 %collective-permute-start.13 = (bf16[8,3584]{1,0:T(8,128)(2,1)S(1)}, bf16[8,3584]{1,0:T(8,128)(2,1)S(1)}, u32[]{:S(2)}, u32[]{:S(2)}) collective-permute-start(bf16[8,3584]{1,0:T(8,128)(2,1)S(1)} %get-tuple-element.32), channel_id=1, source_target_pairs={{0,6},{1,7},{2,4},{3,5},{4,2},{5,3},{6,0},{7,1},{8,14},{9,15},{10,... | collective-permute-start | bytes 172040 | tf_op jit(solution)/shard_map/ppermute | solution.py:17
  45.6 5.5 %collective-permute-start.15 = (bf16[8,3584]{1,0:T(8,128)(2,1)S(1)}, bf16[8,3584]{1,0:T(8,128)(2,1)S(1)}, u32[]{:S(2)}, u32[]{:S(2)}) collective-permute-start(bf16[8,3584]{1,0:T(8,128)(2,1)S(1)} %get-tuple-element.33), channel_id=1, source_target_pairs={{0,2},{1,3},{2,0},{3,1},{4,6},{5,7},{6,4},{7,5},{8,10},{9,11},{10,... | collective-permute-start | bytes 172040 | tf_op jit(solution)/shard_map/ppermute | solution.py:17
  45.6 5.7 %collective-permute-start.14 = (bf16[8,3584]{1,0:T(8,128)(2,1)S(1)}, bf16[8,3584]{1,0:T(8,128)(2,1)S(1)}, u32[]{:S(2)}, u32[]{:S(2)}) collective-permute-start(bf16[8,3584]{1,0:T(8,128)(2,1)S(1)} %get-tuple-element.34), channel_id=1, source_target_pairs={{0,4},{1,5},{2,6},{3,7},{4,0},{5,1},{6,2},{7,3},{8,12},{9,13},{10,... | collective-permute-start | bytes 172040 | tf_op jit(solution)/shard_map/ppermute | solution.py:17
  46.6 6.2 %collective-permute-start.9 = (bf16[8,3584]{1,0:T(8,128)(2,1)S(1)}, bf16[8,3584]{1,0:T(8,128)(2,1)S(1)}, u32[]{:S(2)}, u32[]{:S(2)}) collective-permute-start(bf16[8,3584]{1,0:T(8,128)(2,1)S(1)} %get-tuple-element.29), channel_id=1, source_target_pairs={{0,6},{1,7},{2,4},{3,5},{4,2},{5,3},{6,0},{7,1},{8,14},{9,15},{10,... | collective-permute-start | bytes 172040 | tf_op jit(solution)/shard_map/ppermute | solution.py:17
  50.1 4.2 %collective-permute-start.11 = (bf16[8,3584]{1,0:T(8,128)(2,1)S(1)}, bf16[8,3584]{1,0:T(8,128)(2,1)S(1)}, u32[]{:S(2)}, u32[]{:S(2)}) collective-permute-start(bf16[8,3584]{1,0:T(8,128)(2,1)S(1)} %get-tuple-element.30), channel_id=1, source_target_pairs={{0,2},{1,3},{2,0},{3,1},{4,6},{5,7},{6,4},{7,5},{8,10},{9,11},{10,... | collective-permute-start | bytes 172040 | tf_op jit(solution)/shard_map/ppermute | solution.py:17
  50.1 6.6 %collective-permute-start.10 = (bf16[8,3584]{1,0:T(8,128)(2,1)S(1)}, bf16[8,3584]{1,0:T(8,128)(2,1)S(1)}, u32[]{:S(2)}, u32[]{:S(2)}) collective-permute-start(bf16[8,3584]{1,0:T(8,128)(2,1)S(1)} %get-tuple-element.31), channel_id=1, source_target_pairs={{0,4},{1,5},{2,6},{3,7},{4,0},{5,1},{6,2},{7,3},{8,12},{9,13},{10,... | collective-permute-start | bytes 172040 | tf_op jit(solution)/shard_map/ppermute | solution.py:17
  57.1 7.2 %collective-permute-start.21 = (bf16[8,3584]{1,0:T(8,128)(2,1)S(1)}, bf16[8,3584]{1,0:T(8,128)(2,1)S(1)}, u32[]{:S(2)}, u32[]{:S(2)}) collective-permute-start(bf16[8,3584]{1,0:T(8,128)(2,1)S(1)} %get-tuple-element.42), channel_id=1, source_target_pairs={{0,4},{1,5},{2,6},{3,7},{4,0},{5,1},{6,2},{7,3},{8,12},{9,13},{10,... | collective-permute-start | bytes 172040 | tf_op jit(solution)/shard_map/ppermute | solution.py:17
  57.5 8.4 %collective-permute-start.20 = (bf16[8,3584]{1,0:T(8,128)(2,1)S(1)}, bf16[8,3584]{1,0:T(8,128)(2,1)S(1)}, u32[]{:S(2)}, u32[]{:S(2)}) collective-permute-start(bf16[8,3584]{1,0:T(8,128)(2,1)S(1)} %get-tuple-element.42), channel_id=1, source_target_pairs={{0,2},{1,3},{2,0},{3,1},{4,6},{5,7},{6,4},{7,5},{8,10},{9,11},{10,... | collective-permute-start | bytes 172040 | tf_op jit(solution)/shard_map/ppermute | solution.py:17
  59.8 6.2 %collective-permute-start.22 = (bf16[8,3584]{1,0:T(8,128)(2,1)S(1)}, bf16[8,3584]{1,0:T(8,128)(2,1)S(1)}, u32[]{:S(2)}, u32[]{:S(2)}) collective-permute-start(bf16[8,3584]{1,0:T(8,128)(2,1)S(1)} %get-tuple-element.42), channel_id=1, source_target_pairs={{0,6},{1,7},{2,4},{3,5},{4,2},{5,3},{6,0},{7,1},{8,14},{9,15},{10,... | collective-permute-start | bytes 172040 | tf_op jit(solution)/shard_map/ppermute | solution.py:17
  61.5 5.6 %collective-permute-start.17 = (bf16[8,3712]{1,0:T(8,128)(2,1)S(1)}, bf16[8,3712]{1,0:T(8,128)(2,1)S(1)}, u32[]{:S(2)}, u32[]{:S(2)}) collective-permute-start(bf16[8,3712]{1,0:T(8,128)(2,1)S(1)} %get-tuple-element.45), channel_id=1, source_target_pairs={{0,4},{1,5},{2,6},{3,7},{4,0},{5,1},{6,2},{7,3},{8,12},{9,13},{10,... | collective-permute-start | bytes 178184 | tf_op jit(solution)/shard_map/ppermute | solution.py:17
  61.6 5.5 %collective-permute-start.16 = (bf16[8,3712]{1,0:T(8,128)(2,1)S(1)}, bf16[8,3712]{1,0:T(8,128)(2,1)S(1)}, u32[]{:S(2)}, u32[]{:S(2)}) collective-permute-start(bf16[8,3712]{1,0:T(8,128)(2,1)S(1)} %get-tuple-element.45), channel_id=1, source_target_pairs={{0,2},{1,3},{2,0},{3,1},{4,6},{5,7},{6,4},{7,5},{8,10},{9,11},{10,... | collective-permute-start | bytes 178184 | tf_op jit(solution)/shard_map/ppermute | solution.py:17
  64.3 6.0 %collective-permute-start.18 = (bf16[8,3712]{1,0:T(8,128)(2,1)S(1)}, bf16[8,3712]{1,0:T(8,128)(2,1)S(1)}, u32[]{:S(2)}, u32[]{:S(2)}) collective-permute-start(bf16[8,3712]{1,0:T(8,128)(2,1)S(1)} %get-tuple-element.45), channel_id=1, source_target_pairs={{0,6},{1,7},{2,4},{3,5},{4,2},{5,3},{6,0},{7,1},{8,14},{9,15},{10,... | collective-permute-start | bytes 178184 | tf_op jit(solution)/shard_map/ppermute | solution.py:17
  66.0 6.1 %collective-permute-start.23 = (bf16[4,1,8,3584]{3,2,0,1:T(8,128)(2,1)S(1)}, bf16[4,1,8,3584]{3,2,0,1:T(8,128)(2,1)S(1)}, u32[]{:S(2)}, u32[]{:S(2)}) collective-permute-start(bf16[4,1,8,3584]{3,2,0,1:T(8,128)(2,1)S(1)} %maximum_bitcast_fusion.1), channel_id=1, source_target_pairs={{0,1},{1,0},{2,3},{3,2},{4,5},{5,4},{6,7},{7,6},{8,9},{9,8},{10,11... | collective-permute-start | bytes 688136 | tf_op jit(solution)/shard_map/ppermute | solution.py:17
  70.3 7.5 %collective-permute-start.19 = (bf16[4,1,8,3712]{3,2,0,1:T(8,128)(2,1)S(1)}, bf16[4,1,8,3712]{3,2,0,1:T(8,128)(2,1)S(1)}, u32[]{:S(2)}, u32[]{:S(2)}) collective-permute-start(bf16[4,1,8,3712]{3,2,0,1:T(8,128)(2,1)S(1)} %maximum_bitcast_fusion), channel_id=1, source_target_pairs={{0,1},{1,0},{2,3},{3,2},{4,5},{5,4},{6,7},{7,6},{8,9},{9,8},{10,11... | collective-permute-start | bytes 712712 | tf_op jit(solution)/shard_map/ppermute | solution.py:17
  87.9 6.1 %collective-permute-start.28 = (bf16[4,1,8,3584]{3,2,1,0:T(8,128)(2,1)S(1)}, bf16[4,1,8,3584]{3,2,1,0:T(8,128)(2,1)S(1)}, u32[]{:S(2)}, u32[]{:S(2)}) collective-permute-start(bf16[4,1,8,3584]{3,2,1,0:T(8,128)(2,1)S(1)} %slice.198), channel_id=1, source_target_pairs={{0,1},{1,0},{2,3},{3,2},{4,5},{5,4},{6,7},{7,6},{8,9},{9,8},{10,11... | collective-permute-start | bytes 688136 | tf_op jit(solution)/shard_map/ppermute | solution.py:17
  92.0 6.6 %collective-permute-start.24 = (bf16[4,1,8,3584]{3,2,1,0:T(8,128)(2,1)S(1)}, bf16[4,1,8,3584]{3,2,1,0:T(8,128)(2,1)S(1)}, u32[]{:S(2)}, u32[]{:S(2)}) collective-permute-start(bf16[4,1,8,3584]{3,2,1,0:T(8,128)(2,1)S(1)} %slice.192), channel_id=1, source_target_pairs={{0,1},{1,0},{2,3},{3,2},{4,5},{5,4},{6,7},{7,6},{8,9},{9,8},{10,11... | collective-permute-start | bytes 688136 | tf_op jit(solution)/shard_map/ppermute | solution.py:17
  94.1 6.8 %collective-permute-start.29 = (bf16[8,3584]{1,0:T(8,128)(2,1)S(1)}, bf16[8,3584]{1,0:T(8,128)(2,1)S(1)}, u32[]{:S(2)}, u32[]{:S(2)}) collective-permute-start(bf16[8,3584]{1,0:T(8,128)(2,1)S(1)} %get-tuple-element.26), channel_id=1, source_target_pairs={{0,6},{1,7},{2,4},{3,5},{4,2},{5,3},{6,0},{7,1},{8,14},{9,15},{10,... | collective-permute-start | bytes 172040 | tf_op jit(solution)/shard_map/ppermute | solution.py:17
  96.3 6.8 %collective-permute-start.31 = (bf16[8,3584]{1,0:T(8,128)(2,1)S(1)}, bf16[8,3584]{1,0:T(8,128)(2,1)S(1)}, u32[]{:S(2)}, u32[]{:S(2)}) collective-permute-start(bf16[8,3584]{1,0:T(8,128)(2,1)S(1)} %get-tuple-element.27), channel_id=1, source_target_pairs={{0,2},{1,3},{2,0},{3,1},{4,6},{5,7},{6,4},{7,5},{8,10},{9,11},{10,... | collective-permute-start | bytes 172040 | tf_op jit(solution)/shard_map/ppermute | solution.py:17
  96.3 6.8 %collective-permute-start.30 = (bf16[8,3584]{1,0:T(8,128)(2,1)S(1)}, bf16[8,3584]{1,0:T(8,128)(2,1)S(1)}, u32[]{:S(2)}, u32[]{:S(2)}) collective-permute-start(bf16[8,3584]{1,0:T(8,128)(2,1)S(1)} %get-tuple-element.28), channel_id=1, source_target_pairs={{0,4},{1,5},{2,6},{3,7},{4,0},{5,1},{6,2},{7,3},{8,12},{9,13},{10,... | collective-permute-start | bytes 172040 | tf_op jit(solution)/shard_map/ppermute | solution.py:17
  98.6 6.1 %collective-permute-start.25 = (bf16[8,3584]{1,0:T(8,128)(2,1)S(1)}, bf16[8,3584]{1,0:T(8,128)(2,1)S(1)}, u32[]{:S(2)}, u32[]{:S(2)}) collective-permute-start(bf16[8,3584]{1,0:T(8,128)(2,1)S(1)} %get-tuple-element.23), channel_id=1, source_target_pairs={{0,6},{1,7},{2,4},{3,5},{4,2},{5,3},{6,0},{7,1},{8,14},{9,15},{10,... | collective-permute-start | bytes 172040 | tf_op jit(solution)/shard_map/ppermute | solution.py:17
  100.8 4.5 %collective-permute-start.27 = (bf16[8,3584]{1,0:T(8,128)(2,1)S(1)}, bf16[8,3584]{1,0:T(8,128)(2,1)S(1)}, u32[]{:S(2)}, u32[]{:S(2)}) collective-permute-start(bf16[8,3584]{1,0:T(8,128)(2,1)S(1)} %get-tuple-element.24), channel_id=1, source_target_pairs={{0,2},{1,3},{2,0},{3,1},{4,6},{5,7},{6,4},{7,5},{8,10},{9,11},{10,... | collective-permute-start | bytes 172040 | tf_op jit(solution)/shard_map/ppermute | solution.py:17
  100.8 5.1 %collective-permute-start.26 = (bf16[8,3584]{1,0:T(8,128)(2,1)S(1)}, bf16[8,3584]{1,0:T(8,128)(2,1)S(1)}, u32[]{:S(2)}, u32[]{:S(2)}) collective-permute-start(bf16[8,3584]{1,0:T(8,128)(2,1)S(1)} %get-tuple-element.25), channel_id=1, source_target_pairs={{0,4},{1,5},{2,6},{3,7},{4,0},{5,1},{6,2},{7,3},{8,12},{9,13},{10,... | collective-permute-start | bytes 172040 | tf_op jit(solution)/shard_map/ppermute | solution.py:17
  (8 other events, 140.5 us)

commit v5 on v4

--- a/solution.py
+++ b/solution.py
@@ -8,7 +8,10 @@
 from jax.sharding import PartitionSpec as P
 
 EXPERTS = 4
-CHUNKS = 2
+SUM_SPLIT = ((0, 4096), (4096, None))
+GATHER_SPLIT = ((0, 3072), (3072, None))
+MOE_SPLIT = ((0, 4096), (4096, None))
+HOPS = (2,1,3)
 LANES = 128
 
 
@@ -24,7 +27,7 @@
         x = (x[:, :slabs].astype(jnp.float32) + got.astype(jnp.float32)).astype(jnp.bfloat16)
     step = lax.axis_size("dev") // x.shape[0]
     total = x[0, 0].astype(jnp.float32)
-    for by in reversed(range(1, x.shape[0])):
+    for by in HOPS:
         total = total + swap(x[by, 0], by * step).astype(jnp.float32)
     return total
 
@@ -34,7 +37,7 @@
         x, _ = lax.optimization_barrier((x, earlier))
     slabs = x.shape[1]
     column = [x[0]] + [None] * (EXPERTS - 1)
-    for by in reversed(range(1, EXPERTS)):
+    for by in HOPS:
         column[by] = swap(x[by], by * slabs)
     column_first = column[EXPERTS - 1]
     column = jnp.stack(column, axis=0)
@@ -44,7 +47,7 @@
 
 def gather_rows(x, slabs):
     column = [x] + [None] * (EXPERTS - 1)
-    for by in reversed(range(1, EXPERTS)):
+    for by in HOPS:
         column[by] = swap(x, by * slabs)
     column = jnp.stack(column, axis=0)[:, None]
     by = 1
@@ -67,13 +70,15 @@
     together,
     first_token,
     place_ref,
-    length_ref,
+    length_hbm,
     query_hbm,
     cache_hbm,
     _,
     out_ref,
+    length_ref,
     query_ref,
     cache_ref,
+    length_sem,
     query_sem,
     cache_sem,
 ):
@@ -83,12 +88,15 @@
     chosen = pl.ds(first_token, tokens)
     query_copy = pltpu.make_async_copy(query_hbm.at[chosen], query_ref, query_sem)
     query_copy.start()
+    length_copy = pltpu.make_async_copy(length_hbm, length_ref, length_sem)
+    length_copy.start()
     copies = [
         pltpu.make_async_copy(cache_hbm.at[first_token + t], cache_ref.at[t], cache_sem.at[t])
         for t in range(tokens)
     ]
     for copy in copies[:ATTEND_WINDOW]:
         copy.start()
+    length_copy.wait()
     query_copy.wait()
 
     def scores_of(t):
@@ -133,12 +141,14 @@
     return pl.pallas_call(
         functools.partial(attend_kernel, scale, groups, together, first),
         out_shape=jax.ShapeDtypeStruct((groups, token_count * each, latent_width), jnp.bfloat16),
-        in_specs=[pl.BlockSpec(memory_space=pltpu.SMEM)] * 2
-        + [pl.BlockSpec(memory_space=pl.ANY)] * 3,
+        in_specs=[pl.BlockSpec(memory_space=pltpu.SMEM)]
+        + [pl.BlockSpec(memory_space=pl.ANY)] * 4,
         out_specs=pl.BlockSpec(memory_space=pltpu.VMEM),
         scratch_shapes=[
+            pltpu.SMEM(cache_length.shape, cache_length.dtype),
             pltpu.VMEM((token_count, heads, key_width), queries.dtype),
             pltpu.VMEM((token_count, key_width, length), latent_cache.dtype),
+            pltpu.SemaphoreType.DMA,
             pltpu.SemaphoreType.DMA,
             pltpu.SemaphoreType.DMA((token_count,)),
         ],
@@ -150,7 +160,7 @@
         ),
     )(
         me.reshape(1),
-        cache_length,
+        streamed(cache_length),
         streamed(queries),
         streamed(jnp.swapaxes(latent_cache, 1, 2)),
         after,
@@ -287,7 +297,6 @@
     latent_width = value_up.shape[1]
     score_scale = (value_up.shape[2] + queries.shape[2] - latent_width) ** (-0.5)
     width = residual.shape[1]
-    part = width // CHUNKS
 
     each = queries.shape[1] // group_size
     last = max(1, 16 // each)
@@ -321,8 +330,9 @@
     head_flat = head_out.reshape(head_out.shape[0], -1)
     ones = jnp.ones((head_flat.shape[0], 1), jnp.float32)
     attended = []
-    for i in range(CHUNKS):
-        product = project(head_flat, ones, out_weight, i * part, part)
+    for first, end in SUM_SPLIT:
+        part = (end or width) - first
+        product = project(head_flat, ones, out_weight, first, part)
         attended.append(sum_scatter(product.reshape(EXPERTS, slabs, token_count, part), slabs))
     attended = jnp.concatenate(attended, axis=1)
     stream = (residual.astype(jnp.float32) + attended).astype(jnp.bfloat16)
@@ -340,13 +350,13 @@
     mix_row = jnp.where(lane[0] < EXPERTS, high, mix_of - high).astype(jnp.bfloat16)
 
     rows = []
-    for i in range(CHUNKS):
-        piece = normed[:, i * part : (i + 1) * part]
-        if i == CHUNKS - 1:
+    for first, end in GATHER_SPLIT:
+        piece = normed[:, first:end]
+        if end is None:
             piece = jnp.concatenate([piece, mix_row], axis=1)
         rows.append(gather_rows(piece, slabs).reshape(group_size * token_count, -1))
-    mix_rows = rows[-1][:, part:].astype(jnp.float32)
-    rows[-1] = rows[-1][:, :part]
+    mix_rows = rows[-1][:, -LANES:].astype(jnp.float32)
+    rows[-1] = rows[-1][:, :-LANES]
     mine = me // slabs
     mix_mine = jnp.sum(
         jnp.where((lane[0] < 2 * EXPERTS) & (lane[0] % EXPERTS == mine), mix_rows, 0.0),
@@ -355,12 +365,13 @@
     )
 
     gate = up = jnp.zeros((rows[0].shape[0], gate_weight.shape[1]), jnp.float32)
-    for i in range(CHUNKS):
-        gate, up = hidden(rows[i], gate_weight, up_weight, gate, up, i * part, part)
+    for (first, _), piece in zip(GATHER_SPLIT, rows):
+        gate, up = hidden(piece, gate_weight, up_weight, gate, up, first, piece.shape[1])
     activated = (jax.nn.silu(gate) * up).astype(jnp.bfloat16)
     moe = []
-    for i in range(CHUNKS):
-        product = project(activated, mix_mine, down_weight, i * part, part)
+    for first, end in MOE_SPLIT:
+        part = (end or width) - first
+        product = project(activated, mix_mine, down_weight, first, part)
         moe.append(sum_scatter(product.reshape(EXPERTS, slabs, token_count, part), slabs))
     moe = jnp.concatenate(moe, axis=1)
     result = (stream_float + moe).astype(jnp.bfloat16)

time: 107 us -> 104 us (0.972)
  local copies, waits for them, and re-layouts: 1.91 us -> 0.52 us
  Pallas kernels: 36.1 us -> 35 us
    unnamed x17 -> x13, local copies, waits for them, and re-layouts: 1.45 us -> 0.06 us
  transfers between devices with their start and end apart: 32 -> 32, of which waited for: 14 -> 20; matrix products, arithmetic and copies ran while one was open for 1% -> 1% of each run, Pallas kernels for 15% -> 15%
where the time goes in v5:
time: 104 us
  starting transfers between devices  44.8 us (43%)
  Pallas kernels  35 us (34%)
  waiting for transfers between devices  20.8 us (20%)
  other arithmetic  1.97 us (2%)
    ppermute x32, starting transfers between devices, swap(): return lax.ppermute(x, 'dev', [(i, i ^ by) for i in range(size)])  44.8 us
    ppermute x32, waiting for transfers between devices, swap(): return lax.ppermute(x, 'dev', [(i, i ^ by) for i in range(size)])  20.8 us
    pallas_call x4, Pallas kernels, project(): pl.pallas_call(functools.partial(project_kernel, first), out_shape=jax.Sh...  14.6 us
    pallas_call x2, Pallas kernels, hidden(): pl.pallas_call(functools.partial(hidden_kernel, first), out_shape=[jax.Sh...  11.4 us
    pallas_call x2, Pallas kernels, attend(): pl.pallas_call(functools.partial(attend_kernel, scale, groups, together,...  9.01 us
  transfers between devices with their start and end apart: 32, of which 20 were waited for; matrix products, arithmetic and copies ran while one was open for 1% of the time, Pallas kernels for 15%

profile of v5, /device:TPU:0, one launch (start us, length us, event | category | flops | bytes accessed | tf_op | source)
XLA Modules:
  0.0 104.0 jit_solution(16626566017539582698)
XLA Ops:
  0.0 6.3 %shard_map.118._ = bf16[8,48,512]{2,1,0:T(8,128)(2,1)S(1)} custom-call(s32[1]{0:T(128)} %bitcast.place_ref, s32[8]{0:T(128)} %length_hbm.3, bf16[8,64,576]{2,1,0:T(8,128)(2,1)} %query_hbm.3, bf16[8,576,1024]{2,1,0:T(8,128)(2,1)} %bitcast.122, s32[8]{0:T(128)} %length_hbm.3), custom_call_target="tpu_custom_call" | custom-call | flops 855638016 | bytes 7077888 | tf_op jit(solution)/shard_map/pallas_call | solution.py:141
  6.4 5.1 %collective-permute-start.2 = (bf16[2,48,512]{2,1,0:T(8,128)(2,1)S(1)}, bf16[2,48,512]{2,1,0:T(8,128)(2,1)S(1)}, u32[]{:S(2)}, u32[]{:S(2)}) collective-permute-start(bf16[2,48,512]{2,1,0:T(8,128)(2,1)S(1)} %get-tuple-element.20), channel_id=1, source_target_pairs={{0,6},{1,7},{2,4},{3,5},{4,2},{5,3},{6,0},{7,1},{8,14},{9,15},{10,... | collective-permute-start | bytes 294920 | tf_op jit(solution)/shard_map/ppermute | solution.py:20
  12.1 2.7 %shard_map.119 = bf16[8,16,512]{2,1,0:T(8,128)(2,1)S(1)} custom-call(s32[1]{0:T(128)} %bitcast.place_ref, s32[8]{0:T(128)} %length_hbm.3, bf16[8,64,576]{2,1,0:T(8,128)(2,1)} %query_hbm.3, bf16[8,576,1024]{2,1,0:T(8,128)(2,1)} %bitcast.123, bf16[8,48,512]{2,1,0:T(8,128)(2,1)S(1)} %shard_map.118._), custom_call_target="tpu_custom_call" | custom-call | flops 285212672 | bytes 2359296 | tf_op jit(solution)/shard_map/pallas_call | solution.py:141
  15.2 3.8 %collective-permute-start.6 = (bf16[2,16,512]{2,1,0:T(8,128)(2,1)S(1)}, bf16[2,16,512]{2,1,0:T(8,128)(2,1)S(1)}, u32[]{:S(2)}, u32[]{:S(2)}) collective-permute-start(bf16[2,16,512]{2,1,0:T(8,128)(2,1)S(1)} %get-tuple-element.38), channel_id=1, source_target_pairs={{0,6},{1,7},{2,4},{3,5},{4,2},{5,3},{6,0},{7,1},{8,14},{9,15},{10,... | collective-permute-start | bytes 98312 | tf_op jit(solution)/shard_map/ppermute | solution.py:20
  19.1 1.7 %collective-permute-start.5 = (bf16[2,16,512]{2,1,0:T(8,128)(2,1)S(1)}, bf16[2,16,512]{2,1,0:T(8,128)(2,1)S(1)}, u32[]{:S(2)}, u32[]{:S(2)}) collective-permute-start(bf16[2,16,512]{2,1,0:T(8,128)(2,1)S(1)} %get-tuple-element.39), channel_id=1, source_target_pairs={{0,4},{1,5},{2,6},{3,7},{4,0},{5,1},{6,2},{7,3},{8,12},{9,13},{10,... | collective-permute-start | bytes 98312 | tf_op jit(solution)/shard_map/ppermute | solution.py:20
  21.4 1.6 %collective-permute-start.3 = (bf16[4,48,512]{2,1,0:T(8,128)(2,1)S(1)}, bf16[4,48,512]{2,1,0:T(8,128)(2,1)S(1)}, u32[]{:S(2)}, u32[]{:S(2)}) collective-permute-start(bf16[4,48,512]{2,1,0:T(8,128)(2,1)S(1)} %get-tuple-element.18), channel_id=1, source_target_pairs={{0,1},{1,0},{2,3},{3,2},{4,5},{5,4},{6,7},{7,6},{8,9},{9,8},{10,11... | collective-permute-start | bytes 589832 | tf_op jit(solution)/shard_map/ppermute | solution.py:20
  24.7 1.6 %collective-permute-start.7 = (bf16[4,16,512]{2,1,0:T(8,128)(2,1)S(1)}, bf16[4,16,512]{2,1,0:T(8,128)(2,1)S(1)}, u32[]{:S(2)}, u32[]{:S(2)}) collective-permute-start(bf16[4,16,512]{2,1,0:T(8,128)(2,1)S(1)} %get-tuple-element.36), channel_id=1, source_target_pairs={{0,1},{1,0},{2,3},{3,2},{4,5},{5,4},{6,7},{7,6},{8,9},{9,8},{10,11... | collective-permute-start | bytes 196616 | tf_op jit(solution)/shard_map/ppermute | solution.py:20
  26.3 2.8 %collective-permute-done.7 = bf16[4,16,512]{2,1,0:T(8,128)(2,1)S(1)} collective-permute-done((bf16[4,16,512]{2,1,0:T(8,128)(2,1)S(1)}, bf16[4,16,512]{2,1,0:T(8,128)(2,1)S(1)}, u32[]{:S(2)}, u32[]{:S(2)}) %collective-permute-start.7) | collective-permute-done | bytes 65568 | tf_op jit(solution)/shard_map/ppermute | solution.py:20
  29.6 3.3 %shard_map.121 = bf16[64,3072]{1,0:T(8,128)(2,1)S(1)} custom-call(bf16[64,1024]{1,0:T(8,128)(2,1)S(1)} %bitcast.119, f32[64,1]{1,0:T(8,128)S(1)} %broadcast_in_dim.55.scale_ref, bf16[1024,7168]{1,0:T(8,128)(2,1)} %weight_hbm.5), custom_call_target="tpu_custom_call" | custom-call | flops 402653184 | bytes 6291456 | tf_op jit(solution)/shard_map/pallas_call | solution.py:204
  33.0 1.6 %collective-permute-start.12 = (bf16[4,1,8,3072]{3,2,1,0:T(8,128)(2,1)S(1)}, bf16[4,1,8,3072]{3,2,1,0:T(8,128)(2,1)S(1)}, u32[]{:S(2)}, u32[]{:S(2)}) collective-permute-start(bf16[4,1,8,3072]{3,2,1,0:T(8,128)(2,1)S(1)} %slice.182), channel_id=1, source_target_pairs={{0,1},{1,0},{2,3},{3,2},{4,5},{5,4},{6,7},{7,6},{8,9},{9,8},{10,11... | collective-permute-start | bytes 589832 | tf_op jit(solution)/shard_map/ppermute | solution.py:20
  34.5 4.0 %shard_map.120 = bf16[64,4096]{1,0:T(8,128)(2,1)S(1)} custom-call(bf16[64,1024]{1,0:T(8,128)(2,1)S(1)} %bitcast.120, f32[64,1]{1,0:T(8,128)S(1)} %broadcast_in_dim.55.scale_ref, bf16[1024,7168]{1,0:T(8,128)(2,1)} %weight_hbm.5), custom_call_target="tpu_custom_call" | custom-call | flops 536870912 | bytes 8388608 | tf_op jit(solution)/shard_map/pallas_call | solution.py:204
  39.2 1.0 collective-permute-done.12
  40.3 2.1 %collective-permute-start.13 = (bf16[8,3072]{1,0:T(8,128)(2,1)S(1)}, bf16[8,3072]{1,0:T(8,128)(2,1)S(1)}, u32[]{:S(2)}, u32[]{:S(2)}) collective-permute-start(bf16[8,3072]{1,0:T(8,128)(2,1)S(1)} %get-tuple-element.32), channel_id=1, source_target_pairs={{0,4},{1,5},{2,6},{3,7},{4,0},{5,1},{6,2},{7,3},{8,12},{9,13},{10,... | collective-permute-start | bytes 147464 | tf_op jit(solution)/shard_map/ppermute | solution.py:20
  42.4 2.1 %collective-permute-start.15 = (bf16[8,3072]{1,0:T(8,128)(2,1)S(1)}, bf16[8,3072]{1,0:T(8,128)(2,1)S(1)}, u32[]{:S(2)}, u32[]{:S(2)}) collective-permute-start(bf16[8,3072]{1,0:T(8,128)(2,1)S(1)} %get-tuple-element.33), channel_id=1, source_target_pairs={{0,6},{1,7},{2,4},{3,5},{4,2},{5,3},{6,0},{7,1},{8,14},{9,15},{10,... | collective-permute-start | bytes 147464 | tf_op jit(solution)/shard_map/ppermute | solution.py:20
  45.1 1.8 %collective-permute-start.9 = (bf16[8,4096]{1,0:T(8,128)(2,1)S(1)}, bf16[8,4096]{1,0:T(8,128)(2,1)S(1)}, u32[]{:S(2)}, u32[]{:S(2)}) collective-permute-start(bf16[8,4096]{1,0:T(8,128)(2,1)S(1)} %get-tuple-element.26), channel_id=1, source_target_pairs={{0,4},{1,5},{2,6},{3,7},{4,0},{5,1},{6,2},{7,3},{8,12},{9,13},{10,... | collective-permute-start | bytes 196616 | tf_op jit(solution)/shard_map/ppermute | solution.py:20
  46.9 2.1 %collective-permute-start.11 = (bf16[8,4096]{1,0:T(8,128)(2,1)S(1)}, bf16[8,4096]{1,0:T(8,128)(2,1)S(1)}, u32[]{:S(2)}, u32[]{:S(2)}) collective-permute-start(bf16[8,4096]{1,0:T(8,128)(2,1)S(1)} %get-tuple-element.27), channel_id=1, source_target_pairs={{0,6},{1,7},{2,4},{3,5},{4,2},{5,3},{6,0},{7,1},{8,14},{9,15},{10,... | collective-permute-start | bytes 196616 | tf_op jit(solution)/shard_map/ppermute | solution.py:20
  50.4 2.6 %collective-permute-done.11 = bf16[8,4096]{1,0:T(8,128)(2,1)S(1)} collective-permute-done((bf16[8,4096]{1,0:T(8,128)(2,1)S(1)}, bf16[8,4096]{1,0:T(8,128)(2,1)S(1)}, u32[]{:S(2)}, u32[]{:S(2)}) %collective-permute-start.11) | collective-permute-done | bytes 65568 | tf_op jit(solution)/shard_map/ppermute | solution.py:20
  54.9 2.7 %collective-permute-start.20 = (bf16[8,3072]{1,0:T(8,128)(2,1)S(1)}, bf16[8,3072]{1,0:T(8,128)(2,1)S(1)}, u32[]{:S(2)}, u32[]{:S(2)}) collective-permute-start(bf16[8,3072]{1,0:T(8,128)(2,1)S(1)} %get-tuple-element.42), channel_id=1, source_target_pairs={{0,2},{1,3},{2,0},{3,1},{4,6},{5,7},{6,4},{7,5},{8,10},{9,11},{10,... | collective-permute-start | bytes 147464 | tf_op jit(solution)/shard_map/ppermute | solution.py:20
  57.5 1.0 collective-permute-start.22
  59.1 2.9 %collective-permute-start.16 = (bf16[8,4224]{1,0:T(8,128)(2,1)S(1)}, bf16[8,4224]{1,0:T(8,128)(2,1)S(1)}, u32[]{:S(2)}, u32[]{:S(2)}) collective-permute-start(bf16[8,4224]{1,0:T(8,128)(2,1)S(1)} %get-tuple-element.44), channel_id=1, source_target_pairs={{0,2},{1,3},{2,0},{3,1},{4,6},{5,7},{6,4},{7,5},{8,10},{9,11},{10,... | collective-permute-start | bytes 202760 | tf_op jit(solution)/shard_map/ppermute | solution.py:20
  65.0 3.1 %collective-permute-done.18 = bf16[8,4224]{1,0:T(8,128)(2,1)S(1)} collective-permute-done((bf16[8,4224]{1,0:T(8,128)(2,1)S(1)}, bf16[8,4224]{1,0:T(8,128)(2,1)S(1)}, u32[]{:S(2)}, u32[]{:S(2)}) %collective-permute-start.18) | collective-permute-done | bytes 67616 | tf_op jit(solution)/shard_map/ppermute | solution.py:20
  69.3 5.0 %shard_map.122 = (f32[64,1024]{1,0:T(8,128)S(1)}, f32[64,1024]{1,0:T(8,128)S(1)}) custom-call(bf16[64,3072]{1,0:T(8,128)(2,1)S(1)} %bitcast.114, bf16[7168,1024]{1,0:T(8,128)(2,1)} %gate_hbm.3, bf16[7168,1024]{1,0:T(8,128)(2,1)} %up_hbm.3, f32[64,1024]{1,0:T(8,128)S(1)} %broadcast_in_dim.61.gate_in.up_in, f32[64,1024]{1,0:T(8,128)S(1)} %broadcast_in_dim.61.gate_in.up_in), custom_call_target="tpu_custom_call" | custom-call | flops 805306368 | bytes 12582912 | tf_op jit(solution)/shard_map/pallas_call | solution.py:262
  75.0 6.4 %shard_map.123 = (f32[64,1024]{1,0:T(8,128)S(1)}, f32[64,1024]{1,0:T(8,128)S(1)}) custom-call(bf16[64,4096]{1,0:T(8,128)(2,1)S(1)} %slice.188.rows_ref, bf16[7168,1024]{1,0:T(8,128)(2,1)} %gate_hbm.3, bf16[7168,1024]{1,0:T(8,128)(2,1)} %up_hbm.3, f32[64,1024]{1,0:T(8,128)S(1)} %get-tuple-element.11.gate_in, f32[64,1024]{1,0:T(8,128)S(1)} %get-tuple-element.12.up_in), custom_call_target="tpu_custom_call" | custom-call | flops 1073741824 | bytes 16777216 | tf_op jit(solution)/shard_map/pallas_call | solution.py:262
  81.6 3.3 %shard_map.125 = bf16[64,3072]{1,0:T(8,128)(2,1)S(1)} custom-call(bf16[64,1024]{1,0:T(8,128)(2,1)S(1)} %multiply_convert_fusion.rows_ref, f32[64,1]{1,0:T(8,128)S(1)} %copy.46.scale_ref, bf16[1024,7168]{1,0:T(8,128)(2,1)} %weight_hbm.7), custom_call_target="tpu_custom_call" | custom-call | flops 402653184 | bytes 6291456 | tf_op jit(solution)/shard_map/pallas_call | solution.py:204
  85.8 4.0 %shard_map.124 = bf16[64,4096]{1,0:T(8,128)(2,1)S(1)} custom-call(bf16[64,1024]{1,0:T(8,128)(2,1)S(1)} %multiply_convert_fusion.rows_ref, f32[64,1]{1,0:T(8,128)S(1)} %copy.46.scale_ref, bf16[1024,7168]{1,0:T(8,128)(2,1)} %weight_hbm.7), custom_call_target="tpu_custom_call" | custom-call | flops 536870912 | bytes 8388608 | tf_op jit(solution)/shard_map/pallas_call | solution.py:204
  89.8 1.3 %collective-permute-start.24 = (bf16[4,1,8,4096]{3,2,1,0:T(8,128)(2,1)S(1)}, bf16[4,1,8,4096]{3,2,1,0:T(8,128)(2,1)S(1)}, u32[]{:S(2)}, u32[]{:S(2)}) collective-permute-start(bf16[4,1,8,4096]{3,2,1,0:T(8,128)(2,1)S(1)} %slice.192), channel_id=1, source_target_pairs={{0,1},{1,0},{2,3},{3,2},{4,5},{5,4},{6,7},{7,6},{8,9},{9,8},{10,11... | collective-permute-start | bytes 786440 | tf_op jit(solution)/shard_map/ppermute | solution.py:20
  91.2 2.7 %collective-permute-start.31 = (bf16[8,3072]{1,0:T(8,128)(2,1)S(1)}, bf16[8,3072]{1,0:T(8,128)(2,1)S(1)}, u32[]{:S(2)}, u32[]{:S(2)}) collective-permute-start(bf16[8,3072]{1,0:T(8,128)(2,1)S(1)} %get-tuple-element.30), channel_id=1, source_target_pairs={{0,6},{1,7},{2,4},{3,5},{4,2},{5,3},{6,0},{7,1},{8,14},{9,15},{10,... | collective-permute-start | bytes 147464 | tf_op jit(solution)/shard_map/ppermute | solution.py:20
  94.7 1.5 %collective-permute-done.24 = bf16[4,1,8,4096]{3,2,1,0:T(8,128)(2,1)S(1)} collective-permute-done((bf16[4,1,8,4096]{3,2,1,0:T(8,128)(2,1)S(1)}, bf16[4,1,8,4096]{3,2,1,0:T(8,128)(2,1)S(1)}, u32[]{:S(2)}, u32[]{:S(2)}) %collective-permute-start.24) | collective-permute-done | bytes 262176 | tf_op jit(solution)/shard_map/ppermute | solution.py:20
  96.4 2.1 %collective-permute-start.27 = (bf16[8,4096]{1,0:T(8,128)(2,1)S(1)}, bf16[8,4096]{1,0:T(8,128)(2,1)S(1)}, u32[]{:S(2)}, u32[]{:S(2)}) collective-permute-start(bf16[8,4096]{1,0:T(8,128)(2,1)S(1)} %get-tuple-element.24), channel_id=1, source_target_pairs={{0,6},{1,7},{2,4},{3,5},{4,2},{5,3},{6,0},{7,1},{8,14},{9,15},{10,... | collective-permute-start | bytes 196616 | tf_op jit(solution)/shard_map/ppermute | solution.py:20
  98.6 1.3 %collective-permute-start.26 = (bf16[8,4096]{1,0:T(8,128)(2,1)S(1)}, bf16[8,4096]{1,0:T(8,128)(2,1)S(1)}, u32[]{:S(2)}, u32[]{:S(2)}) collective-permute-start(bf16[8,4096]{1,0:T(8,128)(2,1)S(1)} %get-tuple-element.25), channel_id=1, source_target_pairs={{0,2},{1,3},{2,0},{3,1},{4,6},{5,7},{6,4},{7,5},{8,10},{9,11},{10,... | collective-permute-start | bytes 196616 | tf_op jit(solution)/shard_map/ppermute | solution.py:20
  99.9 1.6 %collective-permute-done.25 = bf16[8,4096]{1,0:T(8,128)(2,1)S(1)} collective-permute-done((bf16[8,4096]{1,0:T(8,128)(2,1)S(1)}, bf16[8,4096]{1,0:T(8,128)(2,1)S(1)}, u32[]{:S(2)}, u32[]{:S(2)}) %collective-permute-start.25) | collective-permute-done | bytes 65568 | tf_op jit(solution)/shard_map/ppermute | solution.py:20
  101.6 1.0 collective-permute-done.27
  (106 shorter events, 17.3 us)
Async XLA Ops:
  6.4 8.8 %collective-permute-start.2 = (bf16[2,48,512]{2,1,0:T(8,128)(2,1)S(1)}, bf16[2,48,512]{2,1,0:T(8,128)(2,1)S(1)}, u32[]{:S(2)}, u32[]{:S(2)}) collective-permute-start(bf16[2,48,512]{2,1,0:T(8,128)(2,1)S(1)} %get-tuple-element.20), channel_id=1, source_target_pairs={{0,6},{1,7},{2,4},{3,5},{4,2},{5,3},{6,0},{7,1},{8,14},{9,15},{10,... | collective-permute-start | bytes 294920 | tf_op jit(solution)/shard_map/ppermute | solution.py:20
  11.5 9.8 %collective-permute-start.1 = (bf16[2,48,512]{2,1,0:T(8,128)(2,1)S(1)}, bf16[2,48,512]{2,1,0:T(8,128)(2,1)S(1)}, u32[]{:S(2)}, u32[]{:S(2)}) collective-permute-start(bf16[2,48,512]{2,1,0:T(8,128)(2,1)S(1)} %get-tuple-element.21), channel_id=1, source_target_pairs={{0,4},{1,5},{2,6},{3,7},{4,0},{5,1},{6,2},{7,3},{8,12},{9,13},{10,... | collective-permute-start | bytes 294920 | tf_op jit(solution)/shard_map/ppermute | solution.py:20
  11.5 9.8 %collective-permute-start = (bf16[2,48,512]{2,1,0:T(8,128)(2,1)S(1)}, bf16[2,48,512]{2,1,0:T(8,128)(2,1)S(1)}, u32[]{:S(2)}, u32[]{:S(2)}) collective-permute-start(bf16[2,48,512]{2,1,0:T(8,128)(2,1)S(1)} %get-tuple-element.22), channel_id=1, source_target_pairs={{0,2},{1,3},{2,0},{3,1},{4,6},{5,7},{6,4},{7,5},{8,10},{9,11},{10,... | collective-permute-start | bytes 294920 | tf_op jit(solution)/shard_map/ppermute | solution.py:20
  15.2 7.8 %collective-permute-start.6 = (bf16[2,16,512]{2,1,0:T(8,128)(2,1)S(1)}, bf16[2,16,512]{2,1,0:T(8,128)(2,1)S(1)}, u32[]{:S(2)}, u32[]{:S(2)}) collective-permute-start(bf16[2,16,512]{2,1,0:T(8,128)(2,1)S(1)} %get-tuple-element.38), channel_id=1, source_target_pairs={{0,6},{1,7},{2,4},{3,5},{4,2},{5,3},{6,0},{7,1},{8,14},{9,15},{10,... | collective-permute-start | bytes 98312 | tf_op jit(solution)/shard_map/ppermute | solution.py:20
  19.1 4.8 %collective-permute-start.5 = (bf16[2,16,512]{2,1,0:T(8,128)(2,1)S(1)}, bf16[2,16,512]{2,1,0:T(8,128)(2,1)S(1)}, u32[]{:S(2)}, u32[]{:S(2)}) collective-permute-start(bf16[2,16,512]{2,1,0:T(8,128)(2,1)S(1)} %get-tuple-element.39), channel_id=1, source_target_pairs={{0,4},{1,5},{2,6},{3,7},{4,0},{5,1},{6,2},{7,3},{8,12},{9,13},{10,... | collective-permute-start | bytes 98312 | tf_op jit(solution)/shard_map/ppermute | solution.py:20
  20.7 3.9 %collective-permute-start.4 = (bf16[2,16,512]{2,1,0:T(8,128)(2,1)S(1)}, bf16[2,16,512]{2,1,0:T(8,128)(2,1)S(1)}, u32[]{:S(2)}, u32[]{:S(2)}) collective-permute-start(bf16[2,16,512]{2,1,0:T(8,128)(2,1)S(1)} %get-tuple-element.40), channel_id=1, source_target_pairs={{0,2},{1,3},{2,0},{3,1},{4,6},{5,7},{6,4},{7,5},{8,10},{9,11},{10,... | collective-permute-start | bytes 98312 | tf_op jit(solution)/shard_map/ppermute | solution.py:20
  21.4 7.6 %collective-permute-start.3 = (bf16[4,48,512]{2,1,0:T(8,128)(2,1)S(1)}, bf16[4,48,512]{2,1,0:T(8,128)(2,1)S(1)}, u32[]{:S(2)}, u32[]{:S(2)}) collective-permute-start(bf16[4,48,512]{2,1,0:T(8,128)(2,1)S(1)} %get-tuple-element.18), channel_id=1, source_target_pairs={{0,1},{1,0},{2,3},{3,2},{4,5},{5,4},{6,7},{7,6},{8,9},{9,8},{10,11... | collective-permute-start | bytes 589832 | tf_op jit(solution)/shard_map/ppermute | solution.py:20
  24.7 4.3 %collective-permute-start.7 = (bf16[4,16,512]{2,1,0:T(8,128)(2,1)S(1)}, bf16[4,16,512]{2,1,0:T(8,128)(2,1)S(1)}, u32[]{:S(2)}, u32[]{:S(2)}) collective-permute-start(bf16[4,16,512]{2,1,0:T(8,128)(2,1)S(1)} %get-tuple-element.36), channel_id=1, source_target_pairs={{0,1},{1,0},{2,3},{3,2},{4,5},{5,4},{6,7},{7,6},{8,9},{9,8},{10,11... | collective-permute-start | bytes 196616 | tf_op jit(solution)/shard_map/ppermute | solution.py:20
  33.0 7.2 %collective-permute-start.12 = (bf16[4,1,8,3072]{3,2,1,0:T(8,128)(2,1)S(1)}, bf16[4,1,8,3072]{3,2,1,0:T(8,128)(2,1)S(1)}, u32[]{:S(2)}, u32[]{:S(2)}) collective-permute-start(bf16[4,1,8,3072]{3,2,1,0:T(8,128)(2,1)S(1)} %slice.182), channel_id=1, source_target_pairs={{0,1},{1,0},{2,3},{3,2},{4,5},{5,4},{6,7},{7,6},{8,9},{9,8},{10,11... | collective-permute-start | bytes 589832 | tf_op jit(solution)/shard_map/ppermute | solution.py:20
  38.6 6.4 %collective-permute-start.8 = (bf16[4,1,8,4096]{3,2,1,0:T(8,128)(2,1)S(1)}, bf16[4,1,8,4096]{3,2,1,0:T(8,128)(2,1)S(1)}, u32[]{:S(2)}, u32[]{:S(2)}) collective-permute-start(bf16[4,1,8,4096]{3,2,1,0:T(8,128)(2,1)S(1)} %slice.176), channel_id=1, source_target_pairs={{0,1},{1,0},{2,3},{3,2},{4,5},{5,4},{6,7},{7,6},{8,9},{9,8},{10,11... | collective-permute-start | bytes 786440 | tf_op jit(solution)/shard_map/ppermute | solution.py:20
  40.3 8.7 %collective-permute-start.13 = (bf16[8,3072]{1,0:T(8,128)(2,1)S(1)}, bf16[8,3072]{1,0:T(8,128)(2,1)S(1)}, u32[]{:S(2)}, u32[]{:S(2)}) collective-permute-start(bf16[8,3072]{1,0:T(8,128)(2,1)S(1)} %get-tuple-element.32), channel_id=1, source_target_pairs={{0,4},{1,5},{2,6},{3,7},{4,0},{5,1},{6,2},{7,3},{8,12},{9,13},{10,... | collective-permute-start | bytes 147464 | tf_op jit(solution)/shard_map/ppermute | solution.py:20
  42.4 6.7 %collective-permute-start.15 = (bf16[8,3072]{1,0:T(8,128)(2,1)S(1)}, bf16[8,3072]{1,0:T(8,128)(2,1)S(1)}, u32[]{:S(2)}, u32[]{:S(2)}) collective-permute-start(bf16[8,3072]{1,0:T(8,128)(2,1)S(1)} %get-tuple-element.33), channel_id=1, source_target_pairs={{0,6},{1,7},{2,4},{3,5},{4,2},{5,3},{6,0},{7,1},{8,14},{9,15},{10,... | collective-permute-start | bytes 147464 | tf_op jit(solution)/shard_map/ppermute | solution.py:20
  44.4 5.2 %collective-permute-start.14 = (bf16[8,3072]{1,0:T(8,128)(2,1)S(1)}, bf16[8,3072]{1,0:T(8,128)(2,1)S(1)}, u32[]{:S(2)}, u32[]{:S(2)}) collective-permute-start(bf16[8,3072]{1,0:T(8,128)(2,1)S(1)} %get-tuple-element.34), channel_id=1, source_target_pairs={{0,2},{1,3},{2,0},{3,1},{4,6},{5,7},{6,4},{7,5},{8,10},{9,11},{10,... | collective-permute-start | bytes 147464 | tf_op jit(solution)/shard_map/ppermute | solution.py:20
  45.1 5.3 %collective-permute-start.9 = (bf16[8,4096]{1,0:T(8,128)(2,1)S(1)}, bf16[8,4096]{1,0:T(8,128)(2,1)S(1)}, u32[]{:S(2)}, u32[]{:S(2)}) collective-permute-start(bf16[8,4096]{1,0:T(8,128)(2,1)S(1)} %get-tuple-element.26), channel_id=1, source_target_pairs={{0,4},{1,5},{2,6},{3,7},{4,0},{5,1},{6,2},{7,3},{8,12},{9,13},{10,... | collective-permute-start | bytes 196616 | tf_op jit(solution)/shard_map/ppermute | solution.py:20
  46.9 6.1 %collective-permute-start.11 = (bf16[8,4096]{1,0:T(8,128)(2,1)S(1)}, bf16[8,4096]{1,0:T(8,128)(2,1)S(1)}, u32[]{:S(2)}, u32[]{:S(2)}) collective-permute-start(bf16[8,4096]{1,0:T(8,128)(2,1)S(1)} %get-tuple-element.27), channel_id=1, source_target_pairs={{0,6},{1,7},{2,4},{3,5},{4,2},{5,3},{6,0},{7,1},{8,14},{9,15},{10,... | collective-permute-start | bytes 196616 | tf_op jit(solution)/shard_map/ppermute | solution.py:20
  49.0 4.7 %collective-permute-start.10 = (bf16[8,4096]{1,0:T(8,128)(2,1)S(1)}, bf16[8,4096]{1,0:T(8,128)(2,1)S(1)}, u32[]{:S(2)}, u32[]{:S(2)}) collective-permute-start(bf16[8,4096]{1,0:T(8,128)(2,1)S(1)} %get-tuple-element.28), channel_id=1, source_target_pairs={{0,2},{1,3},{2,0},{3,1},{4,6},{5,7},{6,4},{7,5},{8,10},{9,11},{10,... | collective-permute-start | bytes 196616 | tf_op jit(solution)/shard_map/ppermute | solution.py:20
  54.1 7.9 %collective-permute-start.21 = (bf16[8,3072]{1,0:T(8,128)(2,1)S(1)}, bf16[8,3072]{1,0:T(8,128)(2,1)S(1)}, u32[]{:S(2)}, u32[]{:S(2)}) collective-permute-start(bf16[8,3072]{1,0:T(8,128)(2,1)S(1)} %get-tuple-element.42), channel_id=1, source_target_pairs={{0,4},{1,5},{2,6},{3,7},{4,0},{5,1},{6,2},{7,3},{8,12},{9,13},{10,... | collective-permute-start | bytes 147464 | tf_op jit(solution)/shard_map/ppermute | solution.py:20
  54.9 8.1 %collective-permute-start.20 = (bf16[8,3072]{1,0:T(8,128)(2,1)S(1)}, bf16[8,3072]{1,0:T(8,128)(2,1)S(1)}, u32[]{:S(2)}, u32[]{:S(2)}) collective-permute-start(bf16[8,3072]{1,0:T(8,128)(2,1)S(1)} %get-tuple-element.42), channel_id=1, source_target_pairs={{0,2},{1,3},{2,0},{3,1},{4,6},{5,7},{6,4},{7,5},{8,10},{9,11},{10,... | collective-permute-start | bytes 147464 | tf_op jit(solution)/shard_map/ppermute | solution.py:20
  57.5 5.9 %collective-permute-start.22 = (bf16[8,3072]{1,0:T(8,128)(2,1)S(1)}, bf16[8,3072]{1,0:T(8,128)(2,1)S(1)}, u32[]{:S(2)}, u32[]{:S(2)}) collective-permute-start(bf16[8,3072]{1,0:T(8,128)(2,1)S(1)} %get-tuple-element.42), channel_id=1, source_target_pairs={{0,6},{1,7},{2,4},{3,5},{4,2},{5,3},{6,0},{7,1},{8,14},{9,15},{10,... | collective-permute-start | bytes 147464 | tf_op jit(solution)/shard_map/ppermute | solution.py:20
  58.5 6.4 %collective-permute-start.17 = (bf16[8,4224]{1,0:T(8,128)(2,1)S(1)}, bf16[8,4224]{1,0:T(8,128)(2,1)S(1)}, u32[]{:S(2)}, u32[]{:S(2)}) collective-permute-start(bf16[8,4224]{1,0:T(8,128)(2,1)S(1)} %get-tuple-element.44), channel_id=1, source_target_pairs={{0,4},{1,5},{2,6},{3,7},{4,0},{5,1},{6,2},{7,3},{8,12},{9,13},{10,... | collective-permute-start | bytes 202760 | tf_op jit(solution)/shard_map/ppermute | solution.py:20
  59.1 5.9 %collective-permute-start.16 = (bf16[8,4224]{1,0:T(8,128)(2,1)S(1)}, bf16[8,4224]{1,0:T(8,128)(2,1)S(1)}, u32[]{:S(2)}, u32[]{:S(2)}) collective-permute-start(bf16[8,4224]{1,0:T(8,128)(2,1)S(1)} %get-tuple-element.44), channel_id=1, source_target_pairs={{0,2},{1,3},{2,0},{3,1},{4,6},{5,7},{6,4},{7,5},{8,10},{9,11},{10,... | collective-permute-start | bytes 202760 | tf_op jit(solution)/shard_map/ppermute | solution.py:20
  62.0 6.1 %collective-permute-start.18 = (bf16[8,4224]{1,0:T(8,128)(2,1)S(1)}, bf16[8,4224]{1,0:T(8,128)(2,1)S(1)}, u32[]{:S(2)}, u32[]{:S(2)}) collective-permute-start(bf16[8,4224]{1,0:T(8,128)(2,1)S(1)} %get-tuple-element.44), channel_id=1, source_target_pairs={{0,6},{1,7},{2,4},{3,5},{4,2},{5,3},{6,0},{7,1},{8,14},{9,15},{10,... | collective-permute-start | bytes 202760 | tf_op jit(solution)/shard_map/ppermute | solution.py:20
  63.5 5.7 %collective-permute-start.23 = (bf16[4,1,8,3072]{3,2,0,1:T(8,128)(2,1)S(1)}, bf16[4,1,8,3072]{3,2,0,1:T(8,128)(2,1)S(1)}, u32[]{:S(2)}, u32[]{:S(2)}) collective-permute-start(bf16[4,1,8,3072]{3,2,0,1:T(8,128)(2,1)S(1)} %maximum_bitcast_fusion.1), channel_id=1, source_target_pairs={{0,1},{1,0},{2,3},{3,2},{4,5},{5,4},{6,7},{7,6},{8,9},{9,8},{10,11... | collective-permute-start | bytes 589832 | tf_op jit(solution)/shard_map/ppermute | solution.py:20
  68.1 6.5 %collective-permute-start.19 = (bf16[4,1,8,4224]{3,2,0,1:T(8,128)(2,1)S(1)}, bf16[4,1,8,4224]{3,2,0,1:T(8,128)(2,1)S(1)}, u32[]{:S(2)}, u32[]{:S(2)}) collective-permute-start(bf16[4,1,8,4224]{3,2,0,1:T(8,128)(2,1)S(1)} %maximum_bitcast_fusion), channel_id=1, source_target_pairs={{0,1},{1,0},{2,3},{3,2},{4,5},{5,4},{6,7},{7,6},{8,9},{9,8},{10,11... | collective-permute-start | bytes 811016 | tf_op jit(solution)/shard_map/ppermute | solution.py:20
  84.9 6.2 %collective-permute-start.28 = (bf16[4,1,8,3072]{3,2,1,0:T(8,128)(2,1)S(1)}, bf16[4,1,8,3072]{3,2,1,0:T(8,128)(2,1)S(1)}, u32[]{:S(2)}, u32[]{:S(2)}) collective-permute-start(bf16[4,1,8,3072]{3,2,1,0:T(8,128)(2,1)S(1)} %slice.198), channel_id=1, source_target_pairs={{0,1},{1,0},{2,3},{3,2},{4,5},{5,4},{6,7},{7,6},{8,9},{9,8},{10,11... | collective-permute-start | bytes 589832 | tf_op jit(solution)/shard_map/ppermute | solution.py:20
  89.8 6.4 %collective-permute-start.24 = (bf16[4,1,8,4096]{3,2,1,0:T(8,128)(2,1)S(1)}, bf16[4,1,8,4096]{3,2,1,0:T(8,128)(2,1)S(1)}, u32[]{:S(2)}, u32[]{:S(2)}) collective-permute-start(bf16[4,1,8,4096]{3,2,1,0:T(8,128)(2,1)S(1)} %slice.192), channel_id=1, source_target_pairs={{0,1},{1,0},{2,3},{3,2},{4,5},{5,4},{6,7},{7,6},{8,9},{9,8},{10,11... | collective-permute-start | bytes 786440 | tf_op jit(solution)/shard_map/ppermute | solution.py:20
  91.2 7.4 %collective-permute-start.29 = (bf16[8,3072]{1,0:T(8,128)(2,1)S(1)}, bf16[8,3072]{1,0:T(8,128)(2,1)S(1)}, u32[]{:S(2)}, u32[]{:S(2)}) collective-permute-start(bf16[8,3072]{1,0:T(8,128)(2,1)S(1)} %get-tuple-element.29), channel_id=1, source_target_pairs={{0,4},{1,5},{2,6},{3,7},{4,0},{5,1},{6,2},{7,3},{8,12},{9,13},{10,... | collective-permute-start | bytes 147464 | tf_op jit(solution)/shard_map/ppermute | solution.py:20
  91.2 8.7 %collective-permute-start.31 = (bf16[8,3072]{1,0:T(8,128)(2,1)S(1)}, bf16[8,3072]{1,0:T(8,128)(2,1)S(1)}, u32[]{:S(2)}, u32[]{:S(2)}) collective-permute-start(bf16[8,3072]{1,0:T(8,128)(2,1)S(1)} %get-tuple-element.30), channel_id=1, source_target_pairs={{0,6},{1,7},{2,4},{3,5},{4,2},{5,3},{6,0},{7,1},{8,14},{9,15},{10,... | collective-permute-start | bytes 147464 | tf_op jit(solution)/shard_map/ppermute | solution.py:20
  93.9 6.0 %collective-permute-start.30 = (bf16[8,3072]{1,0:T(8,128)(2,1)S(1)}, bf16[8,3072]{1,0:T(8,128)(2,1)S(1)}, u32[]{:S(2)}, u32[]{:S(2)}) collective-permute-start(bf16[8,3072]{1,0:T(8,128)(2,1)S(1)} %get-tuple-element.31), channel_id=1, source_target_pairs={{0,2},{1,3},{2,0},{3,1},{4,6},{5,7},{6,4},{7,5},{8,10},{9,11},{10,... | collective-permute-start | bytes 147464 | tf_op jit(solution)/shard_map/ppermute | solution.py:20
  96.3 5.2 %collective-permute-start.25 = (bf16[8,4096]{1,0:T(8,128)(2,1)S(1)}, bf16[8,4096]{1,0:T(8,128)(2,1)S(1)}, u32[]{:S(2)}, u32[]{:S(2)}) collective-permute-start(bf16[8,4096]{1,0:T(8,128)(2,1)S(1)} %get-tuple-element.23), channel_id=1, source_target_pairs={{0,4},{1,5},{2,6},{3,7},{4,0},{5,1},{6,2},{7,3},{8,12},{9,13},{10,... | collective-permute-start | bytes 196616 | tf_op jit(solution)/shard_map/ppermute | solution.py:20
  96.4 6.2 %collective-permute-start.27 = (bf16[8,4096]{1,0:T(8,128)(2,1)S(1)}, bf16[8,4096]{1,0:T(8,128)(2,1)S(1)}, u32[]{:S(2)}, u32[]{:S(2)}) collective-permute-start(bf16[8,4096]{1,0:T(8,128)(2,1)S(1)} %get-tuple-element.24), channel_id=1, source_target_pairs={{0,6},{1,7},{2,4},{3,5},{4,2},{5,3},{6,0},{7,1},{8,14},{9,15},{10,... | collective-permute-start | bytes 196616 | tf_op jit(solution)/shard_map/ppermute | solution.py:20
  98.6 4.7 %collective-permute-start.26 = (bf16[8,4096]{1,0:T(8,128)(2,1)S(1)}, bf16[8,4096]{1,0:T(8,128)(2,1)S(1)}, u32[]{:S(2)}, u32[]{:S(2)}) collective-permute-start(bf16[8,4096]{1,0:T(8,128)(2,1)S(1)} %get-tuple-element.25), channel_id=1, source_target_pairs={{0,2},{1,3},{2,0},{3,1},{4,6},{5,7},{6,4},{7,5},{8,10},{9,11},{10,... | collective-permute-start | bytes 196616 | tf_op jit(solution)/shard_map/ppermute | solution.py:20
  (6 other events, 129.8 us)

commit v6 on v5

--- a/solution.py
+++ b/solution.py
@@ -11,7 +11,7 @@
 SUM_SPLIT = ((0, 4096), (4096, None))
 GATHER_SPLIT = ((0, 3072), (3072, None))
 MOE_SPLIT = ((0, 4096), (4096, None))
-HOPS = (2,1,3)
+HOPS = (2, 1, 3)
 LANES = 128
 
 
@@ -61,7 +61,7 @@
     return pltpu.with_memory_space_constraint(x, pltpu.HBM)
 
 
-ATTEND_WINDOW = 4
+ATTEND_WINDOW = 3
 
 
 def attend_kernel(
@@ -221,8 +221,9 @@
 
 
 def hidden_kernel(
-    first, rows_ref, gate_hbm, up_hbm, gate_in, up_in, gate_out, up_out, gate_ref, up_ref, sem
+    first, finish, rows_ref, gate_hbm, up_hbm, gate_in, up_in, *refs
 ):
+    out_refs, (gate_ref, up_ref, sem) = refs[:-3], refs[-3:]
     count = gate_ref.shape[0]
     copies = []
     for i in range(count // STEP):
@@ -233,37 +234,39 @@
                 sem.at[k, i],
             )
             copies.append(copy)
-    ahead = 2 * HIDDEN_WINDOW
-    for copy in copies[:ahead]:
+    for copy in copies:
         copy.start()
+    totals = [gate_in[...], up_in[...]]
     for i in range(count // STEP):
         part = pl.ds(i * STEP, STEP)
-        for k, (weight, before, after) in enumerate(
-            ((gate_ref, gate_in, gate_out), (up_ref, up_in, up_out))
-        ):
+        for k, weight in enumerate((gate_ref, up_ref)):
             copies[2 * i + k].wait()
-            if 2 * i + k + ahead < len(copies):
-                copies[2 * i + k + ahead].start()
-            product = jnp.dot(
+            totals[k] += jnp.dot(
                 rows_ref[:, part], weight[part, :], preferred_element_type=jnp.float32
             )
-            after[...] = product + (before if i == 0 else after)[...]
+    gate, up = totals
+    if finish:
+        out_refs[0][...] = (gate / (1.0 + jnp.exp(-gate)) * up).astype(out_refs[0].dtype)
+    else:
+        out_refs[0][...] = gate
+        out_refs[1][...] = up
 
 
 STEP = 512
-HIDDEN_WINDOW = 16
-
-
-def hidden(rows, gate_weight, up_weight, gate, up, first, count):
+
+
+def hidden(rows, gate_weight, up_weight, gate, up, first, count, finish):
     width = gate_weight.shape[1]
     shape = (rows.shape[0], width)
     vmem = pl.BlockSpec(memory_space=pltpu.VMEM)
     hbm = pl.BlockSpec(memory_space=pl.ANY)
     return pl.pallas_call(
-        functools.partial(hidden_kernel, first),
-        out_shape=[jax.ShapeDtypeStruct(shape, jnp.float32)] * 2,
+        functools.partial(hidden_kernel, first, finish),
+        out_shape=[jax.ShapeDtypeStruct(shape, jnp.bfloat16)]
+        if finish
+        else [jax.ShapeDtypeStruct(shape, jnp.float32)] * 2,
         in_specs=[vmem, hbm, hbm, vmem, vmem],
-        out_specs=[vmem] * 2,
+        out_specs=[vmem] * (1 if finish else 2),
         scratch_shapes=[pltpu.VMEM((count, width), gate_weight.dtype)] * 2
         + [pltpu.SemaphoreType.DMA((2, count // STEP))],
         compiler_params=pltpu.CompilerParams(vmem_limit_bytes=24 * 1024 * 1024),
@@ -365,9 +368,13 @@
     )
 
     gate = up = jnp.zeros((rows[0].shape[0], gate_weight.shape[1]), jnp.float32)
-    for (first, _), piece in zip(GATHER_SPLIT, rows):
-        gate, up = hidden(piece, gate_weight, up_weight, gate, up, first, piece.shape[1])
-    activated = (jax.nn.silu(gate) * up).astype(jnp.bfloat16)
+    for (first, end), piece in zip(GATHER_SPLIT, rows):
+        found = hidden(
+            piece, gate_weight, up_weight, gate, up, first, piece.shape[1], end is None
+        )
+        if end is not None:
+            gate, up = found
+    (activated,) = found
     moe = []
     for first, end in MOE_SPLIT:
         part = (end or width) - first

time: 104 us -> 104 us (level)
  no operation moved by 1% of the time
where the time goes in v6:
time: 104 us; the launch traced here: 103 us
  starting transfers between devices  44.8 us (43%)
  Pallas kernels  34.6 us (33%)
  waiting for transfers between devices  20.8 us (20%)
  other arithmetic  1.89 us (2%)
    ppermute x32, starting transfers between devices, swap(): return lax.ppermute(x, 'dev', [(i, i ^ by) for i in range(size)])  44.8 us
    ppermute x32, waiting for transfers between devices, swap(): return lax.ppermute(x, 'dev', [(i, i ^ by) for i in range(size)])  20.8 us
    pallas_call x4, Pallas kernels, project(): pl.pallas_call(functools.partial(project_kernel, first), out_shape=jax.Sh...  14.5 us
    pallas_call x2, Pallas kernels, hidden(): pl.pallas_call(functools.partial(hidden_kernel, first, finish), out_shape...  11.4 us
    pallas_call x2, Pallas kernels, attend(): pl.pallas_call(functools.partial(attend_kernel, scale, groups, together,...  8.67 us
  transfers between devices with their start and end apart: 32, of which 20 were waited for; matrix products, arithmetic and copies ran while one was open for 1% of the time, Pallas kernels for 15%

profile of v6, /device:TPU:0, one launch (start us, length us, event | category | flops | bytes accessed | tf_op | source)
XLA Modules:
  0.0 103.4 jit_solution(13868303154267659450)
XLA Ops:
  0.0 6.0 %shard_map.118._ = bf16[8,48,512]{2,1,0:T(8,128)(2,1)S(1)} custom-call(s32[1]{0:T(128)} %bitcast.place_ref, s32[8]{0:T(128)} %length_hbm.3, bf16[8,64,576]{2,1,0:T(8,128)(2,1)} %query_hbm.3, bf16[8,576,1024]{2,1,0:T(8,128)(2,1)} %bitcast.122, s32[8]{0:T(128)} %length_hbm.3), custom_call_target="tpu_custom_call" | custom-call | flops 855638016 | bytes 7077888 | tf_op jit(solution)/shard_map/pallas_call | solution.py:141
  6.0 5.1 %collective-permute-start.2 = (bf16[2,48,512]{2,1,0:T(8,128)(2,1)S(1)}, bf16[2,48,512]{2,1,0:T(8,128)(2,1)S(1)}, u32[]{:S(2)}, u32[]{:S(2)}) collective-permute-start(bf16[2,48,512]{2,1,0:T(8,128)(2,1)S(1)} %get-tuple-element.16), channel_id=1, source_target_pairs={{0,6},{1,7},{2,4},{3,5},{4,2},{5,3},{6,0},{7,1},{8,14},{9,15},{10,... | collective-permute-start | bytes 294920 | tf_op jit(solution)/shard_map/ppermute | solution.py:20
  11.8 2.7 %shard_map.119 = bf16[8,16,512]{2,1,0:T(8,128)(2,1)S(1)} custom-call(s32[1]{0:T(128)} %bitcast.place_ref, s32[8]{0:T(128)} %length_hbm.3, bf16[8,64,576]{2,1,0:T(8,128)(2,1)} %query_hbm.3, bf16[8,576,1024]{2,1,0:T(8,128)(2,1)} %bitcast.123, bf16[8,48,512]{2,1,0:T(8,128)(2,1)S(1)} %shard_map.118._), custom_call_target="tpu_custom_call" | custom-call | flops 285212672 | bytes 2359296 | tf_op jit(solution)/shard_map/pallas_call | solution.py:141
  14.9 3.9 %collective-permute-start.6 = (bf16[2,16,512]{2,1,0:T(8,128)(2,1)S(1)}, bf16[2,16,512]{2,1,0:T(8,128)(2,1)S(1)}, u32[]{:S(2)}, u32[]{:S(2)}) collective-permute-start(bf16[2,16,512]{2,1,0:T(8,128)(2,1)S(1)} %get-tuple-element.34), channel_id=1, source_target_pairs={{0,6},{1,7},{2,4},{3,5},{4,2},{5,3},{6,0},{7,1},{8,14},{9,15},{10,... | collective-permute-start | bytes 98312 | tf_op jit(solution)/shard_map/ppermute | solution.py:20
  18.7 1.7 %collective-permute-start.5 = (bf16[2,16,512]{2,1,0:T(8,128)(2,1)S(1)}, bf16[2,16,512]{2,1,0:T(8,128)(2,1)S(1)}, u32[]{:S(2)}, u32[]{:S(2)}) collective-permute-start(bf16[2,16,512]{2,1,0:T(8,128)(2,1)S(1)} %get-tuple-element.35), channel_id=1, source_target_pairs={{0,4},{1,5},{2,6},{3,7},{4,0},{5,1},{6,2},{7,3},{8,12},{9,13},{10,... | collective-permute-start | bytes 98312 | tf_op jit(solution)/shard_map/ppermute | solution.py:20
  21.0 1.6 %collective-permute-start.3 = (bf16[4,48,512]{2,1,0:T(8,128)(2,1)S(1)}, bf16[4,48,512]{2,1,0:T(8,128)(2,1)S(1)}, u32[]{:S(2)}, u32[]{:S(2)}) collective-permute-start(bf16[4,48,512]{2,1,0:T(8,128)(2,1)S(1)} %get-tuple-element.14), channel_id=1, source_target_pairs={{0,1},{1,0},{2,3},{3,2},{4,5},{5,4},{6,7},{7,6},{8,9},{9,8},{10,11... | collective-permute-start | bytes 589832 | tf_op jit(solution)/shard_map/ppermute | solution.py:20
  24.3 1.6 %collective-permute-start.7 = (bf16[4,16,512]{2,1,0:T(8,128)(2,1)S(1)}, bf16[4,16,512]{2,1,0:T(8,128)(2,1)S(1)}, u32[]{:S(2)}, u32[]{:S(2)}) collective-permute-start(bf16[4,16,512]{2,1,0:T(8,128)(2,1)S(1)} %get-tuple-element.32), channel_id=1, source_target_pairs={{0,1},{1,0},{2,3},{3,2},{4,5},{5,4},{6,7},{7,6},{8,9},{9,8},{10,11... | collective-permute-start | bytes 196616 | tf_op jit(solution)/shard_map/ppermute | solution.py:20
  25.9 2.7 %collective-permute-done.7 = bf16[4,16,512]{2,1,0:T(8,128)(2,1)S(1)} collective-permute-done((bf16[4,16,512]{2,1,0:T(8,128)(2,1)S(1)}, bf16[4,16,512]{2,1,0:T(8,128)(2,1)S(1)}, u32[]{:S(2)}, u32[]{:S(2)}) %collective-permute-start.7) | collective-permute-done | bytes 65568 | tf_op jit(solution)/shard_map/ppermute | solution.py:20
  29.3 3.3 %shard_map.121 = bf16[64,3072]{1,0:T(8,128)(2,1)S(1)} custom-call(bf16[64,1024]{1,0:T(8,128)(2,1)S(1)} %bitcast.119, f32[64,1]{1,0:T(8,128)S(1)} %broadcast_in_dim.55.scale_ref, bf16[1024,7168]{1,0:T(8,128)(2,1)} %weight_hbm.5), custom_call_target="tpu_custom_call" | custom-call | flops 402653184 | bytes 6291456 | tf_op jit(solution)/shard_map/pallas_call | solution.py:204
  32.6 1.6 %collective-permute-start.12 = (bf16[4,1,8,3072]{3,2,1,0:T(8,128)(2,1)S(1)}, bf16[4,1,8,3072]{3,2,1,0:T(8,128)(2,1)S(1)}, u32[]{:S(2)}, u32[]{:S(2)}) collective-permute-start(bf16[4,1,8,3072]{3,2,1,0:T(8,128)(2,1)S(1)} %slice.182), channel_id=1, source_target_pairs={{0,1},{1,0},{2,3},{3,2},{4,5},{5,4},{6,7},{7,6},{8,9},{9,8},{10,11... | collective-permute-start | bytes 589832 | tf_op jit(solution)/shard_map/ppermute | solution.py:20
  34.2 4.0 %shard_map.120 = bf16[64,4096]{1,0:T(8,128)(2,1)S(1)} custom-call(bf16[64,1024]{1,0:T(8,128)(2,1)S(1)} %bitcast.120, f32[64,1]{1,0:T(8,128)S(1)} %broadcast_in_dim.55.scale_ref, bf16[1024,7168]{1,0:T(8,128)(2,1)} %weight_hbm.5), custom_call_target="tpu_custom_call" | custom-call | flops 536870912 | bytes 8388608 | tf_op jit(solution)/shard_map/pallas_call | solution.py:204
  38.8 1.0 collective-permute-done.12
  39.9 2.1 %collective-permute-start.13 = (bf16[8,3072]{1,0:T(8,128)(2,1)S(1)}, bf16[8,3072]{1,0:T(8,128)(2,1)S(1)}, u32[]{:S(2)}, u32[]{:S(2)}) collective-permute-start(bf16[8,3072]{1,0:T(8,128)(2,1)S(1)} %get-tuple-element.28), channel_id=1, source_target_pairs={{0,4},{1,5},{2,6},{3,7},{4,0},{5,1},{6,2},{7,3},{8,12},{9,13},{10,... | collective-permute-start | bytes 147464 | tf_op jit(solution)/shard_map/ppermute | solution.py:20
  42.0 2.1 %collective-permute-start.15 = (bf16[8,3072]{1,0:T(8,128)(2,1)S(1)}, bf16[8,3072]{1,0:T(8,128)(2,1)S(1)}, u32[]{:S(2)}, u32[]{:S(2)}) collective-permute-start(bf16[8,3072]{1,0:T(8,128)(2,1)S(1)} %get-tuple-element.29), channel_id=1, source_target_pairs={{0,6},{1,7},{2,4},{3,5},{4,2},{5,3},{6,0},{7,1},{8,14},{9,15},{10,... | collective-permute-start | bytes 147464 | tf_op jit(solution)/shard_map/ppermute | solution.py:20
  44.8 1.8 %collective-permute-start.9 = (bf16[8,4096]{1,0:T(8,128)(2,1)S(1)}, bf16[8,4096]{1,0:T(8,128)(2,1)S(1)}, u32[]{:S(2)}, u32[]{:S(2)}) collective-permute-start(bf16[8,4096]{1,0:T(8,128)(2,1)S(1)} %get-tuple-element.22), channel_id=1, source_target_pairs={{0,4},{1,5},{2,6},{3,7},{4,0},{5,1},{6,2},{7,3},{8,12},{9,13},{10,... | collective-permute-start | bytes 196616 | tf_op jit(solution)/shard_map/ppermute | solution.py:20
  46.6 2.1 %collective-permute-start.11 = (bf16[8,4096]{1,0:T(8,128)(2,1)S(1)}, bf16[8,4096]{1,0:T(8,128)(2,1)S(1)}, u32[]{:S(2)}, u32[]{:S(2)}) collective-permute-start(bf16[8,4096]{1,0:T(8,128)(2,1)S(1)} %get-tuple-element.23), channel_id=1, source_target_pairs={{0,6},{1,7},{2,4},{3,5},{4,2},{5,3},{6,0},{7,1},{8,14},{9,15},{10,... | collective-permute-start | bytes 196616 | tf_op jit(solution)/shard_map/ppermute | solution.py:20
  50.1 2.6 %collective-permute-done.11 = bf16[8,4096]{1,0:T(8,128)(2,1)S(1)} collective-permute-done((bf16[8,4096]{1,0:T(8,128)(2,1)S(1)}, bf16[8,4096]{1,0:T(8,128)(2,1)S(1)}, u32[]{:S(2)}, u32[]{:S(2)}) %collective-permute-start.11) | collective-permute-done | bytes 65568 | tf_op jit(solution)/shard_map/ppermute | solution.py:20
  54.5 2.7 %collective-permute-start.20 = (bf16[8,3072]{1,0:T(8,128)(2,1)S(1)}, bf16[8,3072]{1,0:T(8,128)(2,1)S(1)}, u32[]{:S(2)}, u32[]{:S(2)}) collective-permute-start(bf16[8,3072]{1,0:T(8,128)(2,1)S(1)} %get-tuple-element.38), channel_id=1, source_target_pairs={{0,2},{1,3},{2,0},{3,1},{4,6},{5,7},{6,4},{7,5},{8,10},{9,11},{10,... | collective-permute-start | bytes 147464 | tf_op jit(solution)/shard_map/ppermute | solution.py:20
  57.2 1.0 collective-permute-start.22
  58.7 2.9 %collective-permute-start.16 = (bf16[8,4224]{1,0:T(8,128)(2,1)S(1)}, bf16[8,4224]{1,0:T(8,128)(2,1)S(1)}, u32[]{:S(2)}, u32[]{:S(2)}) collective-permute-start(bf16[8,4224]{1,0:T(8,128)(2,1)S(1)} %get-tuple-element.40), channel_id=1, source_target_pairs={{0,2},{1,3},{2,0},{3,1},{4,6},{5,7},{6,4},{7,5},{8,10},{9,11},{10,... | collective-permute-start | bytes 202760 | tf_op jit(solution)/shard_map/ppermute | solution.py:20
  64.6 3.1 %collective-permute-done.18 = bf16[8,4224]{1,0:T(8,128)(2,1)S(1)} collective-permute-done((bf16[8,4224]{1,0:T(8,128)(2,1)S(1)}, bf16[8,4224]{1,0:T(8,128)(2,1)S(1)}, u32[]{:S(2)}, u32[]{:S(2)}) %collective-permute-start.18) | collective-permute-done | bytes 67616 | tf_op jit(solution)/shard_map/ppermute | solution.py:20
  69.0 5.0 %shard_map.122 = (f32[64,1024]{1,0:T(8,128)S(1)}, f32[64,1024]{1,0:T(8,128)S(1)}) custom-call(bf16[64,3072]{1,0:T(8,128)(2,1)S(1)} %bitcast.114, bf16[7168,1024]{1,0:T(8,128)(2,1)} %gate_hbm.3, bf16[7168,1024]{1,0:T(8,128)(2,1)} %up_hbm.3, f32[64,1024]{1,0:T(8,128)S(1)} %broadcast_in_dim.61.gate_in.up_in, f32[64,1024]{1,0:T(8,128)S(1)} %broadcast_in_dim.61.gate_in.up_in), custom_call_target="tpu_custom_call" | custom-call | flops 805306368 | bytes 12582912 | tf_op jit(solution)/shard_map/pallas_call | solution.py:263
  74.7 6.4 %shard_map.123.rows_ref = bf16[64,1024]{1,0:T(8,128)(2,1)S(1)} custom-call(bf16[64,4096]{1,0:T(8,128)(2,1)S(1)} %slice.188.rows_ref, bf16[7168,1024]{1,0:T(8,128)(2,1)} %gate_hbm.3, bf16[7168,1024]{1,0:T(8,128)(2,1)} %up_hbm.3, f32[64,1024]{1,0:T(8,128)S(1)} %get-tuple-element.9.gate_in, f32[64,1024]{1,0:T(8,128)S(1)} %get-tuple-element.10.up_in), custom_call_target="tpu_custom_call" | custom-call | flops 1073741824 | bytes 16777216 | tf_op jit(solution)/shard_map/pallas_call | solution.py:263
  81.1 3.3 %shard_map.125 = bf16[64,3072]{1,0:T(8,128)(2,1)S(1)} custom-call(bf16[64,1024]{1,0:T(8,128)(2,1)S(1)} %shard_map.123.rows_ref, f32[64,1]{1,0:T(8,128)S(1)} %copy.46.scale_ref, bf16[1024,7168]{1,0:T(8,128)(2,1)} %weight_hbm.7), custom_call_target="tpu_custom_call" | custom-call | flops 402653184 | bytes 6291456 | tf_op jit(solution)/shard_map/pallas_call | solution.py:204
  85.2 4.0 %shard_map.124 = bf16[64,4096]{1,0:T(8,128)(2,1)S(1)} custom-call(bf16[64,1024]{1,0:T(8,128)(2,1)S(1)} %shard_map.123.rows_ref, f32[64,1]{1,0:T(8,128)S(1)} %copy.46.scale_ref, bf16[1024,7168]{1,0:T(8,128)(2,1)} %weight_hbm.7), custom_call_target="tpu_custom_call" | custom-call | flops 536870912 | bytes 8388608 | tf_op jit(solution)/shard_map/pallas_call | solution.py:204
  89.3 1.3 %collective-permute-start.24 = (bf16[4,1,8,4096]{3,2,1,0:T(8,128)(2,1)S(1)}, bf16[4,1,8,4096]{3,2,1,0:T(8,128)(2,1)S(1)}, u32[]{:S(2)}, u32[]{:S(2)}) collective-permute-start(bf16[4,1,8,4096]{3,2,1,0:T(8,128)(2,1)S(1)} %slice.192), channel_id=1, source_target_pairs={{0,1},{1,0},{2,3},{3,2},{4,5},{5,4},{6,7},{7,6},{8,9},{9,8},{10,11... | collective-permute-start | bytes 786440 | tf_op jit(solution)/shard_map/ppermute | solution.py:20
  90.7 2.7 %collective-permute-start.31 = (bf16[8,3072]{1,0:T(8,128)(2,1)S(1)}, bf16[8,3072]{1,0:T(8,128)(2,1)S(1)}, u32[]{:S(2)}, u32[]{:S(2)}) collective-permute-start(bf16[8,3072]{1,0:T(8,128)(2,1)S(1)} %get-tuple-element.26), channel_id=1, source_target_pairs={{0,6},{1,7},{2,4},{3,5},{4,2},{5,3},{6,0},{7,1},{8,14},{9,15},{10,... | collective-permute-start | bytes 147464 | tf_op jit(solution)/shard_map/ppermute | solution.py:20
  94.2 1.5 %collective-permute-done.24 = bf16[4,1,8,4096]{3,2,1,0:T(8,128)(2,1)S(1)} collective-permute-done((bf16[4,1,8,4096]{3,2,1,0:T(8,128)(2,1)S(1)}, bf16[4,1,8,4096]{3,2,1,0:T(8,128)(2,1)S(1)}, u32[]{:S(2)}, u32[]{:S(2)}) %collective-permute-start.24) | collective-permute-done | bytes 262176 | tf_op jit(solution)/shard_map/ppermute | solution.py:20
  95.9 2.2 %collective-permute-start.27 = (bf16[8,4096]{1,0:T(8,128)(2,1)S(1)}, bf16[8,4096]{1,0:T(8,128)(2,1)S(1)}, u32[]{:S(2)}, u32[]{:S(2)}) collective-permute-start(bf16[8,4096]{1,0:T(8,128)(2,1)S(1)} %get-tuple-element.20), channel_id=1, source_target_pairs={{0,6},{1,7},{2,4},{3,5},{4,2},{5,3},{6,0},{7,1},{8,14},{9,15},{10,... | collective-permute-start | bytes 196616 | tf_op jit(solution)/shard_map/ppermute | solution.py:20
  98.0 1.3 %collective-permute-start.26 = (bf16[8,4096]{1,0:T(8,128)(2,1)S(1)}, bf16[8,4096]{1,0:T(8,128)(2,1)S(1)}, u32[]{:S(2)}, u32[]{:S(2)}) collective-permute-start(bf16[8,4096]{1,0:T(8,128)(2,1)S(1)} %get-tuple-element.21), channel_id=1, source_target_pairs={{0,2},{1,3},{2,0},{3,1},{4,6},{5,7},{6,4},{7,5},{8,10},{9,11},{10,... | collective-permute-start | bytes 196616 | tf_op jit(solution)/shard_map/ppermute | solution.py:20
  99.4 1.6 %collective-permute-done.25 = bf16[8,4096]{1,0:T(8,128)(2,1)S(1)} collective-permute-done((bf16[8,4096]{1,0:T(8,128)(2,1)S(1)}, bf16[8,4096]{1,0:T(8,128)(2,1)S(1)}, u32[]{:S(2)}, u32[]{:S(2)}) %collective-permute-start.25) | collective-permute-done | bytes 65568 | tf_op jit(solution)/shard_map/ppermute | solution.py:20
  101.0 1.0 collective-permute-done.27
  (105 shorter events, 17.3 us)
Async XLA Ops:
  6.0 8.8 %collective-permute-start.2 = (bf16[2,48,512]{2,1,0:T(8,128)(2,1)S(1)}, bf16[2,48,512]{2,1,0:T(8,128)(2,1)S(1)}, u32[]{:S(2)}, u32[]{:S(2)}) collective-permute-start(bf16[2,48,512]{2,1,0:T(8,128)(2,1)S(1)} %get-tuple-element.16), channel_id=1, source_target_pairs={{0,6},{1,7},{2,4},{3,5},{4,2},{5,3},{6,0},{7,1},{8,14},{9,15},{10,... | collective-permute-start | bytes 294920 | tf_op jit(solution)/shard_map/ppermute | solution.py:20
  11.1 9.8 %collective-permute-start.1 = (bf16[2,48,512]{2,1,0:T(8,128)(2,1)S(1)}, bf16[2,48,512]{2,1,0:T(8,128)(2,1)S(1)}, u32[]{:S(2)}, u32[]{:S(2)}) collective-permute-start(bf16[2,48,512]{2,1,0:T(8,128)(2,1)S(1)} %get-tuple-element.17), channel_id=1, source_target_pairs={{0,4},{1,5},{2,6},{3,7},{4,0},{5,1},{6,2},{7,3},{8,12},{9,13},{10,... | collective-permute-start | bytes 294920 | tf_op jit(solution)/shard_map/ppermute | solution.py:20
  11.1 9.8 %collective-permute-start = (bf16[2,48,512]{2,1,0:T(8,128)(2,1)S(1)}, bf16[2,48,512]{2,1,0:T(8,128)(2,1)S(1)}, u32[]{:S(2)}, u32[]{:S(2)}) collective-permute-start(bf16[2,48,512]{2,1,0:T(8,128)(2,1)S(1)} %get-tuple-element.18), channel_id=1, source_target_pairs={{0,2},{1,3},{2,0},{3,1},{4,6},{5,7},{6,4},{7,5},{8,10},{9,11},{10,... | collective-permute-start | bytes 294920 | tf_op jit(solution)/shard_map/ppermute | solution.py:20
  14.9 7.8 %collective-permute-start.6 = (bf16[2,16,512]{2,1,0:T(8,128)(2,1)S(1)}, bf16[2,16,512]{2,1,0:T(8,128)(2,1)S(1)}, u32[]{:S(2)}, u32[]{:S(2)}) collective-permute-start(bf16[2,16,512]{2,1,0:T(8,128)(2,1)S(1)} %get-tuple-element.34), channel_id=1, source_target_pairs={{0,6},{1,7},{2,4},{3,5},{4,2},{5,3},{6,0},{7,1},{8,14},{9,15},{10,... | collective-permute-start | bytes 98312 | tf_op jit(solution)/shard_map/ppermute | solution.py:20
  18.7 4.8 %collective-permute-start.5 = (bf16[2,16,512]{2,1,0:T(8,128)(2,1)S(1)}, bf16[2,16,512]{2,1,0:T(8,128)(2,1)S(1)}, u32[]{:S(2)}, u32[]{:S(2)}) collective-permute-start(bf16[2,16,512]{2,1,0:T(8,128)(2,1)S(1)} %get-tuple-element.35), channel_id=1, source_target_pairs={{0,4},{1,5},{2,6},{3,7},{4,0},{5,1},{6,2},{7,3},{8,12},{9,13},{10,... | collective-permute-start | bytes 98312 | tf_op jit(solution)/shard_map/ppermute | solution.py:20
  20.4 3.9 %collective-permute-start.4 = (bf16[2,16,512]{2,1,0:T(8,128)(2,1)S(1)}, bf16[2,16,512]{2,1,0:T(8,128)(2,1)S(1)}, u32[]{:S(2)}, u32[]{:S(2)}) collective-permute-start(bf16[2,16,512]{2,1,0:T(8,128)(2,1)S(1)} %get-tuple-element.36), channel_id=1, source_target_pairs={{0,2},{1,3},{2,0},{3,1},{4,6},{5,7},{6,4},{7,5},{8,10},{9,11},{10,... | collective-permute-start | bytes 98312 | tf_op jit(solution)/shard_map/ppermute | solution.py:20
  21.0 7.6 %collective-permute-start.3 = (bf16[4,48,512]{2,1,0:T(8,128)(2,1)S(1)}, bf16[4,48,512]{2,1,0:T(8,128)(2,1)S(1)}, u32[]{:S(2)}, u32[]{:S(2)}) collective-permute-start(bf16[4,48,512]{2,1,0:T(8,128)(2,1)S(1)} %get-tuple-element.14), channel_id=1, source_target_pairs={{0,1},{1,0},{2,3},{3,2},{4,5},{5,4},{6,7},{7,6},{8,9},{9,8},{10,11... | collective-permute-start | bytes 589832 | tf_op jit(solution)/shard_map/ppermute | solution.py:20
  24.3 4.3 %collective-permute-start.7 = (bf16[4,16,512]{2,1,0:T(8,128)(2,1)S(1)}, bf16[4,16,512]{2,1,0:T(8,128)(2,1)S(1)}, u32[]{:S(2)}, u32[]{:S(2)}) collective-permute-start(bf16[4,16,512]{2,1,0:T(8,128)(2,1)S(1)} %get-tuple-element.32), channel_id=1, source_target_pairs={{0,1},{1,0},{2,3},{3,2},{4,5},{5,4},{6,7},{7,6},{8,9},{9,8},{10,11... | collective-permute-start | bytes 196616 | tf_op jit(solution)/shard_map/ppermute | solution.py:20
  32.6 7.2 %collective-permute-start.12 = (bf16[4,1,8,3072]{3,2,1,0:T(8,128)(2,1)S(1)}, bf16[4,1,8,3072]{3,2,1,0:T(8,128)(2,1)S(1)}, u32[]{:S(2)}, u32[]{:S(2)}) collective-permute-start(bf16[4,1,8,3072]{3,2,1,0:T(8,128)(2,1)S(1)} %slice.182), channel_id=1, source_target_pairs={{0,1},{1,0},{2,3},{3,2},{4,5},{5,4},{6,7},{7,6},{8,9},{9,8},{10,11... | collective-permute-start | bytes 589832 | tf_op jit(solution)/shard_map/ppermute | solution.py:20
  38.2 6.4 %collective-permute-start.8 = (bf16[4,1,8,4096]{3,2,1,0:T(8,128)(2,1)S(1)}, bf16[4,1,8,4096]{3,2,1,0:T(8,128)(2,1)S(1)}, u32[]{:S(2)}, u32[]{:S(2)}) collective-permute-start(bf16[4,1,8,4096]{3,2,1,0:T(8,128)(2,1)S(1)} %slice.176), channel_id=1, source_target_pairs={{0,1},{1,0},{2,3},{3,2},{4,5},{5,4},{6,7},{7,6},{8,9},{9,8},{10,11... | collective-permute-start | bytes 786440 | tf_op jit(solution)/shard_map/ppermute | solution.py:20
  39.9 8.7 %collective-permute-start.13 = (bf16[8,3072]{1,0:T(8,128)(2,1)S(1)}, bf16[8,3072]{1,0:T(8,128)(2,1)S(1)}, u32[]{:S(2)}, u32[]{:S(2)}) collective-permute-start(bf16[8,3072]{1,0:T(8,128)(2,1)S(1)} %get-tuple-element.28), channel_id=1, source_target_pairs={{0,4},{1,5},{2,6},{3,7},{4,0},{5,1},{6,2},{7,3},{8,12},{9,13},{10,... | collective-permute-start | bytes 147464 | tf_op jit(solution)/shard_map/ppermute | solution.py:20
  42.0 6.6 %collective-permute-start.15 = (bf16[8,3072]{1,0:T(8,128)(2,1)S(1)}, bf16[8,3072]{1,0:T(8,128)(2,1)S(1)}, u32[]{:S(2)}, u32[]{:S(2)}) collective-permute-start(bf16[8,3072]{1,0:T(8,128)(2,1)S(1)} %get-tuple-element.29), channel_id=1, source_target_pairs={{0,6},{1,7},{2,4},{3,5},{4,2},{5,3},{6,0},{7,1},{8,14},{9,15},{10,... | collective-permute-start | bytes 147464 | tf_op jit(solution)/shard_map/ppermute | solution.py:20
  44.1 5.2 %collective-permute-start.14 = (bf16[8,3072]{1,0:T(8,128)(2,1)S(1)}, bf16[8,3072]{1,0:T(8,128)(2,1)S(1)}, u32[]{:S(2)}, u32[]{:S(2)}) collective-permute-start(bf16[8,3072]{1,0:T(8,128)(2,1)S(1)} %get-tuple-element.30), channel_id=1, source_target_pairs={{0,2},{1,3},{2,0},{3,1},{4,6},{5,7},{6,4},{7,5},{8,10},{9,11},{10,... | collective-permute-start | bytes 147464 | tf_op jit(solution)/shard_map/ppermute | solution.py:20
  44.8 5.3 %collective-permute-start.9 = (bf16[8,4096]{1,0:T(8,128)(2,1)S(1)}, bf16[8,4096]{1,0:T(8,128)(2,1)S(1)}, u32[]{:S(2)}, u32[]{:S(2)}) collective-permute-start(bf16[8,4096]{1,0:T(8,128)(2,1)S(1)} %get-tuple-element.22), channel_id=1, source_target_pairs={{0,4},{1,5},{2,6},{3,7},{4,0},{5,1},{6,2},{7,3},{8,12},{9,13},{10,... | collective-permute-start | bytes 196616 | tf_op jit(solution)/shard_map/ppermute | solution.py:20
  46.6 6.1 %collective-permute-start.11 = (bf16[8,4096]{1,0:T(8,128)(2,1)S(1)}, bf16[8,4096]{1,0:T(8,128)(2,1)S(1)}, u32[]{:S(2)}, u32[]{:S(2)}) collective-permute-start(bf16[8,4096]{1,0:T(8,128)(2,1)S(1)} %get-tuple-element.23), channel_id=1, source_target_pairs={{0,6},{1,7},{2,4},{3,5},{4,2},{5,3},{6,0},{7,1},{8,14},{9,15},{10,... | collective-permute-start | bytes 196616 | tf_op jit(solution)/shard_map/ppermute | solution.py:20
  48.6 4.7 %collective-permute-start.10 = (bf16[8,4096]{1,0:T(8,128)(2,1)S(1)}, bf16[8,4096]{1,0:T(8,128)(2,1)S(1)}, u32[]{:S(2)}, u32[]{:S(2)}) collective-permute-start(bf16[8,4096]{1,0:T(8,128)(2,1)S(1)} %get-tuple-element.24), channel_id=1, source_target_pairs={{0,2},{1,3},{2,0},{3,1},{4,6},{5,7},{6,4},{7,5},{8,10},{9,11},{10,... | collective-permute-start | bytes 196616 | tf_op jit(solution)/shard_map/ppermute | solution.py:20
  53.7 7.9 %collective-permute-start.21 = (bf16[8,3072]{1,0:T(8,128)(2,1)S(1)}, bf16[8,3072]{1,0:T(8,128)(2,1)S(1)}, u32[]{:S(2)}, u32[]{:S(2)}) collective-permute-start(bf16[8,3072]{1,0:T(8,128)(2,1)S(1)} %get-tuple-element.38), channel_id=1, source_target_pairs={{0,4},{1,5},{2,6},{3,7},{4,0},{5,1},{6,2},{7,3},{8,12},{9,13},{10,... | collective-permute-start | bytes 147464 | tf_op jit(solution)/shard_map/ppermute | solution.py:20
  54.5 8.1 %collective-permute-start.20 = (bf16[8,3072]{1,0:T(8,128)(2,1)S(1)}, bf16[8,3072]{1,0:T(8,128)(2,1)S(1)}, u32[]{:S(2)}, u32[]{:S(2)}) collective-permute-start(bf16[8,3072]{1,0:T(8,128)(2,1)S(1)} %get-tuple-element.38), channel_id=1, source_target_pairs={{0,2},{1,3},{2,0},{3,1},{4,6},{5,7},{6,4},{7,5},{8,10},{9,11},{10,... | collective-permute-start | bytes 147464 | tf_op jit(solution)/shard_map/ppermute | solution.py:20
  57.2 5.9 %collective-permute-start.22 = (bf16[8,3072]{1,0:T(8,128)(2,1)S(1)}, bf16[8,3072]{1,0:T(8,128)(2,1)S(1)}, u32[]{:S(2)}, u32[]{:S(2)}) collective-permute-start(bf16[8,3072]{1,0:T(8,128)(2,1)S(1)} %get-tuple-element.38), channel_id=1, source_target_pairs={{0,6},{1,7},{2,4},{3,5},{4,2},{5,3},{6,0},{7,1},{8,14},{9,15},{10,... | collective-permute-start | bytes 147464 | tf_op jit(solution)/shard_map/ppermute | solution.py:20
  58.2 6.4 %collective-permute-start.17 = (bf16[8,4224]{1,0:T(8,128)(2,1)S(1)}, bf16[8,4224]{1,0:T(8,128)(2,1)S(1)}, u32[]{:S(2)}, u32[]{:S(2)}) collective-permute-start(bf16[8,4224]{1,0:T(8,128)(2,1)S(1)} %get-tuple-element.40), channel_id=1, source_target_pairs={{0,4},{1,5},{2,6},{3,7},{4,0},{5,1},{6,2},{7,3},{8,12},{9,13},{10,... | collective-permute-start | bytes 202760 | tf_op jit(solution)/shard_map/ppermute | solution.py:20
  58.7 5.9 %collective-permute-start.16 = (bf16[8,4224]{1,0:T(8,128)(2,1)S(1)}, bf16[8,4224]{1,0:T(8,128)(2,1)S(1)}, u32[]{:S(2)}, u32[]{:S(2)}) collective-permute-start(bf16[8,4224]{1,0:T(8,128)(2,1)S(1)} %get-tuple-element.40), channel_id=1, source_target_pairs={{0,2},{1,3},{2,0},{3,1},{4,6},{5,7},{6,4},{7,5},{8,10},{9,11},{10,... | collective-permute-start | bytes 202760 | tf_op jit(solution)/shard_map/ppermute | solution.py:20
  61.6 6.1 %collective-permute-start.18 = (bf16[8,4224]{1,0:T(8,128)(2,1)S(1)}, bf16[8,4224]{1,0:T(8,128)(2,1)S(1)}, u32[]{:S(2)}, u32[]{:S(2)}) collective-permute-start(bf16[8,4224]{1,0:T(8,128)(2,1)S(1)} %get-tuple-element.40), channel_id=1, source_target_pairs={{0,6},{1,7},{2,4},{3,5},{4,2},{5,3},{6,0},{7,1},{8,14},{9,15},{10,... | collective-permute-start | bytes 202760 | tf_op jit(solution)/shard_map/ppermute | solution.py:20
  63.1 5.7 %collective-permute-start.23 = (bf16[4,1,8,3072]{3,2,0,1:T(8,128)(2,1)S(1)}, bf16[4,1,8,3072]{3,2,0,1:T(8,128)(2,1)S(1)}, u32[]{:S(2)}, u32[]{:S(2)}) collective-permute-start(bf16[4,1,8,3072]{3,2,0,1:T(8,128)(2,1)S(1)} %maximum_bitcast_fusion.1), channel_id=1, source_target_pairs={{0,1},{1,0},{2,3},{3,2},{4,5},{5,4},{6,7},{7,6},{8,9},{9,8},{10,11... | collective-permute-start | bytes 589832 | tf_op jit(solution)/shard_map/ppermute | solution.py:20
  67.8 6.5 %collective-permute-start.19 = (bf16[4,1,8,4224]{3,2,0,1:T(8,128)(2,1)S(1)}, bf16[4,1,8,4224]{3,2,0,1:T(8,128)(2,1)S(1)}, u32[]{:S(2)}, u32[]{:S(2)}) collective-permute-start(bf16[4,1,8,4224]{3,2,0,1:T(8,128)(2,1)S(1)} %maximum_bitcast_fusion), channel_id=1, source_target_pairs={{0,1},{1,0},{2,3},{3,2},{4,5},{5,4},{6,7},{7,6},{8,9},{9,8},{10,11... | collective-permute-start | bytes 811016 | tf_op jit(solution)/shard_map/ppermute | solution.py:20
  84.4 6.2 %collective-permute-start.28 = (bf16[4,1,8,3072]{3,2,1,0:T(8,128)(2,1)S(1)}, bf16[4,1,8,3072]{3,2,1,0:T(8,128)(2,1)S(1)}, u32[]{:S(2)}, u32[]{:S(2)}) collective-permute-start(bf16[4,1,8,3072]{3,2,1,0:T(8,128)(2,1)S(1)} %slice.198), channel_id=1, source_target_pairs={{0,1},{1,0},{2,3},{3,2},{4,5},{5,4},{6,7},{7,6},{8,9},{9,8},{10,11... | collective-permute-start | bytes 589832 | tf_op jit(solution)/shard_map/ppermute | solution.py:20
  89.3 6.4 %collective-permute-start.24 = (bf16[4,1,8,4096]{3,2,1,0:T(8,128)(2,1)S(1)}, bf16[4,1,8,4096]{3,2,1,0:T(8,128)(2,1)S(1)}, u32[]{:S(2)}, u32[]{:S(2)}) collective-permute-start(bf16[4,1,8,4096]{3,2,1,0:T(8,128)(2,1)S(1)} %slice.192), channel_id=1, source_target_pairs={{0,1},{1,0},{2,3},{3,2},{4,5},{5,4},{6,7},{7,6},{8,9},{9,8},{10,11... | collective-permute-start | bytes 786440 | tf_op jit(solution)/shard_map/ppermute | solution.py:20
  90.6 7.4 %collective-permute-start.29 = (bf16[8,3072]{1,0:T(8,128)(2,1)S(1)}, bf16[8,3072]{1,0:T(8,128)(2,1)S(1)}, u32[]{:S(2)}, u32[]{:S(2)}) collective-permute-start(bf16[8,3072]{1,0:T(8,128)(2,1)S(1)} %get-tuple-element.25), channel_id=1, source_target_pairs={{0,4},{1,5},{2,6},{3,7},{4,0},{5,1},{6,2},{7,3},{8,12},{9,13},{10,... | collective-permute-start | bytes 147464 | tf_op jit(solution)/shard_map/ppermute | solution.py:20
  90.7 8.7 %collective-permute-start.31 = (bf16[8,3072]{1,0:T(8,128)(2,1)S(1)}, bf16[8,3072]{1,0:T(8,128)(2,1)S(1)}, u32[]{:S(2)}, u32[]{:S(2)}) collective-permute-start(bf16[8,3072]{1,0:T(8,128)(2,1)S(1)} %get-tuple-element.26), channel_id=1, source_target_pairs={{0,6},{1,7},{2,4},{3,5},{4,2},{5,3},{6,0},{7,1},{8,14},{9,15},{10,... | collective-permute-start | bytes 147464 | tf_op jit(solution)/shard_map/ppermute | solution.py:20
  93.4 6.0 %collective-permute-start.30 = (bf16[8,3072]{1,0:T(8,128)(2,1)S(1)}, bf16[8,3072]{1,0:T(8,128)(2,1)S(1)}, u32[]{:S(2)}, u32[]{:S(2)}) collective-permute-start(bf16[8,3072]{1,0:T(8,128)(2,1)S(1)} %get-tuple-element.27), channel_id=1, source_target_pairs={{0,2},{1,3},{2,0},{3,1},{4,6},{5,7},{6,4},{7,5},{8,10},{9,11},{10,... | collective-permute-start | bytes 147464 | tf_op jit(solution)/shard_map/ppermute | solution.py:20
  95.8 5.2 %collective-permute-start.25 = (bf16[8,4096]{1,0:T(8,128)(2,1)S(1)}, bf16[8,4096]{1,0:T(8,128)(2,1)S(1)}, u32[]{:S(2)}, u32[]{:S(2)}) collective-permute-start(bf16[8,4096]{1,0:T(8,128)(2,1)S(1)} %get-tuple-element.19), channel_id=1, source_target_pairs={{0,4},{1,5},{2,6},{3,7},{4,0},{5,1},{6,2},{7,3},{8,12},{9,13},{10,... | collective-permute-start | bytes 196616 | tf_op jit(solution)/shard_map/ppermute | solution.py:20
  95.9 6.2 %collective-permute-start.27 = (bf16[8,4096]{1,0:T(8,128)(2,1)S(1)}, bf16[8,4096]{1,0:T(8,128)(2,1)S(1)}, u32[]{:S(2)}, u32[]{:S(2)}) collective-permute-start(bf16[8,4096]{1,0:T(8,128)(2,1)S(1)} %get-tuple-element.20), channel_id=1, source_target_pairs={{0,6},{1,7},{2,4},{3,5},{4,2},{5,3},{6,0},{7,1},{8,14},{9,15},{10,... | collective-permute-start | bytes 196616 | tf_op jit(solution)/shard_map/ppermute | solution.py:20
  98.0 4.7 %collective-permute-start.26 = (bf16[8,4096]{1,0:T(8,128)(2,1)S(1)}, bf16[8,4096]{1,0:T(8,128)(2,1)S(1)}, u32[]{:S(2)}, u32[]{:S(2)}) collective-permute-start(bf16[8,4096]{1,0:T(8,128)(2,1)S(1)} %get-tuple-element.21), channel_id=1, source_target_pairs={{0,2},{1,3},{2,0},{3,1},{4,6},{5,7},{6,4},{7,5},{8,10},{9,11},{10,... | collective-permute-start | bytes 196616 | tf_op jit(solution)/shard_map/ppermute | solution.py:20
  (6 other events, 135.0 us)

commit v7 on v6

--- a/solution.py
+++ b/solution.py
@@ -355,11 +355,11 @@
     rows = []
     for first, end in GATHER_SPLIT:
         piece = normed[:, first:end]
-        if end is None:
+        if first == 0:
             piece = jnp.concatenate([piece, mix_row], axis=1)
         rows.append(gather_rows(piece, slabs).reshape(group_size * token_count, -1))
-    mix_rows = rows[-1][:, -LANES:].astype(jnp.float32)
-    rows[-1] = rows[-1][:, :-LANES]
+    mix_rows = rows[0][:, -LANES:].astype(jnp.float32)
+    rows[0] = rows[0][:, :-LANES]
     mine = me // slabs
     mix_mine = jnp.sum(
         jnp.where((lane[0] < 2 * EXPERTS) & (lane[0] % EXPERTS == mine), mix_rows, 0.0),

time: 104 us -> 104 us (level)
  transfers between devices with their start and end apart: 32 -> 32, of which waited for: 20 -> 19; matrix products, arithmetic and copies ran while one was open for 1% -> 1% of each run, Pallas kernels for 15% -> 15%
where the time goes in v7:
time: 104 us; the launch traced here: 103 us
  starting transfers between devices  44.9 us (43%)
  Pallas kernels  34.7 us (33%)
  waiting for transfers between devices  20.6 us (20%)
  other arithmetic  1.89 us (2%)
    ppermute x32, starting transfers between devices, swap(): return lax.ppermute(x, 'dev', [(i, i ^ by) for i in range(size)])  44.9 us
    ppermute x32, waiting for transfers between devices, swap(): return lax.ppermute(x, 'dev', [(i, i ^ by) for i in range(size)])  20.6 us
    pallas_call x4, Pallas kernels, project(): pl.pallas_call(functools.partial(project_kernel, first), out_shape=jax.Sh...  14.5 us
    pallas_call x2, Pallas kernels, hidden(): pl.pallas_call(functools.partial(hidden_kernel, first, finish), out_shape...  11.5 us
    pallas_call x2, Pallas kernels, attend(): pl.pallas_call(functools.partial(attend_kernel, scale, groups, together,...  8.67 us
  transfers between devices with their start and end apart: 32, of which 19 were waited for; matrix products, arithmetic and copies ran while one was open for 1% of the time, Pallas kernels for 15%

profile of v7, /device:TPU:0, one launch (start us, length us, event | category | flops | bytes accessed | tf_op | source)
XLA Modules:
  0.0 103.4 jit_solution(6323647017006385891)
XLA Ops:
  0.0 6.0 %shard_map.118._ = bf16[8,48,512]{2,1,0:T(8,128)(2,1)S(1)} custom-call(s32[1]{0:T(128)} %bitcast.place_ref, s32[8]{0:T(128)} %length_hbm.3, bf16[8,64,576]{2,1,0:T(8,128)(2,1)} %query_hbm.3, bf16[8,576,1024]{2,1,0:T(8,128)(2,1)} %bitcast.122, s32[8]{0:T(128)} %length_hbm.3), custom_call_target="tpu_custom_call" | custom-call | flops 855638016 | bytes 7077888 | tf_op jit(solution)/shard_map/pallas_call | solution.py:141
  6.0 5.1 %collective-permute-start.2 = (bf16[2,48,512]{2,1,0:T(8,128)(2,1)S(1)}, bf16[2,48,512]{2,1,0:T(8,128)(2,1)S(1)}, u32[]{:S(2)}, u32[]{:S(2)}) collective-permute-start(bf16[2,48,512]{2,1,0:T(8,128)(2,1)S(1)} %get-tuple-element.16), channel_id=1, source_target_pairs={{0,6},{1,7},{2,4},{3,5},{4,2},{5,3},{6,0},{7,1},{8,14},{9,15},{10,... | collective-permute-start | bytes 294920 | tf_op jit(solution)/shard_map/ppermute | solution.py:20
  11.8 2.7 %shard_map.119 = bf16[8,16,512]{2,1,0:T(8,128)(2,1)S(1)} custom-call(s32[1]{0:T(128)} %bitcast.place_ref, s32[8]{0:T(128)} %length_hbm.3, bf16[8,64,576]{2,1,0:T(8,128)(2,1)} %query_hbm.3, bf16[8,576,1024]{2,1,0:T(8,128)(2,1)} %bitcast.123, bf16[8,48,512]{2,1,0:T(8,128)(2,1)S(1)} %shard_map.118._), custom_call_target="tpu_custom_call" | custom-call | flops 285212672 | bytes 2359296 | tf_op jit(solution)/shard_map/pallas_call | solution.py:141
  14.9 3.9 %collective-permute-start.6 = (bf16[2,16,512]{2,1,0:T(8,128)(2,1)S(1)}, bf16[2,16,512]{2,1,0:T(8,128)(2,1)S(1)}, u32[]{:S(2)}, u32[]{:S(2)}) collective-permute-start(bf16[2,16,512]{2,1,0:T(8,128)(2,1)S(1)} %get-tuple-element.34), channel_id=1, source_target_pairs={{0,6},{1,7},{2,4},{3,5},{4,2},{5,3},{6,0},{7,1},{8,14},{9,15},{10,... | collective-permute-start | bytes 98312 | tf_op jit(solution)/shard_map/ppermute | solution.py:20
  18.7 1.7 %collective-permute-start.5 = (bf16[2,16,512]{2,1,0:T(8,128)(2,1)S(1)}, bf16[2,16,512]{2,1,0:T(8,128)(2,1)S(1)}, u32[]{:S(2)}, u32[]{:S(2)}) collective-permute-start(bf16[2,16,512]{2,1,0:T(8,128)(2,1)S(1)} %get-tuple-element.35), channel_id=1, source_target_pairs={{0,4},{1,5},{2,6},{3,7},{4,0},{5,1},{6,2},{7,3},{8,12},{9,13},{10,... | collective-permute-start | bytes 98312 | tf_op jit(solution)/shard_map/ppermute | solution.py:20
  21.0 1.6 %collective-permute-start.3 = (bf16[4,48,512]{2,1,0:T(8,128)(2,1)S(1)}, bf16[4,48,512]{2,1,0:T(8,128)(2,1)S(1)}, u32[]{:S(2)}, u32[]{:S(2)}) collective-permute-start(bf16[4,48,512]{2,1,0:T(8,128)(2,1)S(1)} %get-tuple-element.14), channel_id=1, source_target_pairs={{0,1},{1,0},{2,3},{3,2},{4,5},{5,4},{6,7},{7,6},{8,9},{9,8},{10,11... | collective-permute-start | bytes 589832 | tf_op jit(solution)/shard_map/ppermute | solution.py:20
  24.3 1.6 %collective-permute-start.7 = (bf16[4,16,512]{2,1,0:T(8,128)(2,1)S(1)}, bf16[4,16,512]{2,1,0:T(8,128)(2,1)S(1)}, u32[]{:S(2)}, u32[]{:S(2)}) collective-permute-start(bf16[4,16,512]{2,1,0:T(8,128)(2,1)S(1)} %get-tuple-element.32), channel_id=1, source_target_pairs={{0,1},{1,0},{2,3},{3,2},{4,5},{5,4},{6,7},{7,6},{8,9},{9,8},{10,11... | collective-permute-start | bytes 196616 | tf_op jit(solution)/shard_map/ppermute | solution.py:20
  25.9 2.7 %collective-permute-done.7 = bf16[4,16,512]{2,1,0:T(8,128)(2,1)S(1)} collective-permute-done((bf16[4,16,512]{2,1,0:T(8,128)(2,1)S(1)}, bf16[4,16,512]{2,1,0:T(8,128)(2,1)S(1)}, u32[]{:S(2)}, u32[]{:S(2)}) %collective-permute-start.7) | collective-permute-done | bytes 65568 | tf_op jit(solution)/shard_map/ppermute | solution.py:20
  29.3 3.3 %shard_map.121 = bf16[64,3072]{1,0:T(8,128)(2,1)S(1)} custom-call(bf16[64,1024]{1,0:T(8,128)(2,1)S(1)} %bitcast.119, f32[64,1]{1,0:T(8,128)S(1)} %broadcast_in_dim.55.scale_ref, bf16[1024,7168]{1,0:T(8,128)(2,1)} %weight_hbm.5), custom_call_target="tpu_custom_call" | custom-call | flops 402653184 | bytes 6291456 | tf_op jit(solution)/shard_map/pallas_call | solution.py:204
  32.6 1.6 %collective-permute-start.12 = (bf16[4,1,8,3072]{3,2,1,0:T(8,128)(2,1)S(1)}, bf16[4,1,8,3072]{3,2,1,0:T(8,128)(2,1)S(1)}, u32[]{:S(2)}, u32[]{:S(2)}) collective-permute-start(bf16[4,1,8,3072]{3,2,1,0:T(8,128)(2,1)S(1)} %slice.182), channel_id=1, source_target_pairs={{0,1},{1,0},{2,3},{3,2},{4,5},{5,4},{6,7},{7,6},{8,9},{9,8},{10,11... | collective-permute-start | bytes 589832 | tf_op jit(solution)/shard_map/ppermute | solution.py:20
  34.2 4.0 %shard_map.120 = bf16[64,4096]{1,0:T(8,128)(2,1)S(1)} custom-call(bf16[64,1024]{1,0:T(8,128)(2,1)S(1)} %bitcast.120, f32[64,1]{1,0:T(8,128)S(1)} %broadcast_in_dim.55.scale_ref, bf16[1024,7168]{1,0:T(8,128)(2,1)} %weight_hbm.5), custom_call_target="tpu_custom_call" | custom-call | flops 536870912 | bytes 8388608 | tf_op jit(solution)/shard_map/pallas_call | solution.py:204
  38.8 1.0 collective-permute-done.12
  39.9 2.1 %collective-permute-start.13 = (bf16[8,3072]{1,0:T(8,128)(2,1)S(1)}, bf16[8,3072]{1,0:T(8,128)(2,1)S(1)}, u32[]{:S(2)}, u32[]{:S(2)}) collective-permute-start(bf16[8,3072]{1,0:T(8,128)(2,1)S(1)} %get-tuple-element.28), channel_id=1, source_target_pairs={{0,4},{1,5},{2,6},{3,7},{4,0},{5,1},{6,2},{7,3},{8,12},{9,13},{10,... | collective-permute-start | bytes 147464 | tf_op jit(solution)/shard_map/ppermute | solution.py:20
  42.0 2.1 %collective-permute-start.15 = (bf16[8,3072]{1,0:T(8,128)(2,1)S(1)}, bf16[8,3072]{1,0:T(8,128)(2,1)S(1)}, u32[]{:S(2)}, u32[]{:S(2)}) collective-permute-start(bf16[8,3072]{1,0:T(8,128)(2,1)S(1)} %get-tuple-element.29), channel_id=1, source_target_pairs={{0,6},{1,7},{2,4},{3,5},{4,2},{5,3},{6,0},{7,1},{8,14},{9,15},{10,... | collective-permute-start | bytes 147464 | tf_op jit(solution)/shard_map/ppermute | solution.py:20
  44.8 1.8 %collective-permute-start.9 = (bf16[8,4096]{1,0:T(8,128)(2,1)S(1)}, bf16[8,4096]{1,0:T(8,128)(2,1)S(1)}, u32[]{:S(2)}, u32[]{:S(2)}) collective-permute-start(bf16[8,4096]{1,0:T(8,128)(2,1)S(1)} %get-tuple-element.22), channel_id=1, source_target_pairs={{0,4},{1,5},{2,6},{3,7},{4,0},{5,1},{6,2},{7,3},{8,12},{9,13},{10,... | collective-permute-start | bytes 196616 | tf_op jit(solution)/shard_map/ppermute | solution.py:20
  46.6 2.1 %collective-permute-start.11 = (bf16[8,4096]{1,0:T(8,128)(2,1)S(1)}, bf16[8,4096]{1,0:T(8,128)(2,1)S(1)}, u32[]{:S(2)}, u32[]{:S(2)}) collective-permute-start(bf16[8,4096]{1,0:T(8,128)(2,1)S(1)} %get-tuple-element.23), channel_id=1, source_target_pairs={{0,6},{1,7},{2,4},{3,5},{4,2},{5,3},{6,0},{7,1},{8,14},{9,15},{10,... | collective-permute-start | bytes 196616 | tf_op jit(solution)/shard_map/ppermute | solution.py:20
  50.1 2.6 %collective-permute-done.11 = bf16[8,4096]{1,0:T(8,128)(2,1)S(1)} collective-permute-done((bf16[8,4096]{1,0:T(8,128)(2,1)S(1)}, bf16[8,4096]{1,0:T(8,128)(2,1)S(1)}, u32[]{:S(2)}, u32[]{:S(2)}) %collective-permute-start.11) | collective-permute-done | bytes 65568 | tf_op jit(solution)/shard_map/ppermute | solution.py:20
  54.5 2.7 %collective-permute-start.20 = (bf16[8,3200]{1,0:T(8,128)(2,1)S(1)}, bf16[8,3200]{1,0:T(8,128)(2,1)S(1)}, u32[]{:S(2)}, u32[]{:S(2)}) collective-permute-start(bf16[8,3200]{1,0:T(8,128)(2,1)S(1)} %get-tuple-element.40), channel_id=1, source_target_pairs={{0,2},{1,3},{2,0},{3,1},{4,6},{5,7},{6,4},{7,5},{8,10},{9,11},{10,... | collective-permute-start | bytes 153608 | tf_op jit(solution)/shard_map/ppermute | solution.py:20
  57.2 1.0 collective-permute-start.22
  58.7 2.9 %collective-permute-start.16 = (bf16[8,4096]{1,0:T(8,128)(2,1)S(1)}, bf16[8,4096]{1,0:T(8,128)(2,1)S(1)}, u32[]{:S(2)}, u32[]{:S(2)}) collective-permute-start(bf16[8,4096]{1,0:T(8,128)(2,1)S(1)} %get-tuple-element.38), channel_id=1, source_target_pairs={{0,2},{1,3},{2,0},{3,1},{4,6},{5,7},{6,4},{7,5},{8,10},{9,11},{10,... | collective-permute-start | bytes 196616 | tf_op jit(solution)/shard_map/ppermute | solution.py:20
  61.7 1.0 collective-permute-start.18
  64.6 3.2 %collective-permute-done.18 = bf16[8,4096]{1,0:T(8,128)(2,1)S(1)} collective-permute-done((bf16[8,4096]{1,0:T(8,128)(2,1)S(1)}, bf16[8,4096]{1,0:T(8,128)(2,1)S(1)}, u32[]{:S(2)}, u32[]{:S(2)}) %collective-permute-start.18) | collective-permute-done | bytes 65568 | tf_op jit(solution)/shard_map/ppermute | solution.py:20
  69.4 5.0 %shard_map.122 = (f32[64,1024]{1,0:T(8,128)S(1)}, f32[64,1024]{1,0:T(8,128)S(1)}) custom-call(bf16[64,3072]{1,0:T(8,128)(2,1)S(1)} %slice.189.rows_ref, bf16[7168,1024]{1,0:T(8,128)(2,1)} %gate_hbm.3, bf16[7168,1024]{1,0:T(8,128)(2,1)} %up_hbm.3, f32[64,1024]{1,0:T(8,128)S(1)} %broadcast_in_dim.61.gate_in.up_in, f32[64,1024]{1,0:T(8,128)S(1)} %broadcast_in_dim.61.gate_in.up_in), custom_call_target="tpu_custom_call" | custom-call | flops 805306368 | bytes 12582912 | tf_op jit(solution)/shard_map/pallas_call | solution.py:263
  74.5 6.5 %shard_map.123.rows_ref = bf16[64,1024]{1,0:T(8,128)(2,1)S(1)} custom-call(bf16[64,4096]{1,0:T(8,128)(2,1)S(1)} %bitcast.114, bf16[7168,1024]{1,0:T(8,128)(2,1)} %gate_hbm.3, bf16[7168,1024]{1,0:T(8,128)(2,1)} %up_hbm.3, f32[64,1024]{1,0:T(8,128)S(1)} %get-tuple-element.9.gate_in, f32[64,1024]{1,0:T(8,128)S(1)} %get-tuple-element.10.up_in), custom_call_target="tpu_custom_call" | custom-call | flops 1073741824 | bytes 16777216 | tf_op jit(solution)/shard_map/pallas_call | solution.py:263
  81.0 3.3 %shard_map.125 = bf16[64,3072]{1,0:T(8,128)(2,1)S(1)} custom-call(bf16[64,1024]{1,0:T(8,128)(2,1)S(1)} %shard_map.123.rows_ref, f32[64,1]{1,0:T(8,128)S(1)} %copy.46.scale_ref, bf16[1024,7168]{1,0:T(8,128)(2,1)} %weight_hbm.7), custom_call_target="tpu_custom_call" | custom-call | flops 402653184 | bytes 6291456 | tf_op jit(solution)/shard_map/pallas_call | solution.py:204
  85.2 4.0 %shard_map.124 = bf16[64,4096]{1,0:T(8,128)(2,1)S(1)} custom-call(bf16[64,1024]{1,0:T(8,128)(2,1)S(1)} %shard_map.123.rows_ref, f32[64,1]{1,0:T(8,128)S(1)} %copy.46.scale_ref, bf16[1024,7168]{1,0:T(8,128)(2,1)} %weight_hbm.7), custom_call_target="tpu_custom_call" | custom-call | flops 536870912 | bytes 8388608 | tf_op jit(solution)/shard_map/pallas_call | solution.py:204
  89.3 1.2 %collective-permute-start.24 = (bf16[4,1,8,4096]{3,2,1,0:T(8,128)(2,1)S(1)}, bf16[4,1,8,4096]{3,2,1,0:T(8,128)(2,1)S(1)}, u32[]{:S(2)}, u32[]{:S(2)}) collective-permute-start(bf16[4,1,8,4096]{3,2,1,0:T(8,128)(2,1)S(1)} %slice.192), channel_id=1, source_target_pairs={{0,1},{1,0},{2,3},{3,2},{4,5},{5,4},{6,7},{7,6},{8,9},{9,8},{10,11... | collective-permute-start | bytes 786440 | tf_op jit(solution)/shard_map/ppermute | solution.py:20
  90.7 2.8 %collective-permute-start.31 = (bf16[8,3072]{1,0:T(8,128)(2,1)S(1)}, bf16[8,3072]{1,0:T(8,128)(2,1)S(1)}, u32[]{:S(2)}, u32[]{:S(2)}) collective-permute-start(bf16[8,3072]{1,0:T(8,128)(2,1)S(1)} %get-tuple-element.26), channel_id=1, source_target_pairs={{0,6},{1,7},{2,4},{3,5},{4,2},{5,3},{6,0},{7,1},{8,14},{9,15},{10,... | collective-permute-start | bytes 147464 | tf_op jit(solution)/shard_map/ppermute | solution.py:20
  94.1 1.6 %collective-permute-done.24 = bf16[4,1,8,4096]{3,2,1,0:T(8,128)(2,1)S(1)} collective-permute-done((bf16[4,1,8,4096]{3,2,1,0:T(8,128)(2,1)S(1)}, bf16[4,1,8,4096]{3,2,1,0:T(8,128)(2,1)S(1)}, u32[]{:S(2)}, u32[]{:S(2)}) %collective-permute-start.24) | collective-permute-done | bytes 262176 | tf_op jit(solution)/shard_map/ppermute | solution.py:20
  95.9 2.4 %collective-permute-start.27 = (bf16[8,4096]{1,0:T(8,128)(2,1)S(1)}, bf16[8,4096]{1,0:T(8,128)(2,1)S(1)}, u32[]{:S(2)}, u32[]{:S(2)}) collective-permute-start(bf16[8,4096]{1,0:T(8,128)(2,1)S(1)} %get-tuple-element.20), channel_id=1, source_target_pairs={{0,6},{1,7},{2,4},{3,5},{4,2},{5,3},{6,0},{7,1},{8,14},{9,15},{10,... | collective-permute-start | bytes 196616 | tf_op jit(solution)/shard_map/ppermute | solution.py:20
  98.3 1.1 %collective-permute-start.26 = (bf16[8,4096]{1,0:T(8,128)(2,1)S(1)}, bf16[8,4096]{1,0:T(8,128)(2,1)S(1)}, u32[]{:S(2)}, u32[]{:S(2)}) collective-permute-start(bf16[8,4096]{1,0:T(8,128)(2,1)S(1)} %get-tuple-element.21), channel_id=1, source_target_pairs={{0,2},{1,3},{2,0},{3,1},{4,6},{5,7},{6,4},{7,5},{8,10},{9,11},{10,... | collective-permute-start | bytes 196616 | tf_op jit(solution)/shard_map/ppermute | solution.py:20
  99.4 1.8 %collective-permute-done.25 = bf16[8,4096]{1,0:T(8,128)(2,1)S(1)} collective-permute-done((bf16[8,4096]{1,0:T(8,128)(2,1)S(1)}, bf16[8,4096]{1,0:T(8,128)(2,1)S(1)}, u32[]{:S(2)}, u32[]{:S(2)}) %collective-permute-start.25) | collective-permute-done | bytes 65568 | tf_op jit(solution)/shard_map/ppermute | solution.py:20
  (105 shorter events, 17.0 us)
Async XLA Ops:
  6.0 8.8 %collective-permute-start.2 = (bf16[2,48,512]{2,1,0:T(8,128)(2,1)S(1)}, bf16[2,48,512]{2,1,0:T(8,128)(2,1)S(1)}, u32[]{:S(2)}, u32[]{:S(2)}) collective-permute-start(bf16[2,48,512]{2,1,0:T(8,128)(2,1)S(1)} %get-tuple-element.16), channel_id=1, source_target_pairs={{0,6},{1,7},{2,4},{3,5},{4,2},{5,3},{6,0},{7,1},{8,14},{9,15},{10,... | collective-permute-start | bytes 294920 | tf_op jit(solution)/shard_map/ppermute | solution.py:20
  11.1 9.8 %collective-permute-start.1 = (bf16[2,48,512]{2,1,0:T(8,128)(2,1)S(1)}, bf16[2,48,512]{2,1,0:T(8,128)(2,1)S(1)}, u32[]{:S(2)}, u32[]{:S(2)}) collective-permute-start(bf16[2,48,512]{2,1,0:T(8,128)(2,1)S(1)} %get-tuple-element.17), channel_id=1, source_target_pairs={{0,4},{1,5},{2,6},{3,7},{4,0},{5,1},{6,2},{7,3},{8,12},{9,13},{10,... | collective-permute-start | bytes 294920 | tf_op jit(solution)/shard_map/ppermute | solution.py:20
  11.1 9.8 %collective-permute-start = (bf16[2,48,512]{2,1,0:T(8,128)(2,1)S(1)}, bf16[2,48,512]{2,1,0:T(8,128)(2,1)S(1)}, u32[]{:S(2)}, u32[]{:S(2)}) collective-permute-start(bf16[2,48,512]{2,1,0:T(8,128)(2,1)S(1)} %get-tuple-element.18), channel_id=1, source_target_pairs={{0,2},{1,3},{2,0},{3,1},{4,6},{5,7},{6,4},{7,5},{8,10},{9,11},{10,... | collective-permute-start | bytes 294920 | tf_op jit(solution)/shard_map/ppermute | solution.py:20
  14.9 7.8 %collective-permute-start.6 = (bf16[2,16,512]{2,1,0:T(8,128)(2,1)S(1)}, bf16[2,16,512]{2,1,0:T(8,128)(2,1)S(1)}, u32[]{:S(2)}, u32[]{:S(2)}) collective-permute-start(bf16[2,16,512]{2,1,0:T(8,128)(2,1)S(1)} %get-tuple-element.34), channel_id=1, source_target_pairs={{0,6},{1,7},{2,4},{3,5},{4,2},{5,3},{6,0},{7,1},{8,14},{9,15},{10,... | collective-permute-start | bytes 98312 | tf_op jit(solution)/shard_map/ppermute | solution.py:20
  18.7 4.8 %collective-permute-start.5 = (bf16[2,16,512]{2,1,0:T(8,128)(2,1)S(1)}, bf16[2,16,512]{2,1,0:T(8,128)(2,1)S(1)}, u32[]{:S(2)}, u32[]{:S(2)}) collective-permute-start(bf16[2,16,512]{2,1,0:T(8,128)(2,1)S(1)} %get-tuple-element.35), channel_id=1, source_target_pairs={{0,4},{1,5},{2,6},{3,7},{4,0},{5,1},{6,2},{7,3},{8,12},{9,13},{10,... | collective-permute-start | bytes 98312 | tf_op jit(solution)/shard_map/ppermute | solution.py:20
  20.4 3.9 %collective-permute-start.4 = (bf16[2,16,512]{2,1,0:T(8,128)(2,1)S(1)}, bf16[2,16,512]{2,1,0:T(8,128)(2,1)S(1)}, u32[]{:S(2)}, u32[]{:S(2)}) collective-permute-start(bf16[2,16,512]{2,1,0:T(8,128)(2,1)S(1)} %get-tuple-element.36), channel_id=1, source_target_pairs={{0,2},{1,3},{2,0},{3,1},{4,6},{5,7},{6,4},{7,5},{8,10},{9,11},{10,... | collective-permute-start | bytes 98312 | tf_op jit(solution)/shard_map/ppermute | solution.py:20
  21.0 7.6 %collective-permute-start.3 = (bf16[4,48,512]{2,1,0:T(8,128)(2,1)S(1)}, bf16[4,48,512]{2,1,0:T(8,128)(2,1)S(1)}, u32[]{:S(2)}, u32[]{:S(2)}) collective-permute-start(bf16[4,48,512]{2,1,0:T(8,128)(2,1)S(1)} %get-tuple-element.14), channel_id=1, source_target_pairs={{0,1},{1,0},{2,3},{3,2},{4,5},{5,4},{6,7},{7,6},{8,9},{9,8},{10,11... | collective-permute-start | bytes 589832 | tf_op jit(solution)/shard_map/ppermute | solution.py:20
  24.3 4.3 %collective-permute-start.7 = (bf16[4,16,512]{2,1,0:T(8,128)(2,1)S(1)}, bf16[4,16,512]{2,1,0:T(8,128)(2,1)S(1)}, u32[]{:S(2)}, u32[]{:S(2)}) collective-permute-start(bf16[4,16,512]{2,1,0:T(8,128)(2,1)S(1)} %get-tuple-element.32), channel_id=1, source_target_pairs={{0,1},{1,0},{2,3},{3,2},{4,5},{5,4},{6,7},{7,6},{8,9},{9,8},{10,11... | collective-permute-start | bytes 196616 | tf_op jit(solution)/shard_map/ppermute | solution.py:20
  32.6 7.2 %collective-permute-start.12 = (bf16[4,1,8,3072]{3,2,1,0:T(8,128)(2,1)S(1)}, bf16[4,1,8,3072]{3,2,1,0:T(8,128)(2,1)S(1)}, u32[]{:S(2)}, u32[]{:S(2)}) collective-permute-start(bf16[4,1,8,3072]{3,2,1,0:T(8,128)(2,1)S(1)} %slice.182), channel_id=1, source_target_pairs={{0,1},{1,0},{2,3},{3,2},{4,5},{5,4},{6,7},{7,6},{8,9},{9,8},{10,11... | collective-permute-start | bytes 589832 | tf_op jit(solution)/shard_map/ppermute | solution.py:20
  38.2 6.4 %collective-permute-start.8 = (bf16[4,1,8,4096]{3,2,1,0:T(8,128)(2,1)S(1)}, bf16[4,1,8,4096]{3,2,1,0:T(8,128)(2,1)S(1)}, u32[]{:S(2)}, u32[]{:S(2)}) collective-permute-start(bf16[4,1,8,4096]{3,2,1,0:T(8,128)(2,1)S(1)} %slice.176), channel_id=1, source_target_pairs={{0,1},{1,0},{2,3},{3,2},{4,5},{5,4},{6,7},{7,6},{8,9},{9,8},{10,11... | collective-permute-start | bytes 786440 | tf_op jit(solution)/shard_map/ppermute | solution.py:20
  39.9 8.7 %collective-permute-start.13 = (bf16[8,3072]{1,0:T(8,128)(2,1)S(1)}, bf16[8,3072]{1,0:T(8,128)(2,1)S(1)}, u32[]{:S(2)}, u32[]{:S(2)}) collective-permute-start(bf16[8,3072]{1,0:T(8,128)(2,1)S(1)} %get-tuple-element.28), channel_id=1, source_target_pairs={{0,4},{1,5},{2,6},{3,7},{4,0},{5,1},{6,2},{7,3},{8,12},{9,13},{10,... | collective-permute-start | bytes 147464 | tf_op jit(solution)/shard_map/ppermute | solution.py:20
  42.0 6.6 %collective-permute-start.15 = (bf16[8,3072]{1,0:T(8,128)(2,1)S(1)}, bf16[8,3072]{1,0:T(8,128)(2,1)S(1)}, u32[]{:S(2)}, u32[]{:S(2)}) collective-permute-start(bf16[8,3072]{1,0:T(8,128)(2,1)S(1)} %get-tuple-element.29), channel_id=1, source_target_pairs={{0,6},{1,7},{2,4},{3,5},{4,2},{5,3},{6,0},{7,1},{8,14},{9,15},{10,... | collective-permute-start | bytes 147464 | tf_op jit(solution)/shard_map/ppermute | solution.py:20
  44.1 5.2 %collective-permute-start.14 = (bf16[8,3072]{1,0:T(8,128)(2,1)S(1)}, bf16[8,3072]{1,0:T(8,128)(2,1)S(1)}, u32[]{:S(2)}, u32[]{:S(2)}) collective-permute-start(bf16[8,3072]{1,0:T(8,128)(2,1)S(1)} %get-tuple-element.30), channel_id=1, source_target_pairs={{0,2},{1,3},{2,0},{3,1},{4,6},{5,7},{6,4},{7,5},{8,10},{9,11},{10,... | collective-permute-start | bytes 147464 | tf_op jit(solution)/shard_map/ppermute | solution.py:20
  44.8 5.3 %collective-permute-start.9 = (bf16[8,4096]{1,0:T(8,128)(2,1)S(1)}, bf16[8,4096]{1,0:T(8,128)(2,1)S(1)}, u32[]{:S(2)}, u32[]{:S(2)}) collective-permute-start(bf16[8,4096]{1,0:T(8,128)(2,1)S(1)} %get-tuple-element.22), channel_id=1, source_target_pairs={{0,4},{1,5},{2,6},{3,7},{4,0},{5,1},{6,2},{7,3},{8,12},{9,13},{10,... | collective-permute-start | bytes 196616 | tf_op jit(solution)/shard_map/ppermute | solution.py:20
  46.6 6.1 %collective-permute-start.11 = (bf16[8,4096]{1,0:T(8,128)(2,1)S(1)}, bf16[8,4096]{1,0:T(8,128)(2,1)S(1)}, u32[]{:S(2)}, u32[]{:S(2)}) collective-permute-start(bf16[8,4096]{1,0:T(8,128)(2,1)S(1)} %get-tuple-element.23), channel_id=1, source_target_pairs={{0,6},{1,7},{2,4},{3,5},{4,2},{5,3},{6,0},{7,1},{8,14},{9,15},{10,... | collective-permute-start | bytes 196616 | tf_op jit(solution)/shard_map/ppermute | solution.py:20
  48.6 4.7 %collective-permute-start.10 = (bf16[8,4096]{1,0:T(8,128)(2,1)S(1)}, bf16[8,4096]{1,0:T(8,128)(2,1)S(1)}, u32[]{:S(2)}, u32[]{:S(2)}) collective-permute-start(bf16[8,4096]{1,0:T(8,128)(2,1)S(1)} %get-tuple-element.24), channel_id=1, source_target_pairs={{0,2},{1,3},{2,0},{3,1},{4,6},{5,7},{6,4},{7,5},{8,10},{9,11},{10,... | collective-permute-start | bytes 196616 | tf_op jit(solution)/shard_map/ppermute | solution.py:20
  53.7 8.0 %collective-permute-start.21 = (bf16[8,3200]{1,0:T(8,128)(2,1)S(1)}, bf16[8,3200]{1,0:T(8,128)(2,1)S(1)}, u32[]{:S(2)}, u32[]{:S(2)}) collective-permute-start(bf16[8,3200]{1,0:T(8,128)(2,1)S(1)} %get-tuple-element.40), channel_id=1, source_target_pairs={{0,4},{1,5},{2,6},{3,7},{4,0},{5,1},{6,2},{7,3},{8,12},{9,13},{10,... | collective-permute-start | bytes 153608 | tf_op jit(solution)/shard_map/ppermute | solution.py:20
  54.5 8.1 %collective-permute-start.20 = (bf16[8,3200]{1,0:T(8,128)(2,1)S(1)}, bf16[8,3200]{1,0:T(8,128)(2,1)S(1)}, u32[]{:S(2)}, u32[]{:S(2)}) collective-permute-start(bf16[8,3200]{1,0:T(8,128)(2,1)S(1)} %get-tuple-element.40), channel_id=1, source_target_pairs={{0,2},{1,3},{2,0},{3,1},{4,6},{5,7},{6,4},{7,5},{8,10},{9,11},{10,... | collective-permute-start | bytes 153608 | tf_op jit(solution)/shard_map/ppermute | solution.py:20
  57.2 6.0 %collective-permute-start.22 = (bf16[8,3200]{1,0:T(8,128)(2,1)S(1)}, bf16[8,3200]{1,0:T(8,128)(2,1)S(1)}, u32[]{:S(2)}, u32[]{:S(2)}) collective-permute-start(bf16[8,3200]{1,0:T(8,128)(2,1)S(1)} %get-tuple-element.40), channel_id=1, source_target_pairs={{0,6},{1,7},{2,4},{3,5},{4,2},{5,3},{6,0},{7,1},{8,14},{9,15},{10,... | collective-permute-start | bytes 153608 | tf_op jit(solution)/shard_map/ppermute | solution.py:20
  58.2 6.4 %collective-permute-start.17 = (bf16[8,4096]{1,0:T(8,128)(2,1)S(1)}, bf16[8,4096]{1,0:T(8,128)(2,1)S(1)}, u32[]{:S(2)}, u32[]{:S(2)}) collective-permute-start(bf16[8,4096]{1,0:T(8,128)(2,1)S(1)} %get-tuple-element.38), channel_id=1, source_target_pairs={{0,4},{1,5},{2,6},{3,7},{4,0},{5,1},{6,2},{7,3},{8,12},{9,13},{10,... | collective-permute-start | bytes 196616 | tf_op jit(solution)/shard_map/ppermute | solution.py:20
  58.7 5.8 %collective-permute-start.16 = (bf16[8,4096]{1,0:T(8,128)(2,1)S(1)}, bf16[8,4096]{1,0:T(8,128)(2,1)S(1)}, u32[]{:S(2)}, u32[]{:S(2)}) collective-permute-start(bf16[8,4096]{1,0:T(8,128)(2,1)S(1)} %get-tuple-element.38), channel_id=1, source_target_pairs={{0,2},{1,3},{2,0},{3,1},{4,6},{5,7},{6,4},{7,5},{8,10},{9,11},{10,... | collective-permute-start | bytes 196616 | tf_op jit(solution)/shard_map/ppermute | solution.py:20
  61.7 6.1 %collective-permute-start.18 = (bf16[8,4096]{1,0:T(8,128)(2,1)S(1)}, bf16[8,4096]{1,0:T(8,128)(2,1)S(1)}, u32[]{:S(2)}, u32[]{:S(2)}) collective-permute-start(bf16[8,4096]{1,0:T(8,128)(2,1)S(1)} %get-tuple-element.38), channel_id=1, source_target_pairs={{0,6},{1,7},{2,4},{3,5},{4,2},{5,3},{6,0},{7,1},{8,14},{9,15},{10,... | collective-permute-start | bytes 196616 | tf_op jit(solution)/shard_map/ppermute | solution.py:20
  63.2 5.8 %collective-permute-start.23 = (bf16[4,1,8,3200]{3,2,0,1:T(8,128)(2,1)S(1)}, bf16[4,1,8,3200]{3,2,0,1:T(8,128)(2,1)S(1)}, u32[]{:S(2)}, u32[]{:S(2)}) collective-permute-start(bf16[4,1,8,3200]{3,2,0,1:T(8,128)(2,1)S(1)} %maximum_bitcast_fusion.1), channel_id=1, source_target_pairs={{0,1},{1,0},{2,3},{3,2},{4,5},{5,4},{6,7},{7,6},{8,9},{9,8},{10,11... | collective-permute-start | bytes 614408 | tf_op jit(solution)/shard_map/ppermute | solution.py:20
  67.8 6.6 %collective-permute-start.19 = (bf16[4,1,8,4096]{3,2,0,1:T(8,128)(2,1)S(1)}, bf16[4,1,8,4096]{3,2,0,1:T(8,128)(2,1)S(1)}, u32[]{:S(2)}, u32[]{:S(2)}) collective-permute-start(bf16[4,1,8,4096]{3,2,0,1:T(8,128)(2,1)S(1)} %maximum_bitcast_fusion), channel_id=1, source_target_pairs={{0,1},{1,0},{2,3},{3,2},{4,5},{5,4},{6,7},{7,6},{8,9},{9,8},{10,11... | collective-permute-start | bytes 786440 | tf_op jit(solution)/shard_map/ppermute | solution.py:20
  84.3 6.2 %collective-permute-start.28 = (bf16[4,1,8,3072]{3,2,1,0:T(8,128)(2,1)S(1)}, bf16[4,1,8,3072]{3,2,1,0:T(8,128)(2,1)S(1)}, u32[]{:S(2)}, u32[]{:S(2)}) collective-permute-start(bf16[4,1,8,3072]{3,2,1,0:T(8,128)(2,1)S(1)} %slice.198), channel_id=1, source_target_pairs={{0,1},{1,0},{2,3},{3,2},{4,5},{5,4},{6,7},{7,6},{8,9},{9,8},{10,11... | collective-permute-start | bytes 589832 | tf_op jit(solution)/shard_map/ppermute | solution.py:20
  89.3 6.4 %collective-permute-start.24 = (bf16[4,1,8,4096]{3,2,1,0:T(8,128)(2,1)S(1)}, bf16[4,1,8,4096]{3,2,1,0:T(8,128)(2,1)S(1)}, u32[]{:S(2)}, u32[]{:S(2)}) collective-permute-start(bf16[4,1,8,4096]{3,2,1,0:T(8,128)(2,1)S(1)} %slice.192), channel_id=1, source_target_pairs={{0,1},{1,0},{2,3},{3,2},{4,5},{5,4},{6,7},{7,6},{8,9},{9,8},{10,11... | collective-permute-start | bytes 786440 | tf_op jit(solution)/shard_map/ppermute | solution.py:20
  90.6 7.7 %collective-permute-start.29 = (bf16[8,3072]{1,0:T(8,128)(2,1)S(1)}, bf16[8,3072]{1,0:T(8,128)(2,1)S(1)}, u32[]{:S(2)}, u32[]{:S(2)}) collective-permute-start(bf16[8,3072]{1,0:T(8,128)(2,1)S(1)} %get-tuple-element.25), channel_id=1, source_target_pairs={{0,4},{1,5},{2,6},{3,7},{4,0},{5,1},{6,2},{7,3},{8,12},{9,13},{10,... | collective-permute-start | bytes 147464 | tf_op jit(solution)/shard_map/ppermute | solution.py:20
  90.7 8.7 %collective-permute-start.31 = (bf16[8,3072]{1,0:T(8,128)(2,1)S(1)}, bf16[8,3072]{1,0:T(8,128)(2,1)S(1)}, u32[]{:S(2)}, u32[]{:S(2)}) collective-permute-start(bf16[8,3072]{1,0:T(8,128)(2,1)S(1)} %get-tuple-element.26), channel_id=1, source_target_pairs={{0,6},{1,7},{2,4},{3,5},{4,2},{5,3},{6,0},{7,1},{8,14},{9,15},{10,... | collective-permute-start | bytes 147464 | tf_op jit(solution)/shard_map/ppermute | solution.py:20
  93.4 5.9 %collective-permute-start.30 = (bf16[8,3072]{1,0:T(8,128)(2,1)S(1)}, bf16[8,3072]{1,0:T(8,128)(2,1)S(1)}, u32[]{:S(2)}, u32[]{:S(2)}) collective-permute-start(bf16[8,3072]{1,0:T(8,128)(2,1)S(1)} %get-tuple-element.27), channel_id=1, source_target_pairs={{0,2},{1,3},{2,0},{3,1},{4,6},{5,7},{6,4},{7,5},{8,10},{9,11},{10,... | collective-permute-start | bytes 147464 | tf_op jit(solution)/shard_map/ppermute | solution.py:20
  95.8 5.4 %collective-permute-start.25 = (bf16[8,4096]{1,0:T(8,128)(2,1)S(1)}, bf16[8,4096]{1,0:T(8,128)(2,1)S(1)}, u32[]{:S(2)}, u32[]{:S(2)}) collective-permute-start(bf16[8,4096]{1,0:T(8,128)(2,1)S(1)} %get-tuple-element.19), channel_id=1, source_target_pairs={{0,4},{1,5},{2,6},{3,7},{4,0},{5,1},{6,2},{7,3},{8,12},{9,13},{10,... | collective-permute-start | bytes 196616 | tf_op jit(solution)/shard_map/ppermute | solution.py:20
  95.9 6.2 %collective-permute-start.27 = (bf16[8,4096]{1,0:T(8,128)(2,1)S(1)}, bf16[8,4096]{1,0:T(8,128)(2,1)S(1)}, u32[]{:S(2)}, u32[]{:S(2)}) collective-permute-start(bf16[8,4096]{1,0:T(8,128)(2,1)S(1)} %get-tuple-element.20), channel_id=1, source_target_pairs={{0,6},{1,7},{2,4},{3,5},{4,2},{5,3},{6,0},{7,1},{8,14},{9,15},{10,... | collective-permute-start | bytes 196616 | tf_op jit(solution)/shard_map/ppermute | solution.py:20
  98.3 4.4 %collective-permute-start.26 = (bf16[8,4096]{1,0:T(8,128)(2,1)S(1)}, bf16[8,4096]{1,0:T(8,128)(2,1)S(1)}, u32[]{:S(2)}, u32[]{:S(2)}) collective-permute-start(bf16[8,4096]{1,0:T(8,128)(2,1)S(1)} %get-tuple-element.21), channel_id=1, source_target_pairs={{0,2},{1,3},{2,0},{3,1},{4,6},{5,7},{6,4},{7,5},{8,10},{9,11},{10,... | collective-permute-start | bytes 196616 | tf_op jit(solution)/shard_map/ppermute | solution.py:20
  (6 other events, 135.2 us)
